TPU v7x, 128 devices: a whole 4x4x4 slice. The times are simulated.
128 devices in a mesh: block: 32 (over z, x, core), grp: 4 (over y).
Axes of the slice: x: 4, y: 4, z: 4, core: 2. Of those that a mesh axis runs over, the one named last changes fastest.
Arguments:
- features: bfloat16 [512, 256, 128], P(('block', 'grp')), may hold values from -6 to 6
- point_counts: int32 [512], P(('block', 'grp')), may hold values from 128 to 256, as said below
- kernel_weights: bfloat16 [15, 128, 128], replicated, may hold values from -0.015625 to 0.015625
- influence: bfloat16 [1024, 15, 256, 256], P(('block', 'grp')), may hold values from 0 to 1
- pair_list: int32 [1024, 2], P(('block', 'grp')), may hold values from 0 to 511, as said below
- pair_counts: int32 [128], P(('block', 'grp')), may hold values from 1 to 8, as said below
- cotangent: bfloat16 [512, 256, 128], P(('block', 'grp')), may hold values from -6 to 6
Outputs:
- activated: bfloat16 [512, 256, 128], P(('block', 'grp'))
- grad_features: bfloat16 [512, 256, 128], P(('block', 'grp'))
- grad_weights: float32 [15, 128, 128], replicated
Inputs may be any that keep to these rules, and one draw needn't show every extreme that they name: `pair_list`: block x lives on device x // 4, and device d has block index d // 4 and grp index d % 4. Column 0 is below 4; the second block of every slot lives on a device whose block index differs from the slot's device's by at most one; any grp index may occur. `pair_counts`: slots at or beyond a device's count are unused. Some device uses all 8 slots. `point_counts`: the real points of a block are its first rows; the others are padding.
All inputs are finite; a program needn't handle non-finite values.
Results may differ from a plain program's by a relative error of at most 0.0063.
Values may be sent and summed in bfloat16 or wider, within the bound.
No kernel may reach another device: no remote copies, remote signals or barrier semaphores. Data moves between devices by JAX's collectives and lax.ppermute only.
A program may use at most 128 MiB of HBM per device.

v0:
```python
import math

import jax
import jax.numpy as jnp
from jax import lax
from jax.sharding import PartitionSpec as P


def with_halo(array, sides, width):
    for axis, dim in sides:
        peers, length = (lax.axis_size(axis), array.shape[dim])
        up = [(i, (i + 1) % peers) for i in range(peers - 1)]
        down = [(j, i) for i, j in up]
        last = lax.slice_in_dim(array, length - width, length, axis=dim)
        initial = lax.slice_in_dim(array, 0, width, axis=dim)
        before = lax.ppermute(last, axis, up)
        after = lax.ppermute(initial, axis, down)
        array = jnp.concatenate([before, array, after], axis=dim)
    return array


def shifted(block, axis, distance):
    devices = range(lax.axis_size(axis))
    route = [(i - distance, i) for i in devices if i - distance in devices]
    return lax.ppermute(block, axis, route)


def gather_terms(tile, rows):
    out = jnp.einsum("kij,jc->ikc", tile, rows, preferred_element_type=jnp.float32)
    return out.astype(jnp.bfloat16).reshape(rows.shape[0], -1)


def scatter_terms(tile, rows):
    out = jnp.einsum("kij,ic->jkc", tile, rows, preferred_element_type=jnp.float32)
    return out.astype(jnp.bfloat16).reshape(rows.shape[0], -1)


def neighbours(values):
    region = lax.all_gather(values, "grp", axis=0, tiled=True)
    return with_halo(region[None], (("block", 0),), 1)


def collect(partial_value):
    from_lower = shifted(partial_value[2], "block", 1)
    from_upper = shifted(partial_value[0], "block", -1)
    return lax.psum_scatter(
        partial_value[1] + from_lower + from_upper, "grp", scatter_dimension=0, tiled=True
    )


def body(features, point_counts, kernel_weights, influence, pair_list, pair_counts, cotangent):
    block_count, points, width = features.shape
    kernels = kernel_weights.shape[0]
    slot_count = influence.shape[0]
    regions = lax.axis_size("grp")
    column_here = lax.axis_index("block")
    valid = (lax.broadcasted_iota(jnp.int32, (block_count, points), 1) < point_counts[:, None])[
        ..., None
    ]
    masked = jnp.where(valid, features, jnp.zeros_like(features))
    direct = kernel_weights.reshape(kernels * width, width)
    mirrored = kernel_weights[::-1].reshape(kernels * width, width)
    used = pair_counts[0]

    def locate(slot):
        pair = pair_list[slot]
        second = pair[1]
        owner = second // block_count
        column = owner // regions - column_here + 1
        row_index = owner % regions * block_count + second % block_count
        return (pair[0], column, row_index)

    near_rows = neighbours(masked)
    own_zero = jnp.zeros((block_count, points, width), jnp.float32)
    sent_zero = jnp.zeros((3, regions * block_count, points, width), jnp.float32)
    store_zero = jnp.zeros((slot_count, points, kernels * width), jnp.bfloat16)

    def forward_pair(slot, carry):
        own_total, sent, near_store, own_store = carry
        first, column, row_index = locate(slot)
        tile = influence[slot]
        near_terms = gather_terms(tile, near_rows[column, row_index])
        own_terms = scatter_terms(tile, masked[first])
        to_first = jnp.dot(near_terms, direct, preferred_element_type=jnp.float32)
        to_second = jnp.dot(own_terms, mirrored, preferred_element_type=jnp.float32)
        own_total = own_total.at[first].add(to_first)
        sent = sent.at[column, row_index].add(to_second)
        near_store = lax.dynamic_update_index_in_dim(near_store, near_terms, slot, 0)
        own_store = lax.dynamic_update_index_in_dim(own_store, own_terms, slot, 0)
        return (own_total, sent, near_store, own_store)

    own_total, sent, near_store, own_store = lax.fori_loop(
        0, used, forward_pair, (own_zero, sent_zero, store_zero, store_zero)
    )
    summed = own_total + collect(sent)
    pre = jnp.where(valid, summed, jnp.zeros_like(summed))
    activated = jax.nn.silu(pre).astype(jnp.bfloat16)
    sig = jax.nn.sigmoid(pre)
    slope = sig * (1.0 + pre * (1.0 - sig))
    upstream = jnp.where(valid, cotangent.astype(jnp.float32) * slope, jnp.zeros_like(pre)).astype(
        jnp.bfloat16
    )
    near_upstream = neighbours(upstream)
    weight_zero = jnp.zeros((kernels * width, width), jnp.float32)

    def backward_pair(slot, carry):
        own_grad, sent_grad, grad_direct, grad_mirror = carry
        first, column, row_index = locate(slot)
        tile = influence[slot]
        near_terms = near_store[slot]
        own_terms = own_store[slot]
        up_first = upstream[first]
        up_second = near_upstream[column, row_index]
        grad_direct = grad_direct + jnp.einsum(
            "pr,pe->re", near_terms, up_first, preferred_element_type=jnp.float32
        )
        grad_mirror = grad_mirror + jnp.einsum(
            "pr,pe->re", own_terms, up_second, preferred_element_type=jnp.float32
        )
        back_near = jnp.einsum("pe,re->pr", up_first, direct, preferred_element_type=jnp.float32)
        back_near = back_near.astype(jnp.bfloat16).reshape(points, kernels, width)
        back_own = jnp.einsum("pe,re->pr", up_second, mirrored, preferred_element_type=jnp.float32)
        back_own = back_own.astype(jnp.bfloat16).reshape(points, kernels, width)
        to_second = jnp.einsum("kij,ikc->jc", tile, back_near, preferred_element_type=jnp.float32)
        to_first = jnp.einsum("kij,jkc->ic", tile, back_own, preferred_element_type=jnp.float32)
        own_grad = own_grad.at[first].add(to_first)
        sent_grad = sent_grad.at[column, row_index].add(to_second)
        return (own_grad, sent_grad, grad_direct, grad_mirror)

    own_grad, sent_grad, grad_direct, grad_mirror = lax.fori_loop(
        0, used, backward_pair, (own_zero, sent_zero, weight_zero, weight_zero)
    )
    grad_rows = own_grad + collect(sent_grad)
    grad_features = jnp.where(valid, grad_rows, jnp.zeros_like(grad_rows)).astype(jnp.bfloat16)
    local_weights = (
        grad_direct.reshape(kernels, width, width)
        + grad_mirror.reshape(kernels, width, width)[::-1]
    )
    total_weights = lax.psum(local_weights, ("block", "grp"))
    total_points = block_count * points * lax.axis_size("block") * regions
    grad_weights = total_weights * (1.0 / math.sqrt(total_points))
    return (activated, grad_features, grad_weights)


def solution(mesh):
    placed = (
        P(("block", "grp"), None, None),
        P(("block", "grp")),
        P(),
        P(("block", "grp"), None, None, None),
        P(("block", "grp"), None),
        P(("block", "grp")),
        P(("block", "grp"), None, None),
    )
    return jax.shard_map(
        body,
        mesh=mesh,
        in_specs=placed,
        out_specs=(P(("block", "grp"), None, None), P(("block", "grp"), None, None), P()),
        check_vma=False,
    )
```

profile of v0, /device:TPU:1, one launch (start us, length us, event | category | flops | bytes accessed | tf_op | source)
XLA Modules:
  0.0 710.6 jit_solution(15849865996113801066)
XLA Ops:
  9.9 26.7 %all-gather.3.cloned.1.call-done = bf16[16,256,128]{2,1,0:T(8,128)(2,1)} async-done(((bf16[4,256,128]{2,1,0:T(8,128)(2,1)}), bf16[16,256,128]{2,1,0:T(8,128)(2,1)}) %all-gather.3.cloned.1.call-update) | async-done | bytes 1048592 | tf_op jit(solution)/shard_map/all_gather | solution.py:39
  36.6 4.5 collective-permute-start
  44.1 9.0 %collective-permute-done = bf16[1,16,256,128]{3,2,1,0:T(8,128)(2,1)S(1)} collective-permute-done((bf16[1,16,256,128]{3,2,1,0:T(8,128)(2,1)}, bf16[1,16,256,128]{3,2,1,0:T(8,128)(2,1)S(1)}, u32[]{:S(2)}, u32[]{:S(2)}) %collective-permute-start) | collective-permute-done | bytes 1048608 | tf_op jit(solution)/shard_map/ppermute | solution.py:16
  53.2 4.3 collective-permute-done.1
  64.2 3.7 broadcast_in_dim.79.clone
  71.4 68.4 %while.42 = (s32[]{:T(128)}, f32[4,256,128]{2,1,0:T(8,128)S(1)}, f32[3,16,256,128]{3,2,1,0:T(8,128)}, bf16[8,256,1920]{1,2,0:T(8,128)(2,1)}, bf16[8,256,1920]{1,...) while((s32[]{:T(128)}, f32[4,256,128]{2,1,0:T(8,128)S(1)}, ...), condition=%wide.region_3.4_spmd, body=%wide.region_0.3_spmd.sunk | while | flops 756088896 | bytes 13438826 | solution.py:92
  142.3 18.8 %collective-permute-start.2 = (f32[16,256,128]{2,1,0:T(8,128)S(1)}, f32[16,256,128]{2,1,0:T(8,128)S(1)}, u32[]{:S(2)}, u32[]{:S(2)}) collective-permute-start(f32[16,256,128]{2,1,0:T(8,128)S(1)} %get-tuple-element.659), channel_id=1, source_target_pairs={{0,4},{4,8},{8,12},{12,16},{16,20},{20,24},{24,28},{28,32},{32,36}... | collective-permute-start | bytes 6291464 | tf_op jit(solution)/shard_map/ppermute | solution.py:25
  161.1 7.0 collective-permute-start.3
  168.1 15.9 %collective-permute-done.2 = f32[16,256,128]{2,1,0:T(8,128)S(1)} collective-permute-done((f32[16,256,128]{2,1,0:T(8,128)S(1)}, f32[16,256,128]{2,1,0:T(8,128)S(1)}, u32[]{:S(2)}, u32[]{:S(2)}) %collective-permute-start.2) | collective-permute-done | bytes 2097184 | tf_op jit(solution)/shard_map/ppermute | solution.py:25
  184.0 4.5 collective-permute-done.3
  191.9 84.1 %reduce-scatter.3.cloned.1.call-done = f32[4,256,128]{2,1,0:T(8,128)} async-done(((f32[16,256,128]{2,1,0:T(8,128)}), f32[4,256,128]{2,1,0:T(8,128)}) %reduce-scatter.3.cloned.1.call-update) | async-done | bytes 524304 | tf_op jit(solution)/shard_map/reduce_scatter | solution.py:46
  278.3 22.9 %all-gather.5.cloned.1.call-done = bf16[16,256,128]{2,1,0:T(8,128)(2,1)} async-done(((bf16[4,256,128]{2,1,0:T(8,128)(2,1)}), bf16[16,256,128]{2,1,0:T(8,128)(2,1)}) %all-gather.5.cloned.1.call-update) | async-done | bytes 1048592 | tf_op jit(solution)/shard_map/all_gather | solution.py:39
  301.2 4.5 collective-permute-start.4
  307.7 10.1 %collective-permute-done.4 = bf16[1,16,256,128]{3,2,1,0:T(8,128)(2,1)S(1)} collective-permute-done((bf16[1,16,256,128]{3,2,1,0:T(8,128)(2,1)}, bf16[1,16,256,128]{3,2,1,0:T(8,128)(2,1)S(1)}, u32[]{:S(2)}, u32[]{:S(2)}) %collective-permute-start.4) | collective-permute-done | bytes 1048608 | tf_op jit(solution)/shard_map/ppermute | solution.py:16
  317.8 4.3 collective-permute-done.5
  330.8 89.9 %while.43 = (s32[]{:T(128)}, f32[4,256,128]{2,1,0:T(8,128)S(1)}, f32[3,16,256,128]{3,2,1,0:T(8,128)}, f32[1920,128]{1,0:T(8,128)}, f32[1920,128]{1,0:T(8,128)}, ...) while((s32[]{:T(128)}, f32[4,256,128]{2,1,0:T(8,128)S(1)}, ...), condition=%wide.region_8.9_spmd, body=%wide.region_5.8_spmd.sunk | while | flops 1008238720 | bytes 27335088 | solution.py:130
  420.8 4.7 slice_bitcast_fusion.1
  425.5 24.2 %collective-permute-start.6 = (f32[16,256,128]{2,1,0:T(8,128)}, f32[16,256,128]{2,1,0:T(8,128)}, u32[]{:S(2)}, u32[]{:S(2)}) collective-permute-start(f32[16,256,128]{2,1,0:T(8,128)} %get-tuple-element.657), channel_id=1, source_target_pairs={{0,4},{4,8},{8,12},{12,16},{16,20},{20,24},{24,28},{28,32},{32,36}... | collective-permute-start | bytes 6291464 | tf_op jit(solution)/shard_map/ppermute | solution.py:25
  449.7 13.5 %collective-permute-start.7 = (f32[16,256,128]{2,1,0:T(8,128)}, f32[16,256,128]{2,1,0:T(8,128)}, u32[]{:S(2)}, u32[]{:S(2)}) collective-permute-start(f32[16,256,128]{2,1,0:T(8,128)} %get-tuple-element.658), channel_id=1, source_target_pairs={{4,0},{8,4},{12,8},{16,12},{20,16},{24,20},{28,24},{32,28},{36,32}... | collective-permute-start | bytes 6291464 | tf_op jit(solution)/shard_map/ppermute | solution.py:25
  465.5 7.5 %collective-permute-done.6 = f32[16,256,128]{2,1,0:T(8,128)} collective-permute-done((f32[16,256,128]{2,1,0:T(8,128)}, f32[16,256,128]{2,1,0:T(8,128)}, u32[]{:S(2)}, u32[]{:S(2)}) %collective-permute-start.6) | collective-permute-done | bytes 2097184 | tf_op jit(solution)/shard_map/ppermute | solution.py:25
  473.0 4.4 collective-permute-done.7
  477.4 4.6 fusion.72
  482.0 189.8 %all-reduce.2.cloned.1.call-done = f32[15,128,128]{2,1,0:T(8,128)} async-done(((f32[15,128,128]{2,1,0:T(8,128)}), f32[15,128,128]{2,1,0:T(8,128)}) %all-reduce.2.cloned.1.call-update) | async-done | bytes 983056 | tf_op jit(solution)/shard_map/psum | solution.py:139
  674.1 28.0 %reduce-scatter.5.cloned.1.call-done = f32[4,256,128]{2,1,0:T(8,128)} async-done(((f32[16,256,128]{2,1,0:T(8,128)}), f32[4,256,128]{2,1,0:T(8,128)}) %reduce-scatter.5.cloned.1.call-update) | async-done | bytes 524304 | tf_op jit(solution)/shard_map/reduce_scatter | solution.py:46
  (142 shorter events, 157.2 us)
Async XLA Ops:
  7.2 29.4 %all-gather.3.cloned.1.call-start = ((), (), s32[]{:S(2)}) async-start(), calls=%async_computation.2 | async-start | bytes 1310720 | tf_op jit(solution)/shard_map/all_gather | solution.py:39
  9.8 266.2 %reduce-scatter.3.cloned.1.call-start = ((), (), s32[]{:S(2)}) async-start(), calls=%async_computation.3 | async-start | bytes 2621440 | tf_op jit(solution)/shard_map/reduce_scatter | solution.py:46
  36.6 16.6 %collective-permute-start = (bf16[1,16,256,128]{3,2,1,0:T(8,128)(2,1)}, bf16[1,16,256,128]{3,2,1,0:T(8,128)(2,1)S(1)}, u32[]{:S(2)}, u32[]{:S(2)}) collective-permute-start(bf16[1,16,256,128]{3,2,1,0:T(8,128)(2,1)} %bitcast.236), channel_id=1, source_target_pairs={{0,4},{4,8},{8,12},{12,16},{16,20},{20,24},{24,28},{28,32},{32,36}... | collective-permute-start | bytes 3145736 | tf_op jit(solution)/shard_map/ppermute | solution.py:16
  41.1 16.3 %collective-permute-start.1 = (bf16[1,16,256,128]{3,2,1,0:T(8,128)(2,1)}, bf16[1,16,256,128]{3,2,1,0:T(8,128)(2,1)S(1)}, u32[]{:S(2)}, u32[]{:S(2)}) collective-permute-start(bf16[1,16,256,128]{3,2,1,0:T(8,128)(2,1)} %bitcast.237), channel_id=1, source_target_pairs={{4,0},{8,4},{12,8},{16,12},{20,16},{24,20},{28,24},{32,28},{36,32}... | collective-permute-start | bytes 3145736 | tf_op jit(solution)/shard_map/ppermute | solution.py:17
  67.9 3.4 copy-start
  67.9 3.4 copy-start.5
  67.9 3.5 copy-start.6
  67.9 3.5 copy-start.7
  142.3 41.8 %collective-permute-start.2 = (f32[16,256,128]{2,1,0:T(8,128)S(1)}, f32[16,256,128]{2,1,0:T(8,128)S(1)}, u32[]{:S(2)}, u32[]{:S(2)}) collective-permute-start(f32[16,256,128]{2,1,0:T(8,128)S(1)} %get-tuple-element.659), channel_id=1, source_target_pairs={{0,4},{4,8},{8,12},{12,16},{16,20},{20,24},{24,28},{28,32},{32,36}... | collective-permute-start | bytes 6291464 | tf_op jit(solution)/shard_map/ppermute | solution.py:25
  161.1 115.0 %copy-start.4 = (bf16[4,256,128]{2,1,0:T(8,128)(2,1)S(1)}, bf16[4,256,128]{2,1,0:T(8,128)(2,1)}, u32[]{:S(2)}) copy-start(bf16[4,256,128]{2,1,0:T(8,128)(2,1)} %param.25) | copy-start | bytes 786436
  161.1 27.5 %collective-permute-start.3 = (f32[16,256,128]{2,1,0:T(8,128)S(1)}, f32[16,256,128]{2,1,0:T(8,128)S(1)}, u32[]{:S(2)}, u32[]{:S(2)}) collective-permute-start(f32[16,256,128]{2,1,0:T(8,128)S(1)} %get-tuple-element.660), channel_id=1, source_target_pairs={{4,0},{8,4},{12,8},{16,12},{20,16},{24,20},{28,24},{32,28},{36,32}... | collective-permute-start | bytes 6291464 | tf_op jit(solution)/shard_map/ppermute | solution.py:25
  191.9 109.3 %all-gather.5.cloned.1.call-start = ((), (), s32[]{:S(2)}) async-start(), calls=%async_computation.4 | async-start | bytes 1310720 | tf_op jit(solution)/shard_map/all_gather | solution.py:39
  278.3 393.5 %all-reduce.2.cloned.1.call-start = ((), (), s32[]{:S(2)}) async-start(), calls=%async_computation.6 | async-start | bytes 1966080 | tf_op jit(solution)/shard_map/psum | solution.py:139
  301.2 16.6 %collective-permute-start.4 = (bf16[1,16,256,128]{3,2,1,0:T(8,128)(2,1)}, bf16[1,16,256,128]{3,2,1,0:T(8,128)(2,1)S(1)}, u32[]{:S(2)}, u32[]{:S(2)}) collective-permute-start(bf16[1,16,256,128]{3,2,1,0:T(8,128)(2,1)} %bitcast.239), channel_id=1, source_target_pairs={{0,4},{4,8},{8,12},{12,16},{16,20},{20,24},{24,28},{28,32},{32,36}... | collective-permute-start | bytes 3145736 | tf_op jit(solution)/shard_map/ppermute | solution.py:16
  305.7 16.3 %collective-permute-start.5 = (bf16[1,16,256,128]{3,2,1,0:T(8,128)(2,1)}, bf16[1,16,256,128]{3,2,1,0:T(8,128)(2,1)S(1)}, u32[]{:S(2)}, u32[]{:S(2)}) collective-permute-start(bf16[1,16,256,128]{3,2,1,0:T(8,128)(2,1)} %bitcast.240), channel_id=1, source_target_pairs={{4,0},{8,4},{12,8},{16,12},{20,16},{24,20},{28,24},{32,28},{36,32}... | collective-permute-start | bytes 3145736 | tf_op jit(solution)/shard_map/ppermute | solution.py:17
  344.7 3.5 copy-start.1
  349.9 3.3 copy-start.2
  367.0 3.5 copy-start.1
  389.3 3.5 copy-start.1
  411.7 3.5 copy-start.1
  420.8 42.4 %copy-start.3 = (f32[1920,128]{1,0:T(8,128)S(1)}, f32[1920,128]{1,0:T(8,128)}, u32[]{:S(2)}) copy-start(f32[1920,128]{1,0:T(8,128)} %get-tuple-element.510) | copy-start | bytes 2949124
  425.5 47.4 %collective-permute-start.6 = (f32[16,256,128]{2,1,0:T(8,128)}, f32[16,256,128]{2,1,0:T(8,128)}, u32[]{:S(2)}, u32[]{:S(2)}) collective-permute-start(f32[16,256,128]{2,1,0:T(8,128)} %get-tuple-element.657), channel_id=1, source_target_pairs={{0,4},{4,8},{8,12},{12,16},{16,20},{20,24},{24,28},{28,32},{32,36}... | collective-permute-start | bytes 6291464 | tf_op jit(solution)/shard_map/ppermute | solution.py:25
  449.7 27.7 %collective-permute-start.7 = (f32[16,256,128]{2,1,0:T(8,128)}, f32[16,256,128]{2,1,0:T(8,128)}, u32[]{:S(2)}, u32[]{:S(2)}) collective-permute-start(f32[16,256,128]{2,1,0:T(8,128)} %get-tuple-element.658), channel_id=1, source_target_pairs={{4,0},{8,4},{12,8},{16,12},{20,16},{24,20},{28,24},{32,28},{36,32}... | collective-permute-start | bytes 6291464 | tf_op jit(solution)/shard_map/ppermute | solution.py:25
  465.5 236.6 %reduce-scatter.5.cloned.1.call-start = ((), (), s32[]{:S(2)}) async-start(), calls=%async_computation.5 | async-start | bytes 2621440 | tf_op jit(solution)/shard_map/reduce_scatter | solution.py:46
  (3 other events, 9.8 us)
Sparse Core Ops, SparseCore 0:
  10.2 26.2 all-gather.2
  192.0 84.0 reduce-scatter.2
  278.4 22.7 all-gather.4
  465.6 206.1 all-reduce.1
  674.1 27.9 reduce-scatter.4
where the time goes:
time: 715 us; the launch traced here: 711 us
  waiting for transfers between devices  412 us (58%)
  matrix products  88.1 us (12%)
  starting transfers between devices  76.6 us (11%)
  loops' own time  42.4 us (6%)
  local copies, waits for them, and re-layouts  40.5 us (6%)
  other arithmetic  37.4 us (5%)
  between operations  14 us (2%)
    psum x1, waiting for transfers between devices, body(): total_weights = lax.psum(local_weights, ('block', 'grp'))  190 us
    reduce_scatter x2, waiting for transfers between devices, collect(): lax.psum_scatter(partial_value[1] + from_lower + from_upper, 'grp', scatt...  112 us
    ppermute x4, starting transfers between devices, shifted(): return lax.ppermute(block, axis, route)  63.4 us
    all_gather x2, waiting for transfers between devices, neighbours(): region = lax.all_gather(values, 'grp', axis=0, tiled=True)  49.6 us
    ppermute x4, waiting for transfers between devices, shifted(): return lax.ppermute(block, axis, route)  32.3 us
    another operation x1, loops' own time, body(): lax.fori_loop(0, used, forward_pair, (own_zero, sent_zero, store_zero, st...  21.7 us
    another operation x1, loops' own time, body(): lax.fori_loop(0, used, backward_pair, (own_zero, sent_zero, weight_zero,...  20.7 us
    ppermute x2, waiting for transfers between devices, with_halo(): before = lax.ppermute(last, axis, up)  19.1 us
  transfers between devices with their start and end apart: 13, of which 13 were waited for; matrix products, arithmetic and copies ran while one was open for 1% of the time, Pallas kernels for 0%

commit v1 on v0

v1 whole, which is shorter than its diff:
```python
import functools
import math

import jax
import jax.numpy as jnp
from jax import lax
from jax.experimental import pallas as pl
from jax.experimental.pallas import tpu as pltpu
from jax.sharding import PartitionSpec as P

BF16 = jnp.bfloat16
F32 = jnp.float32
VMEM_LIMIT = 48 * 1024 * 1024


def dot(a, b):
    return jnp.dot(a, b, preferred_element_type=F32)


def struct(shape, dtype):
    return jax.ShapeDtypeStruct(shape, dtype)


def whole(shape):
    return pl.BlockSpec(shape, lambda *_: (0,) * len(shape))


def slot_of(s, counts):
    return jnp.minimum(s, counts[0] - 1)


def per_slot(shape):
    zeros = (0,) * (len(shape) - 1)
    return pl.BlockSpec(shape, lambda s, counts, *_: (slot_of(s, counts),) + zeros)


def call(kernel, grid, prefetch, in_specs, out_specs, out_shape, scratch, name, flops=0, size=0):
    return pl.pallas_call(
        kernel,
        grid_spec=pltpu.PrefetchScalarGridSpec(
            num_scalar_prefetch=prefetch,
            grid=grid,
            in_specs=in_specs,
            out_specs=out_specs,
            scratch_shapes=scratch,
        ),
        out_shape=out_shape,
        compiler_params=pltpu.CompilerParams(vmem_limit_bytes=VMEM_LIMIT),
        cost_estimate=pl.CostEstimate(flops=flops, bytes_accessed=size, transcendentals=0),
        name=name,
    )


def own_kernel(counts, pairs, m_ref, w_ref, h_ref, out_ref, mt_ref, wmt_ref, yt):
    kernels, points = h_ref.shape[1], h_ref.shape[2]
    s = pl.program_id(0)

    @pl.when(s == 0)
    def _():
        for k in range(kernels):
            wmt_ref[k] = w_ref[kernels - 1 - k].T
        for a in range(m_ref.shape[0]):
            mt_ref[a] = m_ref[a].T
            mt = mt_ref[a]
            for k in range(kernels):
                yt[a, :, k * points : (k + 1) * points] = dot(wmt_ref[k], mt).astype(BF16)

    @pl.when(s < counts[0])
    def _():
        a = pairs[s, 0]
        out_ref[0] = dot(yt[a], h_ref[0].reshape(kernels * points, points)).astype(BF16)


def near_select(second, l_ref, c_ref, r_ref, per_column):
    column = second // per_column - lax.axis_index("block")
    return jnp.where(column < 0, l_ref[0], jnp.where(column == 0, c_ref[0], r_ref[0]))


def near_kernel(per_column, counts, pairs, l_ref, c_ref, r_ref, w_ref, h_ref, total_ref, near_ref):
    kernels, width = w_ref.shape[0], w_ref.shape[1]
    s = pl.program_id(0)

    @pl.when(s == 0)
    def _():
        total_ref[...] = jnp.zeros_like(total_ref)

    @pl.when(s < counts[0])
    def _():
        x = near_select(pairs[s, 1], l_ref, c_ref, r_ref, per_column)
        for k in range(kernels):
            near_ref[0, :, k * width : (k + 1) * width] = dot(h_ref[0, k], x).astype(BF16)
        total_ref[pairs[s, 0]] += dot(near_ref[0], w_ref[...].reshape(kernels * width, width))


def back_near_kernel(counts, pairs, ut_ref, w_ref, near_ref, h_ref, out_ref, gd_ref, vt, gdt):
    kernels, points, width = h_ref.shape[1], h_ref.shape[2], w_ref.shape[1]
    s = pl.program_id(0)

    @pl.when(s == 0)
    def _():
        gdt[...] = jnp.zeros_like(gdt)
        for a in range(ut_ref.shape[0]):
            u = ut_ref[a]
            for k in range(kernels):
                vt[a, :, k * points : (k + 1) * points] = dot(w_ref[k], u).astype(BF16)

    @pl.when(s < counts[0])
    def _():
        a = pairs[s, 0]
        out_ref[0] = dot(vt[a], h_ref[0].reshape(kernels * points, points)).astype(BF16)
        gdt[...] += dot(ut_ref[a], near_ref[0])

    @pl.when(s == pl.num_programs(0) - 1)
    def _():
        for k in range(kernels):
            gd_ref[k] = gdt[:, k * width : (k + 1) * width].T


def back_own_kernel(
    per_column,
    counts,
    pairs,
    l_ref,
    c_ref,
    r_ref,
    mt_ref,
    wmt_ref,
    gd_ref,
    h_ref,
    total_ref,
    keep_ref,
    send_ref,
    z,
    gm,
):
    kernels, width = wmt_ref.shape[0], wmt_ref.shape[1]
    half = width // 2
    s = pl.program_id(0)

    @pl.when(s == 0)
    def _():
        total_ref[...] = jnp.zeros_like(total_ref)
        gm[...] = jnp.zeros_like(gm)

    @pl.when(s < counts[0])
    def _():
        a = pairs[s, 0]
        x = near_select(pairs[s, 1], l_ref, c_ref, r_ref, per_column)
        for k in range(kernels):
            z[:, k * width : (k + 1) * width] = dot(h_ref[0, k], x).astype(BF16)
        total_ref[a] += dot(z[...], wmt_ref[...].reshape(kernels * width, width))
        gm[...] += dot(mt_ref[a], z[...])

    @pl.when(s == pl.num_programs(0) - 1)
    def _():
        core = lax.axis_index("block") % 2
        mine = pl.multiple_of(core * half, half)
        other = pl.multiple_of((1 - core) * half, half)
        for k in range(kernels):
            at = (kernels - 1 - k) * width
            keep_ref[k] = gd_ref[k, pl.ds(mine, half)] + gm[pl.ds(mine, half), at : at + width]
            send_ref[k] = (
                gd_ref[k, pl.ds(other, half)] + gm[pl.ds(other, half), at : at + width]
            ).astype(BF16)


def in_column(code, per_column):
    block = jnp.maximum(code - 1, 0)
    here = (code > 0) & (block // per_column == lax.axis_index("block"))
    return here, block


def pick_kernel(per_column, code_l, code_c, code_r, own, up, down, far, to_l, to_c, to_r):
    blocks = own.shape[0]
    regions = per_column // blocks
    me = lax.axis_index("grp")
    for code, out in ((code_l, to_l), (code_c, to_c), (code_r, to_r)):
        for s in range(out.shape[0]):
            here, block = in_column(code[s], per_column)
            away = (block // blocks - me + 2 * regions) % regions
            local = block % blocks
            for distance, source in enumerate((own, up, far, down)):

                @pl.when(here & (away == distance))
                def _(source=source, out=out, s=s, local=local):
                    out[s] = source[local]


def merge_kernel(
    per_column, code_l, code_c, code_r, part_l, part_c, part_r, own, up, down, far, total
):
    blocks = own.shape[0]
    regions = per_column // blocks
    me = lax.axis_index("grp")
    total[...] = jnp.zeros_like(total)
    for code, part in ((code_l, part_l), (code_c, part_c), (code_r, part_r)):
        for s in range(part.shape[0]):
            here, block = in_column(code[s], per_column)
            away = (block // blocks - me + 2 * regions) % regions
            at = away * blocks + block % blocks

            @pl.when(here)
            def _(part=part, s=s, at=at):
                total[at] += part[s].astype(F32)

    own[...] = total[0:blocks]
    for distance, out in ((1, up), (2, far), (3, down)):
        out[...] = total[distance * blocks : (distance + 1) * blocks].astype(BF16)


def rows_below(count, shape):
    return lax.broadcasted_iota(jnp.int32, shape, 0) < count


def summed_rows(x, total, own, one, two, three):
    scattered = own[x] + one[x].astype(F32) + two[x].astype(F32) + three[x].astype(F32)
    return total[x] + scattered.T


def activate_kernel(counts, total, own, one, two, three, cot, act, up, upt):
    for x in range(total.shape[0]):
        rows = summed_rows(x, total, own, one, two, three)
        valid = rows_below(counts[x], rows.shape)
        pre = jnp.where(valid, rows, 0.0)
        sig = jax.nn.sigmoid(pre)
        act[x] = (pre * sig).astype(BF16)
        slope = sig * (1.0 + pre * (1.0 - sig))
        upstream = jnp.where(valid, cot[x].astype(F32) * slope, 0.0)
        up[x] = upstream.astype(BF16)
        upt[x] = upstream.T.astype(BF16)


def finish_kernel(counts, total, own, one, two, three, out):
    for x in range(total.shape[0]):
        rows = summed_rows(x, total, own, one, two, three)
        out[x] = jnp.where(rows_below(counts[x], rows.shape), rows, 0.0).astype(BF16)


def split_kernel(keep, got, own, up, down, far):
    rows = own.shape[1]
    me = lax.axis_index("grp")
    regions = keep.shape[1] // rows

    def piece(distance):
        at = pl.multiple_of((me + distance) % regions * rows, rows)
        return keep[:, pl.ds(at, rows)] + got[:, pl.ds(at, rows)].astype(F32)

    own[...] = piece(0)
    up[...] = piece(1).astype(BF16)
    far[...] = piece(2).astype(BF16)
    down[...] = piece(3).astype(BF16)


def add_kernel(own, one, two, three, out):
    total = own[...] + one[...].astype(F32) + two[...].astype(F32) + three[...].astype(F32)
    out[...] = total.astype(out.dtype)


def ordered_kernel(place, scale, own, below, above, far, out, held):
    me = place()
    held[me] = own[...]
    held[(me + 3) % 4] = below[...]
    held[(me + 1) % 4] = above[...]
    held[(me + 2) % 4] = far[...]
    total = held[0].astype(F32) + held[1].astype(F32) + held[2].astype(F32) + held[3].astype(F32)
    out[...] = (total * scale).astype(out.dtype)


def join_kernel(own, below, above, far, out):
    rows = own.shape[1]
    me = lax.axis_index("grp")
    regions = out.shape[1] // rows
    for distance, part in ((0, own), (1, above), (2, far), (3, below)):
        at = pl.multiple_of((me + distance) % regions * rows, rows)
        out[:, pl.ds(at, rows)] = part[...]


def widen_kernel(own, other, out):
    half = own.shape[1]
    core = lax.axis_index("block") % 2
    out[:, pl.ds(pl.multiple_of(core * half, half), half)] = own[...].astype(F32)
    out[:, pl.ds(pl.multiple_of((1 - core) * half, half), half)] = other[...].astype(F32)


def simple(kernel, args, outs, name, scratch=(), prefetch=0):
    single = not isinstance(outs, (list, tuple))
    outs = [outs] if single else outs
    result = call(
        kernel,
        (1,),
        prefetch,
        [whole(a.shape) for a in args[prefetch:]],
        [whole(o.shape) for o in outs],
        outs,
        list(scratch),
        name,
        size=sum(a.size * a.dtype.itemsize for a in list(args) + list(outs)),
    )(*args)
    return result[0] if single else result


def along_block(x, distance):
    peers = lax.axis_size("block")
    return lax.ppermute(
        x, "block", [(i, i + distance) for i in range(peers) if 0 <= i + distance < peers]
    )


def around_grp(x, distance):
    peers = lax.axis_size("grp")
    return lax.ppermute(x, "grp", [(i, (i + distance) % peers) for i in range(peers)])


def body(features, point_counts, kernel_weights, influence, pair_list, pair_counts, cotangent):
    blocks, points, width = features.shape
    kernels = kernel_weights.shape[0]
    slots = influence.shape[0]
    peers = lax.axis_size("block")
    regions = lax.axis_size("grp")
    per_column = blocks * regions
    flat = kernels * width
    cells = kernels * points * points
    valid = (lax.broadcasted_iota(jnp.int32, (blocks, points), 1) < point_counts[:, None])[
        ..., None
    ]
    masked = jnp.where(valid, features, jnp.zeros_like(features))
    code = jnp.where(jnp.arange(slots) < pair_counts[0], pair_list[:, 1] + 1, 0)
    code_l = along_block(code, 1)
    code_r = along_block(code, -1)
    codes = (code_l, code, code_r)

    rows_b = struct((slots, points, width), BF16)
    rows_t = struct((slots, width, points), BF16)
    own_t = struct((blocks, width, points), BF16)

    def gather_column(values):
        up, down, far = (around_grp(values, d) for d in (-1, 1, 2))
        return simple(
            functools.partial(pick_kernel, per_column),
            (*codes, values, up, down, far),
            [rows_b] * 3,
            "pick_requested",
            prefetch=3,
        )

    def gather_rest(picked):
        to_l, to_c, to_r = picked
        return along_block(to_r, 1), to_c, along_block(to_l, -1)

    def scatter(part):
        part_l, part_r = along_block(part, 1), along_block(part, -1)
        own, up, down, far = simple(
            functools.partial(merge_kernel, per_column),
            (*codes, part_l, part, part_r),
            [struct((blocks, width, points), F32)] + [own_t] * 3,
            "merge_partials",
            scratch=[pltpu.VMEM((per_column, width, points), F32)],
            prefetch=3,
        )
        return own, around_grp(up, 1), around_grp(down, -1), around_grp(far, 2)

    weight_spec = whole((kernels, width, width))
    block_spec = whole((blocks, points, width))
    turned_spec = whole((blocks, width, points))
    pair_spec = per_slot((1, kernels, points, points))
    row_spec = per_slot((1, points, width))
    part_spec = per_slot((1, width, points))
    store_spec = per_slot((1, points, flat))
    pair_flops = 2 * cells * width * slots
    pair_bytes = 2 * cells * slots
    slot_args = (pair_counts, pair_list)

    picked = gather_column(masked)
    to_second, masked_t, mirrored_t = call(
        own_kernel,
        (slots,),
        2,
        [block_spec, weight_spec, pair_spec],
        [part_spec, turned_spec, weight_spec],
        [rows_t, own_t, struct((kernels, width, width), BF16)],
        [pltpu.VMEM((blocks, width, kernels * points), BF16)],
        "own_to_second",
        pair_flops,
        pair_bytes,
    )(*slot_args, masked, kernel_weights, influence)
    near_rows = gather_rest(picked)
    scattered = scatter(to_second)
    total, near_store = call(
        functools.partial(near_kernel, per_column),
        (slots,),
        2,
        [row_spec, row_spec, row_spec, weight_spec, pair_spec],
        [block_spec, store_spec],
        [struct((blocks, points, width), F32), struct((slots, points, flat), BF16)],
        [],
        "near_to_first",
        2 * pair_flops,
        pair_bytes,
    )(*slot_args, *near_rows, kernel_weights, influence)
    activated, upstream, upstream_t = simple(
        activate_kernel,
        (point_counts, total, *scattered, cotangent),
        [struct((blocks, points, width), BF16)] * 2 + [own_t],
        "activate",
        prefetch=1,
    )

    picked = gather_column(upstream)
    to_second, grad_direct = call(
        back_near_kernel,
        (slots,),
        2,
        [turned_spec, weight_spec, store_spec, pair_spec],
        [part_spec, weight_spec],
        [rows_t, struct((kernels, width, width), F32)],
        [pltpu.VMEM((blocks, width, kernels * points), BF16), pltpu.VMEM((width, flat), F32)],
        "back_to_second",
        2 * pair_flops,
        pair_bytes,
    )(*slot_args, upstream_t, kernel_weights, near_store, influence)
    near_upstream = gather_rest(picked)
    scattered = scatter(to_second)
    half_spec = whole((kernels, width // 2, width))
    total, keep, send = call(
        functools.partial(back_own_kernel, per_column),
        (slots,),
        2,
        [row_spec, row_spec, row_spec, turned_spec, weight_spec, weight_spec, pair_spec],
        [block_spec, half_spec, half_spec],
        [
            struct((blocks, points, width), F32),
            struct((kernels, width // 2, width), F32),
            struct((kernels, width // 2, width), BF16),
        ],
        [pltpu.VMEM((points, flat), BF16), pltpu.VMEM((width, flat), F32)],
        "back_to_first",
        2 * pair_flops,
        pair_bytes,
    )(*slot_args, *near_upstream, masked_t, mirrored_t, grad_direct, influence)

    def over_block(x, partner):
        return lax.ppermute(x, "block", [(i, partner(i)) for i in range(peers)])

    def step(stride, distance):
        return lambda i: i + ((i // stride + distance) % 4 - i // stride % 4) * stride

    got = over_block(send, lambda i: i ^ 1)
    quarter = width // 2 // regions
    piece = (kernels, quarter, width)
    own, up, down, far = simple(
        split_kernel, (keep, got), [struct(piece, F32)] + [struct(piece, BF16)] * 3, "split_half"
    )
    got = around_grp(up, 1), around_grp(down, -1), around_grp(far, 2)
    summed = simple(add_kernel, (own, *got), struct(piece, BF16), "add_quarters")
    scale = 1.0 / math.sqrt(blocks * points * peers * regions)
    for stride, factor in ((2, 1.0), (8, scale)):
        got = [over_block(summed, step(stride, d)) for d in (1, -1, 2)]
        summed = simple(
            functools.partial(
                ordered_kernel, lambda n=stride: lax.axis_index("block") // n % 4, factor
            ),
            (summed, *got),
            struct(piece, BF16),
            "add_in_order",
            scratch=[pltpu.VMEM((4,) + piece, BF16)],
        )
    got = [around_grp(summed, d) for d in (1, -1, 2)]
    joined = simple(
        join_kernel, (summed, *got), struct((kernels, width // 2, width), BF16), "join_quarters"
    )
    grad_weights = simple(
        widen_kernel,
        (joined, over_block(joined, lambda i: i ^ 1)),
        struct((kernels, width, width), F32),
        "join_halves",
    )
    grad_features = simple(
        finish_kernel,
        (point_counts, total, *scattered),
        struct((blocks, points, width), BF16),
        "finish_features",
        prefetch=1,
    )
    return (activated, grad_features, grad_weights)


def solution(mesh):
    placed = (
        P(("block", "grp"), None, None),
        P(("block", "grp")),
        P(),
        P(("block", "grp"), None, None, None),
        P(("block", "grp"), None),
        P(("block", "grp")),
        P(("block", "grp"), None, None),
    )
    return jax.shard_map(
        body,
        mesh=mesh,
        in_specs=placed,
        out_specs=(P(("block", "grp"), None, None), P(("block", "grp"), None, None), P()),
        check_vma=False,
    )
```

time: 715 us -> 169 us (0.24)
  waiting for transfers between devices: 412 us -> 21.9 us
  matrix products: 88.1 us -> 0 us
  loops' own time: 42.4 us -> 0 us
  Pallas kernels: 0 us -> 40.6 us
  local copies, waits for them, and re-layouts: 40.5 us -> 1.8 us
  other arithmetic: 37.4 us -> 2.62 us
  starting transfers between devices: 76.6 us -> 97.3 us
  between operations: 14 us -> 1.59 us
    psum x1 -> x0, waiting for transfers between devices: 190 us -> none  [body(): total_weights = lax.psum(local_weights, ('block', 'grp'))]
    reduce_scatter x2 -> x0, waiting for transfers between devices: 112 us -> none  [collect(): lax.psum_scatter(partial_value[1] + from_lower + from_upper, 'grp', scatt...]
    dot_general x40 -> x0, matrix products: 88.1 us -> none  [the longest x4 14.4 us: backward_pair(): jnp.einsum('kij,ikc->jc', tile, back_near, preferred_element_type=jnp.flo...]
    all_gather x2 -> x0, waiting for transfers between devices: 49.6 us -> none  [neighbours(): region = lax.all_gather(values, 'grp', axis=0, tiled=True)]
    another operation x2 -> x0, loops' own time: 42.4 us -> none  [the longest x1 21.7 us: body(): lax.fori_loop(0, used, forward_pair, (own_zero, sent_zero, store_zero, st...]
    pallas_call x0 -> x16, Pallas kernels: none -> 40.6 us  [the longest x12 9.83 us: simple(): call(kernel, (1,), prefetch, [whole(a.shape) for a in args[prefetch:]], [...]
    ppermute x8 -> x36, waiting for transfers between devices: 60 us -> 21.9 us  [the longest x18 8.85 us: around_grp(): lax.ppermute(x, 'grp', [(i, (i + distance) % peers) for i in range(peers)])]
    ppermute x8 -> x36, starting transfers between devices: 76.4 us -> 97.3 us  [the longest x10 37.2 us: along_block(): lax.ppermute(x, 'block', [(i, i + distance) for i in range(peers) if 0 <=...]
  transfers between devices with their start and end apart: 13 -> 36, of which waited for: 13 -> 13; matrix products, arithmetic and copies ran while one was open for 1% -> 1% of each run, Pallas kernels for 0% -> 22%
where the time goes in v1:
time: 169 us; the launch traced here: 166 us
  starting transfers between devices  97.3 us (58%)
  Pallas kernels  40.6 us (24%)
  waiting for transfers between devices  21.9 us (13%)
  other arithmetic  2.62 us (2%)
  local copies, waits for them, and re-layouts  1.8 us (1%)
    ppermute x10, starting transfers between devices, along_block(): lax.ppermute(x, 'block', [(i, i + distance) for i in range(peers) if 0 <=...  37.2 us
    ppermute x18, starting transfers between devices, around_grp(): lax.ppermute(x, 'grp', [(i, (i + distance) % peers) for i in range(peers)])  34.6 us
    ppermute x8, starting transfers between devices, over_block(): return lax.ppermute(x, 'block', [(i, partner(i)) for i in range(peers)])  25.5 us
    pallas_call x12, Pallas kernels, simple(): call(kernel, (1,), prefetch, [whole(a.shape) for a in args[prefetch:]], [...  9.83 us
    ppermute x18, waiting for transfers between devices, around_grp(): lax.ppermute(x, 'grp', [(i, (i + distance) % peers) for i in range(peers)])  8.85 us
    pallas_call x1, Pallas kernels, body(): call(functools.partial(near_kernel, per_column), (slots,), 2, [row_spec,...  8.31 us
    pallas_call x1, Pallas kernels, body(): call(back_near_kernel, (slots,), 2, [turned_spec, weight_spec, store_spec...  8.26 us
    ppermute x8, waiting for transfers between devices, over_block(): return lax.ppermute(x, 'block', [(i, partner(i)) for i in range(peers)])  8.1 us
  transfers between devices with their start and end apart: 36, of which 13 were waited for; matrix products, arithmetic and copies ran while one was open for 1% of the time, Pallas kernels for 22%

profile of v1, /device:TPU:1, one launch (start us, length us, event | category | flops | bytes accessed | tf_op | source)
XLA Modules:
  0.0 165.8 jit_solution(5214900546245547264)
XLA Ops:
  2.6 3.8 %collective-permute-start.4 = (bf16[4,256,128]{2,1,0:T(8,128)(2,1)S(1)}, bf16[4,256,128]{2,1,0:T(8,128)(2,1)S(1)}, u32[]{:S(2)}, u32[]{:S(2)}) collective-permute-start(bf16[4,256,128]{2,1,0:T(8,128)(2,1)S(1)} %broadcast_select_fusion.own.m_ref), channel_id=1, source_target_pairs={{0,2},{1,3},{2,0},{3,1},{4,6},{5,7},{6,4},{7,5},{8,10},{9,11},{10,... | collective-permute-start | bytes 786440 | tf_op jit(solution)/shard_map/ppermute | solution.py:311
  6.8 2.3 %collective-permute-start.2 = (bf16[4,256,128]{2,1,0:T(8,128)(2,1)S(1)}, bf16[4,256,128]{2,1,0:T(8,128)(2,1)S(1)}, u32[]{:S(2)}, u32[]{:S(2)}) collective-permute-start(bf16[4,256,128]{2,1,0:T(8,128)(2,1)S(1)} %broadcast_select_fusion.own.m_ref), channel_id=1, source_target_pairs={{0,3},{1,0},{2,1},{3,2},{4,7},{5,4},{6,5},{7,6},{8,11},{9,8},{10,9... | collective-permute-start | bytes 786440 | tf_op jit(solution)/shard_map/ppermute | solution.py:311
  10.4 3.4 %collective-permute-start.1 = (s32[8]{0:T(128)S(1)}, s32[8]{0:T(128)S(1)}, u32[]{:S(2)}, u32[]{:S(2)}) collective-permute-start(s32[8]{0:T(128)S(1)} %compare_select_fusion.code_c), channel_id=1, source_target_pairs={{4,0},{8,4},{12,8},{16,12},{20,16},{24,20},{28,24},{32,28},{36,32}... | collective-permute-start | bytes 104 | tf_op jit(solution)/shard_map/ppermute | solution.py:304
  13.8 3.0 %collective-permute-start = (s32[8]{0:T(128)S(1)}, s32[8]{0:T(128)S(1)}, u32[]{:S(2)}, u32[]{:S(2)}) collective-permute-start(s32[8]{0:T(128)S(1)} %compare_select_fusion.code_c), channel_id=1, source_target_pairs={{0,4},{4,8},{8,12},{12,16},{16,20},{20,24},{24,28},{28,32},{32,36}... | collective-permute-start | bytes 104 | tf_op jit(solution)/shard_map/ppermute | solution.py:304
  18.7 6.7 %own_to_second.1 = (bf16[8,128,256]{2,1,0:T(8,128)(2,1)S(1)}, bf16[4,128,256]{2,1,0:T(8,128)(2,1)S(1)}, bf16[15,128,128]{2,1,0:T(8,128)(2,1)S(1)}) custom-call(s32[1]{0:T(128)} %copy.14.counts, s32[8,2]{1,0:T(8,128)S(1)} %copy.10.pairs, bf16[4,256,128]{2,1,0:T(8,128)(2,1)S(1)} %broadcast_select_fusion.own.m_ref, bf16[15,128,128]{2,1,0:T(8,128)(2,1)S(1)} %copy-done, ...), custom_call_target="tpu_custom_call" | custom-call | flops 2013265920 | bytes 15728640 | tf_op jit(solution)/shard_map/own_to_second/pallas_call | solution.py:374
  27.3 4.5 %collective-permute-start.7 = (bf16[8,128,256]{2,1,0:T(8,128)(2,1)S(1)}, bf16[8,128,256]{2,1,0:T(8,128)(2,1)S(1)}, u32[]{:S(2)}, u32[]{:S(2)}) collective-permute-start(bf16[8,128,256]{2,1,0:T(8,128)(2,1)S(1)} %get-tuple-element.38.part_c), channel_id=1, source_target_pairs={{0,4},{4,8},{8,12},{12,16},{16,20},{20,24},{24,28},{28,32},{32,36}... | collective-permute-start | bytes 1572872 | tf_op jit(solution)/shard_map/ppermute | solution.py:304
  33.3 5.1 %collective-permute-start.5 = (bf16[8,256,128]{2,1,0:T(8,128)(2,1)S(1)}, bf16[8,256,128]{2,1,0:T(8,128)(2,1)S(1)}, u32[]{:S(2)}, u32[]{:S(2)}) collective-permute-start(bf16[8,256,128]{2,1,0:T(8,128)(2,1)S(1)} %get-tuple-element.34), channel_id=1, source_target_pairs={{0,4},{4,8},{8,12},{12,16},{16,20},{20,24},{24,28},{28,32},{32,36}... | collective-permute-start | bytes 1572872 | tf_op jit(solution)/shard_map/ppermute | solution.py:304
  41.6 2.7 %collective-permute-start.10 = (bf16[4,128,256]{2,1,0:T(8,128)(2,1)S(1)}, bf16[4,128,256]{2,1,0:T(8,128)(2,1)S(1)}, u32[]{:S(2)}, u32[]{:S(2)}) collective-permute-start(bf16[4,128,256]{2,1,0:T(8,128)(2,1)S(1)} %get-tuple-element.41), channel_id=1, source_target_pairs={{0,3},{1,0},{2,1},{3,2},{4,7},{5,4},{6,5},{7,6},{8,11},{9,8},{10,9... | collective-permute-start | bytes 786440 | tf_op jit(solution)/shard_map/ppermute | solution.py:311
  44.4 4.7 %collective-permute-done.6.r_ref = bf16[8,256,128]{2,1,0:T(8,128)(2,1)S(1)} collective-permute-done((bf16[8,256,128]{2,1,0:T(8,128)(2,1)S(1)}, bf16[8,256,128]{2,1,0:T(8,128)(2,1)S(1)}, u32[]{:S(2)}, u32[]{:S(2)}) %collective-permute-start.6) | collective-permute-done | bytes 524320 | tf_op jit(solution)/shard_map/ppermute | solution.py:304
  49.1 8.3 %near_to_first.1 = (f32[4,256,128]{2,1,0:T(8,128)S(1)}, bf16[8,256,1920]{2,1,0:T(8,128)(2,1)}) custom-call(s32[1]{0:T(128)} %copy.14.counts, s32[8,2]{1,0:T(8,128)S(1)} %copy.10.pairs, bf16[8,256,128]{2,1,0:T(8,128)(2,1)S(1)} %collective-permute-done.5.l_ref, bf16[8,256,128]{2,1,0:T(8,128)(2,1)S(1)} %get-tuple-element.35.c_ref, ...), custom_call_target="tpu_custom_call" | custom-call | flops 4026531840 | bytes 15728640 | tf_op jit(solution)/shard_map/near_to_first/pallas_call | solution.py:388
  59.2 5.2 %collective-permute-start.14 = (bf16[4,256,128]{2,1,0:T(8,128)(2,1)S(1)}, bf16[4,256,128]{2,1,0:T(8,128)(2,1)S(1)}, u32[]{:S(2)}, u32[]{:S(2)}) collective-permute-start(bf16[4,256,128]{2,1,0:T(8,128)(2,1)S(1)} %get-tuple-element.44.own), channel_id=1, source_target_pairs={{0,2},{1,3},{2,0},{3,1},{4,6},{5,7},{6,4},{7,5},{8,10},{9,11},{10,... | collective-permute-start | bytes 786440 | tf_op jit(solution)/shard_map/ppermute | solution.py:311
  64.4 2.7 %collective-permute-start.12 = (bf16[4,256,128]{2,1,0:T(8,128)(2,1)S(1)}, bf16[4,256,128]{2,1,0:T(8,128)(2,1)S(1)}, u32[]{:S(2)}, u32[]{:S(2)}) collective-permute-start(bf16[4,256,128]{2,1,0:T(8,128)(2,1)S(1)} %get-tuple-element.44.own), channel_id=1, source_target_pairs={{0,3},{1,0},{2,1},{3,2},{4,7},{5,4},{6,5},{7,6},{8,11},{9,8},{10,9... | collective-permute-start | bytes 786440 | tf_op jit(solution)/shard_map/ppermute | solution.py:311
  68.2 2.8 %collective-permute-done.13.down = bf16[4,256,128]{2,1,0:T(8,128)(2,1)S(1)} collective-permute-done((bf16[4,256,128]{2,1,0:T(8,128)(2,1)S(1)}, bf16[4,256,128]{2,1,0:T(8,128)(2,1)S(1)}, u32[]{:S(2)}, u32[]{:S(2)}) %collective-permute-start.13) | collective-permute-done | bytes 262176 | tf_op jit(solution)/shard_map/ppermute | solution.py:311
  72.5 7.2 %collective-permute-start.15 = (bf16[8,256,128]{2,1,0:T(8,128)(2,1)S(1)}, bf16[8,256,128]{2,1,0:T(8,128)(2,1)S(1)}, u32[]{:S(2)}, u32[]{:S(2)}) collective-permute-start(bf16[8,256,128]{2,1,0:T(8,128)(2,1)S(1)} %get-tuple-element.45), channel_id=1, source_target_pairs={{0,4},{4,8},{8,12},{12,16},{16,20},{20,24},{24,28},{28,32},{32,36}... | collective-permute-start | bytes 1572872 | tf_op jit(solution)/shard_map/ppermute | solution.py:304
  81.8 8.3 %back_to_second.1 = (bf16[8,128,256]{2,1,0:T(8,128)(2,1)S(1)}, f32[15,128,128]{2,1,0:T(8,128)S(1)}) custom-call(s32[1]{0:T(128)} %copy.14.counts, s32[8,2]{1,0:T(8,128)S(1)} %copy.10.pairs, bf16[4,128,256]{2,1,0:T(8,128)(2,1)S(1)} %get-tuple-element.50.ut_ref, bf16[15,128,128]{2,1,0:T(8,128)(2,1)S(1)} %copy-done.1, ...), custom_call_target="tpu_custom_call" | custom-call | flops 4026531840 | bytes 15728640 | tf_op jit(solution)/shard_map/back_to_second/pallas_call | solution.py:409
  92.0 6.2 %collective-permute-start.17 = (bf16[8,128,256]{2,1,0:T(8,128)(2,1)S(1)}, bf16[8,128,256]{2,1,0:T(8,128)(2,1)S(1)}, u32[]{:S(2)}, u32[]{:S(2)}) collective-permute-start(bf16[8,128,256]{2,1,0:T(8,128)(2,1)S(1)} %get-tuple-element.54.part_c), channel_id=1, source_target_pairs={{0,4},{4,8},{8,12},{12,16},{16,20},{20,24},{24,28},{28,32},{32,36}... | collective-permute-start | bytes 1572872 | tf_op jit(solution)/shard_map/ppermute | solution.py:304
  98.2 7.5 %back_to_first.1 = (f32[4,256,128]{2,1,0:T(8,128)S(1)}, f32[15,64,128]{2,1,0:T(8,128)S(1)}, bf16[15,64,128]{2,1,0:T(8,128)(2,1)S(1)}) custom-call(s32[1]{0:T(128)} %copy.14.counts, s32[8,2]{1,0:T(8,128)S(1)} %copy.10.pairs, bf16[8,256,128]{2,1,0:T(8,128)(2,1)S(1)} %collective-permute-done.15.l_ref, bf16[8,256,128]{2,1,0:T(8,128)(2,1)S(1)} %get-tuple-element.46.c_ref, ...), custom_call_target="tpu_custom_call" | custom-call | flops 4026531840 | bytes 15728640 | tf_op jit(solution)/shard_map/back_to_first/pallas_call | solution.py:424
  107.4 3.9 %collective-permute-start.23 = (bf16[15,16,128]{2,1,0:T(8,128)(2,1)S(1)}, bf16[15,16,128]{2,1,0:T(8,128)(2,1)S(1)}, u32[]{:S(2)}, u32[]{:S(2)}) collective-permute-start(bf16[15,16,128]{2,1,0:T(8,128)(2,1)S(1)} %get-tuple-element.62), channel_id=1, source_target_pairs={{0,1},{1,2},{2,3},{3,0},{4,5},{5,6},{6,7},{7,4},{8,9},{9,10},{10,1... | collective-permute-start | bytes 184328 | tf_op jit(solution)/shard_map/ppermute | solution.py:311
  111.3 7.4 %collective-permute-start.25 = (bf16[15,16,128]{2,1,0:T(8,128)(2,1)S(1)}, bf16[15,16,128]{2,1,0:T(8,128)(2,1)S(1)}, u32[]{:S(2)}, u32[]{:S(2)}) collective-permute-start(bf16[15,16,128]{2,1,0:T(8,128)(2,1)S(1)} %get-tuple-element.64), channel_id=1, source_target_pairs={{0,2},{1,3},{2,0},{3,1},{4,6},{5,7},{6,4},{7,5},{8,10},{9,11},{10,... | collective-permute-start | bytes 184328 | tf_op jit(solution)/shard_map/ppermute | solution.py:311
  120.4 6.5 %collective-permute-start.28 = (bf16[15,16,128]{2,1,0:T(8,128)(2,1)S(1)}, bf16[15,16,128]{2,1,0:T(8,128)(2,1)S(1)}, u32[]{:S(2)}, u32[]{:S(2)}) collective-permute-start(bf16[15,16,128]{2,1,0:T(8,128)(2,1)S(1)} %add_quarters.1.own), channel_id=1, source_target_pairs={{0,16},{4,20},{8,24},{12,28},{16,0},{20,4},{24,8},{28,12},{32,48},... | collective-permute-start | bytes 184328 | tf_op jit(solution)/shard_map/ppermute | solution.py:442
  129.7 2.3 %collective-permute-done.27.above = bf16[15,16,128]{2,1,0:T(8,128)(2,1)S(1)} collective-permute-done((bf16[15,16,128]{2,1,0:T(8,128)(2,1)S(1)}, bf16[15,16,128]{2,1,0:T(8,128)(2,1)S(1)}, u32[]{:S(2)}, u32[]{:S(2)}) %collective-permute-start.27) | collective-permute-done | bytes 61472 | tf_op jit(solution)/shard_map/ppermute | solution.py:442
  133.5 8.3 %collective-permute-start.31 = (bf16[15,16,128]{2,1,0:T(8,128)(2,1)S(1)}, bf16[15,16,128]{2,1,0:T(8,128)(2,1)S(1)}, u32[]{:S(2)}, u32[]{:S(2)}) collective-permute-start(bf16[15,16,128]{2,1,0:T(8,128)(2,1)S(1)} %add_in_order.2.own), channel_id=1, source_target_pairs={{0,64},{4,68},{8,72},{12,76},{16,80},{20,84},{24,88},{28,92},{32,9... | collective-permute-start | bytes 184328 | tf_op jit(solution)/shard_map/ppermute | solution.py:442
  153.5 6.4 %collective-permute-start.35 = (bf16[15,64,128]{2,1,0:T(8,128)(2,1)S(1)}, bf16[15,64,128]{2,1,0:T(8,128)(2,1)S(1)}, u32[]{:S(2)}, u32[]{:S(2)}) collective-permute-start(bf16[15,64,128]{2,1,0:T(8,128)(2,1)S(1)} %join_quarters.1.own), channel_id=1, source_target_pairs={{0,4},{4,0},{8,12},{12,8},{16,20},{20,16},{24,28},{28,24},{32,36},... | collective-permute-start | bytes 737288 | tf_op jit(solution)/shard_map/ppermute | solution.py:442
  159.9 3.3 %collective-permute-done.21.three = bf16[4,128,256]{2,1,0:T(8,128)(2,1)S(1)} collective-permute-done((bf16[4,128,256]{2,1,0:T(8,128)(2,1)S(1)}, bf16[4,128,256]{2,1,0:T(8,128)(2,1)S(1)}, u32[]{:S(2)}, u32[]{:S(2)}) %collective-permute-start.21) | collective-permute-done | bytes 262176 | tf_op jit(solution)/shard_map/ppermute | solution.py:311
  (76 shorter events, 41.7 us)
Async XLA Ops:
  2.6 29.2 %collective-permute-start.4 = (bf16[4,256,128]{2,1,0:T(8,128)(2,1)S(1)}, bf16[4,256,128]{2,1,0:T(8,128)(2,1)S(1)}, u32[]{:S(2)}, u32[]{:S(2)}) collective-permute-start(bf16[4,256,128]{2,1,0:T(8,128)(2,1)S(1)} %broadcast_select_fusion.own.m_ref), channel_id=1, source_target_pairs={{0,2},{1,3},{2,0},{3,1},{4,6},{5,7},{6,4},{7,5},{8,10},{9,11},{10,... | collective-permute-start | bytes 786440 | tf_op jit(solution)/shard_map/ppermute | solution.py:311
  6.4 25.4 %collective-permute-start.3 = (bf16[4,256,128]{2,1,0:T(8,128)(2,1)S(1)}, bf16[4,256,128]{2,1,0:T(8,128)(2,1)S(1)}, u32[]{:S(2)}, u32[]{:S(2)}) collective-permute-start(bf16[4,256,128]{2,1,0:T(8,128)(2,1)S(1)} %broadcast_select_fusion.own.m_ref), channel_id=1, source_target_pairs={{0,1},{1,2},{2,3},{3,0},{4,5},{5,6},{6,7},{7,4},{8,9},{9,10},{10,1... | collective-permute-start | bytes 786440 | tf_op jit(solution)/shard_map/ppermute | solution.py:311
  6.8 25.0 %collective-permute-start.2 = (bf16[4,256,128]{2,1,0:T(8,128)(2,1)S(1)}, bf16[4,256,128]{2,1,0:T(8,128)(2,1)S(1)}, u32[]{:S(2)}, u32[]{:S(2)}) collective-permute-start(bf16[4,256,128]{2,1,0:T(8,128)(2,1)S(1)} %broadcast_select_fusion.own.m_ref), channel_id=1, source_target_pairs={{0,3},{1,0},{2,1},{3,2},{4,7},{5,4},{6,5},{7,6},{8,11},{9,8},{10,9... | collective-permute-start | bytes 786440 | tf_op jit(solution)/shard_map/ppermute | solution.py:311
  10.4 14.9 %collective-permute-start.1 = (s32[8]{0:T(128)S(1)}, s32[8]{0:T(128)S(1)}, u32[]{:S(2)}, u32[]{:S(2)}) collective-permute-start(s32[8]{0:T(128)S(1)} %compare_select_fusion.code_c), channel_id=1, source_target_pairs={{4,0},{8,4},{12,8},{16,12},{20,16},{24,20},{28,24},{32,28},{36,32}... | collective-permute-start | bytes 104 | tf_op jit(solution)/shard_map/ppermute | solution.py:304
  13.8 13.4 %collective-permute-start = (s32[8]{0:T(128)S(1)}, s32[8]{0:T(128)S(1)}, u32[]{:S(2)}, u32[]{:S(2)}) collective-permute-start(s32[8]{0:T(128)S(1)} %compare_select_fusion.code_c), channel_id=1, source_target_pairs={{0,4},{4,8},{8,12},{12,16},{16,20},{20,24},{24,28},{28,32},{32,36}... | collective-permute-start | bytes 104 | tf_op jit(solution)/shard_map/ppermute | solution.py:304
  25.4 14.9 %collective-permute-start.8 = (bf16[8,128,256]{2,1,0:T(8,128)(2,1)S(1)}, bf16[8,128,256]{2,1,0:T(8,128)(2,1)S(1)}, u32[]{:S(2)}, u32[]{:S(2)}) collective-permute-start(bf16[8,128,256]{2,1,0:T(8,128)(2,1)S(1)} %get-tuple-element.38.part_c), channel_id=1, source_target_pairs={{4,0},{8,4},{12,8},{16,12},{20,16},{24,20},{28,24},{32,28},{36,32}... | collective-permute-start | bytes 1572872 | tf_op jit(solution)/shard_map/ppermute | solution.py:304
  27.3 13.0 %collective-permute-start.7 = (bf16[8,128,256]{2,1,0:T(8,128)(2,1)S(1)}, bf16[8,128,256]{2,1,0:T(8,128)(2,1)S(1)}, u32[]{:S(2)}, u32[]{:S(2)}) collective-permute-start(bf16[8,128,256]{2,1,0:T(8,128)(2,1)S(1)} %get-tuple-element.38.part_c), channel_id=1, source_target_pairs={{0,4},{4,8},{8,12},{12,16},{16,20},{20,24},{24,28},{28,32},{32,36}... | collective-permute-start | bytes 1572872 | tf_op jit(solution)/shard_map/ppermute | solution.py:304
  33.3 11.2 %collective-permute-start.5 = (bf16[8,256,128]{2,1,0:T(8,128)(2,1)S(1)}, bf16[8,256,128]{2,1,0:T(8,128)(2,1)S(1)}, u32[]{:S(2)}, u32[]{:S(2)}) collective-permute-start(bf16[8,256,128]{2,1,0:T(8,128)(2,1)S(1)} %get-tuple-element.34), channel_id=1, source_target_pairs={{0,4},{4,8},{8,12},{12,16},{16,20},{20,24},{24,28},{28,32},{32,36}... | collective-permute-start | bytes 1572872 | tf_op jit(solution)/shard_map/ppermute | solution.py:304
  38.3 10.8 %collective-permute-start.6 = (bf16[8,256,128]{2,1,0:T(8,128)(2,1)S(1)}, bf16[8,256,128]{2,1,0:T(8,128)(2,1)S(1)}, u32[]{:S(2)}, u32[]{:S(2)}) collective-permute-start(bf16[8,256,128]{2,1,0:T(8,128)(2,1)S(1)} %get-tuple-element.36), channel_id=1, source_target_pairs={{4,0},{8,4},{12,8},{16,12},{20,16},{24,20},{28,24},{32,28},{36,32}... | collective-permute-start | bytes 1572872 | tf_op jit(solution)/shard_map/ppermute | solution.py:304
  41.5 16.0 %collective-permute-start.9 = (bf16[4,128,256]{2,1,0:T(8,128)(2,1)S(1)}, bf16[4,128,256]{2,1,0:T(8,128)(2,1)S(1)}, u32[]{:S(2)}, u32[]{:S(2)}) collective-permute-start(bf16[4,128,256]{2,1,0:T(8,128)(2,1)S(1)} %get-tuple-element.40), channel_id=1, source_target_pairs={{0,1},{1,2},{2,3},{3,0},{4,5},{5,6},{6,7},{7,4},{8,9},{9,10},{10,1... | collective-permute-start | bytes 786440 | tf_op jit(solution)/shard_map/ppermute | solution.py:311
  41.6 15.9 %collective-permute-start.10 = (bf16[4,128,256]{2,1,0:T(8,128)(2,1)S(1)}, bf16[4,128,256]{2,1,0:T(8,128)(2,1)S(1)}, u32[]{:S(2)}, u32[]{:S(2)}) collective-permute-start(bf16[4,128,256]{2,1,0:T(8,128)(2,1)S(1)} %get-tuple-element.41), channel_id=1, source_target_pairs={{0,3},{1,0},{2,1},{3,2},{4,7},{5,4},{6,5},{7,6},{8,11},{9,8},{10,9... | collective-permute-start | bytes 786440 | tf_op jit(solution)/shard_map/ppermute | solution.py:311
  44.2 13.2 %collective-permute-start.11 = (bf16[4,128,256]{2,1,0:T(8,128)(2,1)S(1)}, bf16[4,128,256]{2,1,0:T(8,128)(2,1)S(1)}, u32[]{:S(2)}, u32[]{:S(2)}) collective-permute-start(bf16[4,128,256]{2,1,0:T(8,128)(2,1)S(1)} %get-tuple-element.42), channel_id=1, source_target_pairs={{0,2},{1,3},{2,0},{3,1},{4,6},{5,7},{6,4},{7,5},{8,10},{9,11},{10,... | collective-permute-start | bytes 786440 | tf_op jit(solution)/shard_map/ppermute | solution.py:311
  59.2 9.0 %collective-permute-start.14 = (bf16[4,256,128]{2,1,0:T(8,128)(2,1)S(1)}, bf16[4,256,128]{2,1,0:T(8,128)(2,1)S(1)}, u32[]{:S(2)}, u32[]{:S(2)}) collective-permute-start(bf16[4,256,128]{2,1,0:T(8,128)(2,1)S(1)} %get-tuple-element.44.own), channel_id=1, source_target_pairs={{0,2},{1,3},{2,0},{3,1},{4,6},{5,7},{6,4},{7,5},{8,10},{9,11},{10,... | collective-permute-start | bytes 786440 | tf_op jit(solution)/shard_map/ppermute | solution.py:311
  72.5 25.7 %collective-permute-start.15 = (bf16[8,256,128]{2,1,0:T(8,128)(2,1)S(1)}, bf16[8,256,128]{2,1,0:T(8,128)(2,1)S(1)}, u32[]{:S(2)}, u32[]{:S(2)}) collective-permute-start(bf16[8,256,128]{2,1,0:T(8,128)(2,1)S(1)} %get-tuple-element.45), channel_id=1, source_target_pairs={{0,4},{4,8},{8,12},{12,16},{16,20},{20,24},{24,28},{28,32},{32,36}... | collective-permute-start | bytes 1572872 | tf_op jit(solution)/shard_map/ppermute | solution.py:304
  79.7 18.5 %collective-permute-start.16 = (bf16[8,256,128]{2,1,0:T(8,128)(2,1)S(1)}, bf16[8,256,128]{2,1,0:T(8,128)(2,1)S(1)}, u32[]{:S(2)}, u32[]{:S(2)}) collective-permute-start(bf16[8,256,128]{2,1,0:T(8,128)(2,1)S(1)} %get-tuple-element.47), channel_id=1, source_target_pairs={{4,0},{8,4},{12,8},{16,12},{20,16},{24,20},{28,24},{32,28},{36,32}... | collective-permute-start | bytes 1572872 | tf_op jit(solution)/shard_map/ppermute | solution.py:304
  90.0 58.7 %collective-permute-start.18 = (bf16[8,128,256]{2,1,0:T(8,128)(2,1)S(1)}, bf16[8,128,256]{2,1,0:T(8,128)(2,1)S(1)}, u32[]{:S(2)}, u32[]{:S(2)}) collective-permute-start(bf16[8,128,256]{2,1,0:T(8,128)(2,1)S(1)} %get-tuple-element.54.part_c), channel_id=1, source_target_pairs={{4,0},{8,4},{12,8},{16,12},{20,16},{24,20},{28,24},{32,28},{36,32}... | collective-permute-start | bytes 1572872 | tf_op jit(solution)/shard_map/ppermute | solution.py:304
  92.0 56.8 %collective-permute-start.17 = (bf16[8,128,256]{2,1,0:T(8,128)(2,1)S(1)}, bf16[8,128,256]{2,1,0:T(8,128)(2,1)S(1)}, u32[]{:S(2)}, u32[]{:S(2)}) collective-permute-start(bf16[8,128,256]{2,1,0:T(8,128)(2,1)S(1)} %get-tuple-element.54.part_c), channel_id=1, source_target_pairs={{0,4},{4,8},{8,12},{12,16},{16,20},{20,24},{24,28},{28,32},{32,36}... | collective-permute-start | bytes 1572872 | tf_op jit(solution)/shard_map/ppermute | solution.py:304
  107.4 11.4 %collective-permute-start.23 = (bf16[15,16,128]{2,1,0:T(8,128)(2,1)S(1)}, bf16[15,16,128]{2,1,0:T(8,128)(2,1)S(1)}, u32[]{:S(2)}, u32[]{:S(2)}) collective-permute-start(bf16[15,16,128]{2,1,0:T(8,128)(2,1)S(1)} %get-tuple-element.62), channel_id=1, source_target_pairs={{0,1},{1,2},{2,3},{3,0},{4,5},{5,6},{6,7},{7,4},{8,9},{9,10},{10,1... | collective-permute-start | bytes 184328 | tf_op jit(solution)/shard_map/ppermute | solution.py:311
  111.3 9.0 %collective-permute-start.25 = (bf16[15,16,128]{2,1,0:T(8,128)(2,1)S(1)}, bf16[15,16,128]{2,1,0:T(8,128)(2,1)S(1)}, u32[]{:S(2)}, u32[]{:S(2)}) collective-permute-start(bf16[15,16,128]{2,1,0:T(8,128)(2,1)S(1)} %get-tuple-element.64), channel_id=1, source_target_pairs={{0,2},{1,3},{2,0},{3,1},{4,6},{5,7},{6,4},{7,5},{8,10},{9,11},{10,... | collective-permute-start | bytes 184328 | tf_op jit(solution)/shard_map/ppermute | solution.py:311
  120.4 9.3 %collective-permute-start.28 = (bf16[15,16,128]{2,1,0:T(8,128)(2,1)S(1)}, bf16[15,16,128]{2,1,0:T(8,128)(2,1)S(1)}, u32[]{:S(2)}, u32[]{:S(2)}) collective-permute-start(bf16[15,16,128]{2,1,0:T(8,128)(2,1)S(1)} %add_quarters.1.own), channel_id=1, source_target_pairs={{0,16},{4,20},{8,24},{12,28},{16,0},{20,4},{24,8},{28,12},{32,48},... | collective-permute-start | bytes 184328 | tf_op jit(solution)/shard_map/ppermute | solution.py:442
  133.5 9.9 %collective-permute-start.31 = (bf16[15,16,128]{2,1,0:T(8,128)(2,1)S(1)}, bf16[15,16,128]{2,1,0:T(8,128)(2,1)S(1)}, u32[]{:S(2)}, u32[]{:S(2)}) collective-permute-start(bf16[15,16,128]{2,1,0:T(8,128)(2,1)S(1)} %add_in_order.2.own), channel_id=1, source_target_pairs={{0,64},{4,68},{8,72},{12,76},{16,80},{20,84},{24,88},{28,92},{32,9... | collective-permute-start | bytes 184328 | tf_op jit(solution)/shard_map/ppermute | solution.py:442
  150.0 9.9 %collective-permute-start.19 = (bf16[4,128,256]{2,1,0:T(8,128)(2,1)S(1)}, bf16[4,128,256]{2,1,0:T(8,128)(2,1)S(1)}, u32[]{:S(2)}, u32[]{:S(2)}) collective-permute-start(bf16[4,128,256]{2,1,0:T(8,128)(2,1)S(1)} %get-tuple-element.56), channel_id=1, source_target_pairs={{0,1},{1,2},{2,3},{3,0},{4,5},{5,6},{6,7},{7,4},{8,9},{9,10},{10,1... | collective-permute-start | bytes 786440 | tf_op jit(solution)/shard_map/ppermute | solution.py:311
  152.7 10.5 %collective-permute-start.21 = (bf16[4,128,256]{2,1,0:T(8,128)(2,1)S(1)}, bf16[4,128,256]{2,1,0:T(8,128)(2,1)S(1)}, u32[]{:S(2)}, u32[]{:S(2)}) collective-permute-start(bf16[4,128,256]{2,1,0:T(8,128)(2,1)S(1)} %get-tuple-element.58), channel_id=1, source_target_pairs={{0,2},{1,3},{2,0},{3,1},{4,6},{5,7},{6,4},{7,5},{8,10},{9,11},{10,... | collective-permute-start | bytes 786440 | tf_op jit(solution)/shard_map/ppermute | solution.py:311
  153.5 11.2 %collective-permute-start.35 = (bf16[15,64,128]{2,1,0:T(8,128)(2,1)S(1)}, bf16[15,64,128]{2,1,0:T(8,128)(2,1)S(1)}, u32[]{:S(2)}, u32[]{:S(2)}) collective-permute-start(bf16[15,64,128]{2,1,0:T(8,128)(2,1)S(1)} %join_quarters.1.own), channel_id=1, source_target_pairs={{0,4},{4,0},{8,12},{12,8},{16,20},{20,16},{24,28},{28,24},{32,36},... | collective-permute-start | bytes 737288 | tf_op jit(solution)/shard_map/ppermute | solution.py:442
  (16 other events, 192.7 us)

commit v2 on v0

v2 whole, which is shorter than its diff:
```python
import functools
import math

import jax
import jax.numpy as jnp
from jax import lax
from jax.experimental import pallas as pl
from jax.experimental.pallas import tpu as pltpu
from jax.sharding import PartitionSpec as P

BF16 = jnp.bfloat16
F32 = jnp.float32
MIB = 1024 * 1024


def dot(a, b):
    return jnp.dot(a, b, preferred_element_type=F32)


def struct(shape, dtype):
    return jax.ShapeDtypeStruct(shape, dtype)


def run(kernel, args, outs, name, scratch=(), flops=0, outside=(), limit=20):
    single = not isinstance(outs, (list, tuple))
    outs = [outs] if single else outs
    vmem = pl.BlockSpec(memory_space=pltpu.VMEM)
    smem = pl.BlockSpec(memory_space=pltpu.SMEM)
    hbm = pl.BlockSpec(memory_space=pltpu.HBM)
    size = sum(a.size * a.dtype.itemsize for a in list(args) + list(outs))
    result = pl.pallas_call(
        kernel,
        in_specs=[
            hbm if i in outside else smem if a.dtype == jnp.int32 else vmem
            for i, a in enumerate(args)
        ],
        out_specs=[vmem] * len(outs),
        out_shape=outs,
        scratch_shapes=list(scratch),
        compiler_params=pltpu.CompilerParams(vmem_limit_bytes=limit * MIB),
        cost_estimate=pl.CostEstimate(flops=flops, bytes_accessed=size, transcendentals=0),
        name=name,
    )(*args)
    return result[0] if single else result


def decode(code, blocks):
    return code > 0, code % blocks, jnp.maximum(code // blocks - 1, 0)


def each_slot(code, blocks, work):
    def step(s, carry):
        used, first, second = decode(code[s], blocks)

        @pl.when(used)
        def _():
            work(s, first, second)

        return carry

    lax.fori_loop(0, code.shape[0], step, 0)


def own_kernel(code, m_ref, w_ref, far_h, out_ref, mt_ref, wmt_ref, h_ref, yt, arrived):
    kernels, points = h_ref.shape[1], h_ref.shape[2]
    blocks = m_ref.shape[0]

    def fetch(s):
        return pltpu.make_async_copy(far_h.at[s], h_ref.at[s], arrived.at[s])

    each_slot(code, blocks, lambda s, first, second: fetch(s).start())
    for k in range(kernels):
        wmt_ref[k] = w_ref[kernels - 1 - k].T
    for a in range(blocks):
        mt = m_ref[a].T
        mt_ref[a] = mt
        for k in range(kernels):
            yt[a, :, k * points : (k + 1) * points] = dot(wmt_ref[k], mt).astype(BF16)

    def work(s, first, second):
        fetch(s).wait()
        out_ref[s] = dot(yt[first], h_ref[s].reshape(kernels * points, points)).astype(BF16)

    each_slot(code, blocks, work)


def second_rows(s, second, per_column, chip_ref, here_ref, far_ref):
    here = lax.axis_index("block")
    column = second // per_column - here
    beside = jnp.where(column == 1 - 2 * (here % 2), chip_ref[s], far_ref[s])
    return jnp.where(column == 0, here_ref[s], beside)


def near_kernel(per_column, code, chip_ref, here_ref, far_ref, w_ref, h_ref, total_ref, near_ref):
    kernels, width = w_ref.shape[0], w_ref.shape[1]
    total_ref[...] = jnp.zeros_like(total_ref)

    def work(s, first, second):
        x = second_rows(s, second, per_column, chip_ref, here_ref, far_ref)
        for k in range(kernels):
            near_ref[s, :, k * width : (k + 1) * width] = dot(h_ref[s, k], x).astype(BF16)
        total_ref[first] += dot(near_ref[s], w_ref[...].reshape(kernels * width, width))

    each_slot(code, total_ref.shape[0], work)


def back_near_kernel(code, ut_ref, w_ref, near_ref, h_ref, out_ref, gd_ref, vt):
    kernels, points, width = h_ref.shape[1], h_ref.shape[2], w_ref.shape[1]
    blocks = ut_ref.shape[0]
    gd_ref[...] = jnp.zeros_like(gd_ref)
    for a in range(blocks):
        u = ut_ref[a]
        for k in range(kernels):
            vt[a, :, k * points : (k + 1) * points] = dot(w_ref[k], u).astype(BF16)

    def work(s, first, second):
        out_ref[s] = dot(vt[first], h_ref[s].reshape(kernels * points, points)).astype(BF16)
        gd_ref[...] += dot(ut_ref[first], near_ref[s])

    each_slot(code, blocks, work)


def back_own_kernel(
    per_column,
    code,
    chip_ref,
    here_ref,
    far_ref,
    mt_ref,
    wmt_ref,
    gd_ref,
    h_ref,
    total_ref,
    keep_ref,
    send_ref,
    z,
    gm,
):
    kernels, width = wmt_ref.shape[0], wmt_ref.shape[1]
    half = width // 2
    total_ref[...] = jnp.zeros_like(total_ref)
    gm[...] = jnp.zeros_like(gm)

    def work(s, first, second):
        x = second_rows(s, second, per_column, chip_ref, here_ref, far_ref)
        for k in range(kernels):
            z[:, k * width : (k + 1) * width] = dot(h_ref[s, k], x).astype(BF16)
        total_ref[first] += dot(z[...], wmt_ref[...].reshape(kernels * width, width))
        gm[...] += dot(mt_ref[first], z[...])

    each_slot(code, total_ref.shape[0], work)
    core = lax.axis_index("block") % 2
    for k in range(kernels):
        at = (kernels - 1 - k) * width
        both = gd_ref[:, k * width : (k + 1) * width].T + gm[:, at : at + width]
        low, high = both[:half], both[half:]
        keep_ref[k] = jnp.where(core == 0, low, high)
        send_ref[k] = jnp.where(core == 0, high, low).astype(BF16)


def pick_kernel(per_column, code_p, code_c, code_f, own, one, two, three, to_p, to_c, to_f):
    blocks = own.shape[0]
    regions = per_column // blocks
    me, column = lax.axis_index("grp"), lax.axis_index("block")
    for code, out in ((code_p, to_p), (code_c, to_c), (code_f, to_f)):
        for s in range(out.shape[0]):
            used, _, block = decode(code[s], blocks)
            here = used & (block // per_column == column)
            away = (block // blocks % regions) ^ me
            for distance, source in enumerate((own, one, two, three)):

                @pl.when(here & (away == distance))
                def _(source=source, out=out, s=s, block=block):
                    out[s] = source[block % blocks]


def merge_kernel(
    per_column, code_p, code_c, code_f, part_p, part_c, part_f, own, one, two, three, total
):
    blocks = own.shape[0]
    regions = per_column // blocks
    me, column = lax.axis_index("grp"), lax.axis_index("block")
    total[...] = jnp.zeros_like(total)
    for code, part in ((code_p, part_p), (code_c, part_c), (code_f, part_f)):
        for s in range(part.shape[0]):
            used, _, block = decode(code[s], blocks)
            away = (block // blocks % regions) ^ me
            at = away * blocks + block % blocks

            @pl.when(used & (block // per_column == column))
            def _(part=part, s=s, at=at):
                total[at] += part[s].astype(F32)

    own[...] = total[0:blocks]
    for distance, out in ((1, one), (2, two), (3, three)):
        out[...] = total[distance * blocks : (distance + 1) * blocks].astype(BF16)


def rows_below(count, shape):
    return lax.broadcasted_iota(jnp.int32, shape, 0) < count


def summed_rows(x, total, own, one, two, three):
    scattered = own[x] + one[x].astype(F32) + two[x].astype(F32) + three[x].astype(F32)
    return total[x] + scattered.T


def activate_kernel(counts, total, own, one, two, three, cot, act, up, upt):
    for x in range(total.shape[0]):
        rows = summed_rows(x, total, own, one, two, three)
        valid = rows_below(counts[x], rows.shape)
        pre = jnp.where(valid, rows, 0.0)
        sig = jax.nn.sigmoid(pre)
        act[x] = (pre * sig).astype(BF16)
        slope = sig * (1.0 + pre * (1.0 - sig))
        upstream = jnp.where(valid, cot[x].astype(F32) * slope, 0.0)
        up[x] = upstream.astype(BF16)
        upt[x] = upstream.T.astype(BF16)


def finish_kernel(counts, total, own, one, two, three, out):
    for x in range(total.shape[0]):
        rows = summed_rows(x, total, own, one, two, three)
        out[x] = jnp.where(rows_below(counts[x], rows.shape), rows, 0.0).astype(BF16)


def quarter_at(index, rows):
    return pl.ds(pl.multiple_of(index * rows, rows), rows)


def halve_kernel(keep, got, kept, sent):
    rows = kept.shape[2]
    me = lax.axis_index("grp")

    def piece(index):
        at = quarter_at(index, rows)
        return keep[:, at] + got[:, at].astype(F32)

    kept[0] = piece(me)
    kept[1] = piece(me ^ 3)
    sent[0] = piece(me ^ 1).astype(BF16)
    sent[1] = piece(me ^ 2).astype(BF16)


def quarter_kernel(pair, got, kept, sent):
    kept[...] = pair[0] + got[0].astype(F32)
    sent[...] = (pair[1] + got[1].astype(F32)).astype(BF16)


def add_kernel(scale, own, got, out):
    out[...] = ((own[...].astype(F32) + got[...].astype(F32)) * scale).astype(out.dtype)


def pair_kernel(own, got, out):
    out[0] = own[...]
    out[1] = got[...]


def join_kernel(own, got, out):
    rows = own.shape[2]
    me = lax.axis_index("grp")
    out[:, quarter_at(me, rows)] = own[0]
    out[:, quarter_at(me ^ 3, rows)] = own[1]
    out[:, quarter_at(me ^ 1, rows)] = got[0]
    out[:, quarter_at(me ^ 2, rows)] = got[1]


def widen_kernel(own, other, out):
    half = own.shape[1]
    core = lax.axis_index("block") % 2
    low, high = own[...], other[...]
    out[:, :half] = jnp.where(core == 0, low, high).astype(F32)
    out[:, half:] = jnp.where(core == 0, high, low).astype(F32)


def after(x, *earlier):
    return lax.optimization_barrier((x, *earlier))[0]


def swap(x, axis, partner):
    peers = range(lax.axis_size(axis))
    return lax.ppermute(x, axis, [(i, partner(i)) for i in peers if partner(i) in peers])


def swap_core(x):
    return swap(x, "block", lambda i: i ^ 1)


def swap_far(x):
    return swap(x, "block", lambda i: i + 1 if i % 2 else i - 1)


def swap_grp(x, bits):
    return swap(x, "grp", lambda i: i ^ bits)


def body(features, point_counts, kernel_weights, influence, pair_list, pair_counts, cotangent):
    blocks, points, width = features.shape
    kernels = kernel_weights.shape[0]
    slots = influence.shape[0]
    regions = lax.axis_size("grp")
    per_column = blocks * regions
    flat = kernels * width
    pair_flops = 2 * slots * kernels * points * points * width
    row = lax.broadcasted_iota(jnp.int32, features.shape, 1)
    masked = jnp.where(row < point_counts[:, None, None], features, jnp.zeros_like(features))
    code = (pair_list[:, 1] + 1) * blocks + pair_list[:, 0]
    code = jnp.where(jnp.arange(slots) < pair_counts[0], code, 0)

    rows_b = struct((slots, points, width), BF16)
    rows_t = struct((slots, width, points), BF16)
    own_b = struct((blocks, points, width), BF16)
    own_t = struct((blocks, width, points), BF16)
    total_b = struct((blocks, points, width), F32)

    def around(values):
        return tuple(swap_grp(values, bits) for bits in (1, 2, 3))

    received = around(masked)
    codes = (swap_core(code), code, swap_far(code))

    def exchange(values, received, part):
        part_p, part_f = swap_core(part), swap_far(part)
        to_p, to_c, to_f = run(
            functools.partial(pick_kernel, per_column),
            (*codes, after(values, part), *received),
            [rows_b] * 3,
            "pick_requested",
        )
        from_p, from_f = swap_core(to_p), swap_far(to_f)
        own, *parts = run(
            functools.partial(merge_kernel, per_column),
            (*codes, part_p, after(part, to_c), part_f),
            [struct((blocks, width, points), F32)] + [own_t] * 3,
            "merge_partials",
            scratch=[pltpu.VMEM((per_column, width, points), F32)],
        )
        scattered = (own, *(swap_grp(parts[bits - 1], bits) for bits in (1, 2, 3)))
        return (from_p, after(to_c, own), from_f), scattered

    to_second, masked_t, mirrored_t, influence = run(
        own_kernel,
        (code, masked, kernel_weights, influence),
        [rows_t, own_t, struct((kernels, width, width), BF16), struct(influence.shape, BF16)],
        "own_to_second",
        [
            pltpu.VMEM((blocks, width, kernels * points), BF16),
            pltpu.SemaphoreType.DMA((slots,)),
        ],
        pair_flops,
        outside=(3,),
        limit=31,
    )
    near_rows, scattered = exchange(masked, received, to_second)
    total, near_store = run(
        functools.partial(near_kernel, per_column),
        (code, *near_rows, kernel_weights, influence),
        [total_b, struct((slots, points, flat), BF16)],
        "near_to_first",
        [],
        2 * pair_flops,
    )
    activated, upstream, upstream_t = run(
        activate_kernel,
        (point_counts, total, *scattered, cotangent),
        [own_b, own_b, own_t],
        "activate",
    )

    received = around(upstream)
    to_second, grad_direct = run(
        back_near_kernel,
        (code, upstream_t, kernel_weights, near_store, influence),
        [rows_t, struct((width, flat), F32)],
        "back_to_second",
        [pltpu.VMEM((blocks, width, kernels * points), BF16)],
        2 * pair_flops,
    )
    near_upstream, scattered = exchange(upstream, received, to_second)
    half = (kernels, width // 2, width)
    total, keep, send = run(
        functools.partial(back_own_kernel, per_column),
        (code, *near_upstream, masked_t, mirrored_t, grad_direct, influence),
        [total_b, struct(half, F32), struct(half, BF16)],
        "back_to_first",
        [pltpu.VMEM((points, flat), BF16), pltpu.VMEM((width, flat), F32)],
        2 * pair_flops,
    )

    piece = (kernels, width // 2 // regions, width)
    pair = (2,) + piece
    got = swap_core(after(send, *scattered))
    kept, sent = run(halve_kernel, (keep, got), [struct(pair, F32), struct(pair, BF16)], "halve")
    kept, sent = run(
        quarter_kernel,
        (kept, swap_grp(sent, 1)),
        [struct(piece, F32), struct(piece, BF16)],
        "quarter",
    )

    def add(own, got, dtype, scale=1.0):
        return run(functools.partial(add_kernel, scale), (own, got), struct(piece, dtype), "add")

    summed = add(kept, swap_grp(sent, 3), BF16)
    everywhere = lax.axis_size("block") * regions * blocks * points
    for stride, bits, dtype, scale in (
        (2, 1, BF16, 1.0),
        (2, 3, F32, 1.0),
        (8, 1, F32, 1.0),
        (8, 3, BF16, 1.0 / math.sqrt(everywhere)),
    ):
        got = swap(summed, "block", lambda i, n=stride * bits: i ^ n)
        summed = add(summed, got, dtype, scale)
    two = run(pair_kernel, (summed, swap_grp(summed, 3)), struct(pair, BF16), "pair_up")
    joined = run(join_kernel, (two, swap_grp(two, 1)), struct(half, BF16), "join_quarters")
    grad_weights = run(
        widen_kernel,
        (joined, swap_core(joined)),
        struct((kernels, width, width), F32),
        "join_halves",
    )
    grad_features = run(
        finish_kernel, (point_counts, total, *scattered), own_b, "finish_features"
    )
    return (activated, grad_features, grad_weights)


def solution(mesh):
    placed = (
        P(("block", "grp"), None, None),
        P(("block", "grp")),
        P(),
        P(("block", "grp"), None, None, None),
        P(("block", "grp"), None),
        P(("block", "grp")),
        P(("block", "grp"), None, None),
    )
    return jax.shard_map(
        body,
        mesh=mesh,
        in_specs=placed,
        out_specs=(P(("block", "grp"), None, None), P(("block", "grp"), None, None), P()),
        check_vma=False,
    )
```

time: 715 us -> 139 us (0.19)
  waiting for transfers between devices: 412 us -> 30.1 us
  matrix products: 88.1 us -> 0 us
  loops' own time: 42.4 us -> 0 us
  Pallas kernels: 0 us -> 41.7 us
  local copies, waits for them, and re-layouts: 40.5 us -> 1.04 us
  other arithmetic: 37.4 us -> 1.87 us
  starting transfers between devices: 76.6 us -> 62.1 us
  between operations: 14 us -> 1.62 us
    psum x1 -> x0, waiting for transfers between devices: 190 us -> none  [body(): total_weights = lax.psum(local_weights, ('block', 'grp'))]
    reduce_scatter x2 -> x0, waiting for transfers between devices: 112 us -> none  [collect(): lax.psum_scatter(partial_value[1] + from_lower + from_upper, 'grp', scatt...]
    dot_general x40 -> x0, matrix products: 88.1 us -> none  [the longest x4 14.4 us: backward_pair(): jnp.einsum('kij,ikc->jc', tile, back_near, preferred_element_type=jnp.flo...]
    all_gather x2 -> x0, waiting for transfers between devices: 49.6 us -> none  [neighbours(): region = lax.all_gather(values, 'grp', axis=0, tiled=True)]
    another operation x2 -> x0, loops' own time: 42.4 us -> none  [the longest x1 21.7 us: body(): lax.fori_loop(0, used, forward_pair, (own_zero, sent_zero, store_zero, st...]
    pallas_call x0 -> x20, Pallas kernels: none -> 41.7 us  [run(): pl.pallas_call(kernel, in_specs=[hbm if i in outside else smem if a.dtype...]
    ppermute x8 -> x32, waiting for transfers between devices: 60 us -> 30.1 us  [swap(): lax.ppermute(x, axis, [(i, partner(i)) for i in peers if partner(i) in pe...]
    broadcast_in_dim x6 -> x0, local copies, waits for them, and re-layouts: 16.1 us -> none  [the longest x2 7.22 us: body(): store_zero = jnp.zeros((slot_count, points, kernels * width), jnp.bfloat16)]
  transfers between devices with their start and end apart: 13 -> 32, of which waited for: 13 -> 13; matrix products, arithmetic and copies ran while one was open for 1% -> 1% of each run, Pallas kernels for 0% -> 28%
where the time goes in v2:
time: 139 us; the launch traced here: 138 us
  starting transfers between devices  62.1 us (45%)
  Pallas kernels  41.7 us (30%)
  waiting for transfers between devices  30.1 us (22%)
  other arithmetic  1.87 us (1%)
  between operations  1.62 us (1%)
    ppermute x32, starting transfers between devices, swap(): lax.ppermute(x, axis, [(i, partner(i)) for i in peers if partner(i) in pe...  62.1 us
    pallas_call x20, Pallas kernels, run(): pl.pallas_call(kernel, in_specs=[hbm if i in outside else smem if a.dtype...  41.7 us
    ppermute x32, waiting for transfers between devices, swap(): lax.ppermute(x, axis, [(i, partner(i)) for i in peers if partner(i) in pe...  30.1 us
  transfers between devices with their start and end apart: 32, of which 13 were waited for; matrix products, arithmetic and copies ran while one was open for 1% of the time, Pallas kernels for 28%

profile of v2, /device:TPU:1, one launch (start us, length us, event | category | flops | bytes accessed | tf_op | source)
XLA Modules:
  0.0 138.4 jit_solution(4511981455860682749)
XLA Ops:
  1.7 3.6 %collective-permute-start.4 = (bf16[4,256,128]{2,1,0:T(8,128)(2,1)S(1)}, bf16[4,256,128]{2,1,0:T(8,128)(2,1)S(1)}, u32[]{:S(2)}, u32[]{:S(2)}) collective-permute-start(bf16[4,256,128]{2,1,0:T(8,128)(2,1)S(1)} %fusion.m_ref.own), channel_id=1, source_target_pairs={{0,3},{1,2},{2,1},{3,0},{4,7},{5,6},{6,5},{7,4},{8,11},{9,10},{10,... | collective-permute-start | bytes 786440 | tf_op jit(solution)/shard_map/ppermute | solution.py:282
  7.5 4.4 %collective-permute-start.1 = (s32[8]{0:T(128)S(1)}, s32[8]{0:T(128)S(1)}, u32[]{:S(2)}, u32[]{:S(2)}) collective-permute-start(s32[8]{0:T(128)S(1)} %compare_select_fusion.code.code_c), channel_id=1, source_target_pairs={{4,8},{8,4},{12,16},{16,12},{20,24},{24,20},{28,32},{32,28},{36,40... | collective-permute-start | bytes 104 | tf_op jit(solution)/shard_map/ppermute | solution.py:282
  13.0 6.6 %own_to_second.1 = (bf16[8,128,256]{2,1,0:T(8,128)(2,1)S(1)}, bf16[4,128,256]{2,1,0:T(8,128)(2,1)S(1)}, bf16[15,128,128]{2,1,0:T(8,128)(2,1)S(1)}, bf16[8,15,256,256]{3,2,1,0:T(8,128)(2,1)S(1)}) custom-call(s32[8]{0:T(128)S(1)} %compare_select_fusion.code.code_c, bf16[4,256,128]{2,1,0:T(8,128)(2,1)S(1)} %fusion.m_ref.own, bf16[15,128,128]{2,1,0:T(8,128)(2,1)S(1)} %copy-done, ...), custom_call_target="tpu_custom_call" | custom-call | flops 2013265920 | bytes 33488928 | tf_op jit(solution)/shard_map/own_to_second/pallas_call | solution.py:31
  23.8 3.6 %collective-permute-start.8 = (bf16[8,256,128]{2,1,0:T(8,128)(2,1)S(1)}, bf16[8,256,128]{2,1,0:T(8,128)(2,1)S(1)}, u32[]{:S(2)}, u32[]{:S(2)}) collective-permute-start(bf16[8,256,128]{2,1,0:T(8,128)(2,1)S(1)} %get-tuple-element.49), channel_id=1, source_target_pairs={{4,8},{8,4},{12,16},{16,12},{20,24},{24,20},{28,32},{32,28},{36,40... | collective-permute-start | bytes 1572872 | tf_op jit(solution)/shard_map/ppermute | solution.py:282
  27.5 2.9 %collective-permute-done.7.part_f = bf16[8,128,256]{2,1,0:T(8,128)(2,1)S(1)} collective-permute-done((bf16[8,128,256]{2,1,0:T(8,128)(2,1)S(1)}, bf16[8,128,256]{2,1,0:T(8,128)(2,1)S(1)}, u32[]{:S(2)}, u32[]{:S(2)}) %collective-permute-start.7) | collective-permute-done | bytes 524320 | tf_op jit(solution)/shard_map/ppermute | solution.py:282
  31.8 3.9 %collective-permute-start.10 = (bf16[4,128,256]{2,1,0:T(8,128)(2,1)S(1)}, bf16[4,128,256]{2,1,0:T(8,128)(2,1)S(1)}, u32[]{:S(2)}, u32[]{:S(2)}) collective-permute-start(bf16[4,128,256]{2,1,0:T(8,128)(2,1)S(1)} %get-tuple-element.53), channel_id=1, source_target_pairs={{0,2},{1,3},{2,0},{3,1},{4,6},{5,7},{6,4},{7,5},{8,10},{9,11},{10,... | collective-permute-start | bytes 786440 | tf_op jit(solution)/shard_map/ppermute | solution.py:282
  36.0 8.2 %near_to_first.1 = (f32[4,256,128]{2,1,0:T(8,128)S(1)}, bf16[8,256,1920]{2,1,0:T(8,128)(2,1)S(1)}) custom-call(s32[8]{0:T(128)S(1)} %compare_select_fusion.code.code_c, bf16[8,256,128]{2,1,0:T(8,128)(2,1)S(1)} %collective-permute-done.5.chip_ref, bf16[8,256,128]{2,1,0:T(8,128)(2,1)S(1)} %get-tuple-element.48.here_ref, ...), custom_call_target="tpu_custom_call" | custom-call | flops 4026531840 | bytes 26181664 | tf_op jit(solution)/shard_map/near_to_first/pallas_call | solution.py:31
  50.4 6.6 %back_to_second.1 = (bf16[8,128,256]{2,1,0:T(8,128)(2,1)S(1)}, f32[128,1920]{1,0:T(8,128)S(1)}) custom-call(s32[8]{0:T(128)S(1)} %compare_select_fusion.code.code_c, bf16[4,128,256]{2,1,0:T(8,128)(2,1)S(1)} %get-tuple-element.57.ut_ref, bf16[15,128,128]{2,1,0:T(8,128)(2,1)S(1)} %copy-done, bf16[8,256,1920]{2,1,0:T(8,128)(2,1)S(1)} %get-tuple-element.58.near_ref, ...), custom_call_target="tpu_custom_call" | custom-call | flops 4026531840 | bytes 25853984 | tf_op jit(solution)/shard_map/back_to_second/pallas_call | solution.py:31
  56.9 5.4 %collective-permute-start.17 = (bf16[8,128,256]{2,1,0:T(8,128)(2,1)S(1)}, bf16[8,128,256]{2,1,0:T(8,128)(2,1)S(1)}, u32[]{:S(2)}, u32[]{:S(2)}) collective-permute-start(bf16[8,128,256]{2,1,0:T(8,128)(2,1)S(1)} %get-tuple-element.63.part_c), channel_id=1, source_target_pairs={{4,8},{8,4},{12,16},{16,12},{20,24},{24,20},{28,32},{32,28},{36,40... | collective-permute-start | bytes 1572872 | tf_op jit(solution)/shard_map/ppermute | solution.py:282
  64.8 5.2 %collective-permute-start.18 = (bf16[8,256,128]{2,1,0:T(8,128)(2,1)S(1)}, bf16[8,256,128]{2,1,0:T(8,128)(2,1)S(1)}, u32[]{:S(2)}, u32[]{:S(2)}) collective-permute-start(bf16[8,256,128]{2,1,0:T(8,128)(2,1)S(1)} %get-tuple-element.66), channel_id=1, source_target_pairs={{4,8},{8,4},{12,16},{16,12},{20,24},{24,20},{28,32},{32,28},{36,40... | collective-permute-start | bytes 1572872 | tf_op jit(solution)/shard_map/ppermute | solution.py:282
  73.2 2.1 %collective-permute-start.21 = (bf16[4,128,256]{2,1,0:T(8,128)(2,1)S(1)}, bf16[4,128,256]{2,1,0:T(8,128)(2,1)S(1)}, u32[]{:S(2)}, u32[]{:S(2)}) collective-permute-start(bf16[4,128,256]{2,1,0:T(8,128)(2,1)S(1)} %get-tuple-element.73), channel_id=1, source_target_pairs={{0,3},{1,2},{2,1},{3,0},{4,7},{5,6},{6,5},{7,4},{8,11},{9,10},{10,... | collective-permute-start | bytes 786440 | tf_op jit(solution)/shard_map/ppermute | solution.py:282
  77.2 9.8 %back_to_first.1 = (f32[4,256,128]{2,1,0:T(8,128)S(1)}, f32[15,64,128]{2,1,0:T(8,128)S(1)}, bf16[15,64,128]{2,1,0:T(8,128)(2,1)S(1)}) custom-call(s32[8]{0:T(128)S(1)} %compare_select_fusion.code.code_c, bf16[8,256,128]{2,1,0:T(8,128)(2,1)S(1)} %collective-permute-done.15.chip_ref, bf16[8,256,128]{2,1,0:T(8,128)(2,1)S(1)} %get-tuple-element.65.here_ref, ...), custom_call_target="tpu_custom_call" | custom-call | flops 4026531840 | bytes 20299808 | tf_op jit(solution)/shard_map/back_to_first/pallas_call | solution.py:31
  88.8 4.8 %collective-permute-done.23.got = bf16[2,15,16,128]{3,2,1,0:T(8,128)(2,1)S(1)} collective-permute-done((bf16[2,15,16,128]{3,2,1,0:T(8,128)(2,1)S(1)}, bf16[2,15,16,128]{3,2,1,0:T(8,128)(2,1)S(1)}, u32[]{:S(2)}, u32[]{:S(2)}) %collective-permute-start.23) | collective-permute-done | bytes 122912 | tf_op jit(solution)/shard_map/ppermute | solution.py:282
  94.2 3.8 %collective-permute-done.24.got = bf16[15,16,128]{2,1,0:T(8,128)(2,1)S(1)} collective-permute-done((bf16[15,16,128]{2,1,0:T(8,128)(2,1)S(1)}, bf16[15,16,128]{2,1,0:T(8,128)(2,1)S(1)}, u32[]{:S(2)}, u32[]{:S(2)}) %collective-permute-start.24) | collective-permute-done | bytes 61472 | tf_op jit(solution)/shard_map/ppermute | solution.py:282
  98.0 2.7 %collective-permute-start.25 = (bf16[15,16,128]{2,1,0:T(8,128)(2,1)S(1)}, bf16[15,16,128]{2,1,0:T(8,128)(2,1)S(1)}, u32[]{:S(2)}, u32[]{:S(2)}) collective-permute-start(bf16[15,16,128]{2,1,0:T(8,128)(2,1)S(1)} %add.20.own), channel_id=1, source_target_pairs={{0,8},{4,12},{8,0},{12,4},{16,24},{20,28},{24,16},{28,20},{32,40},... | collective-permute-start | bytes 184328 | tf_op jit(solution)/shard_map/ppermute | solution.py:282
  102.3 5.6 %collective-permute-start.26 = (bf16[15,16,128]{2,1,0:T(8,128)(2,1)S(1)}, bf16[15,16,128]{2,1,0:T(8,128)(2,1)S(1)}, u32[]{:S(2)}, u32[]{:S(2)}) collective-permute-start(bf16[15,16,128]{2,1,0:T(8,128)(2,1)S(1)} %add.21.own), channel_id=1, source_target_pairs={{0,24},{4,28},{8,16},{12,20},{16,8},{20,12},{24,0},{28,4},{32,56},... | collective-permute-start | bytes 184328 | tf_op jit(solution)/shard_map/ppermute | solution.py:282
  109.6 2.1 %collective-permute-start.27 = (f32[15,16,128]{2,1,0:T(8,128)S(1)}, f32[15,16,128]{2,1,0:T(8,128)S(1)}, u32[]{:S(2)}, u32[]{:S(2)}) collective-permute-start(f32[15,16,128]{2,1,0:T(8,128)S(1)} %add.22.own), channel_id=1, source_target_pairs={{0,32},{4,36},{8,40},{12,44},{16,48},{20,52},{24,56},{28,60},{32,0... | collective-permute-start | bytes 368648 | tf_op jit(solution)/shard_map/ppermute | solution.py:282
  111.7 2.3 %collective-permute-done.27.got = f32[15,16,128]{2,1,0:T(8,128)S(1)} collective-permute-done((f32[15,16,128]{2,1,0:T(8,128)S(1)}, f32[15,16,128]{2,1,0:T(8,128)S(1)}, u32[]{:S(2)}, u32[]{:S(2)}) %collective-permute-start.27) | collective-permute-done | bytes 122912 | tf_op jit(solution)/shard_map/ppermute | solution.py:282
  114.0 2.6 %collective-permute-start.28 = (f32[15,16,128]{2,1,0:T(8,128)S(1)}, f32[15,16,128]{2,1,0:T(8,128)S(1)}, u32[]{:S(2)}, u32[]{:S(2)}) collective-permute-start(f32[15,16,128]{2,1,0:T(8,128)S(1)} %add.23.own), channel_id=1, source_target_pairs={{0,96},{4,100},{8,104},{12,108},{16,112},{20,116},{24,120},{28,124... | collective-permute-start | bytes 368648 | tf_op jit(solution)/shard_map/ppermute | solution.py:282
  116.6 2.4 %collective-permute-done.28.got = f32[15,16,128]{2,1,0:T(8,128)S(1)} collective-permute-done((f32[15,16,128]{2,1,0:T(8,128)S(1)}, f32[15,16,128]{2,1,0:T(8,128)S(1)}, u32[]{:S(2)}, u32[]{:S(2)}) %collective-permute-start.28) | collective-permute-done | bytes 122912 | tf_op jit(solution)/shard_map/ppermute | solution.py:282
  119.0 2.4 %collective-permute-start.29 = (bf16[15,16,128]{2,1,0:T(8,128)(2,1)S(1)}, bf16[15,16,128]{2,1,0:T(8,128)(2,1)S(1)}, u32[]{:S(2)}, u32[]{:S(2)}) collective-permute-start(bf16[15,16,128]{2,1,0:T(8,128)(2,1)S(1)} %add.24.own), channel_id=1, source_target_pairs={{0,3},{1,2},{2,1},{3,0},{4,7},{5,6},{6,5},{7,4},{8,11},{9,10},{10,... | collective-permute-start | bytes 184328 | tf_op jit(solution)/shard_map/ppermute | solution.py:282
  121.4 2.2 %collective-permute-done.29.got = bf16[15,16,128]{2,1,0:T(8,128)(2,1)S(1)} collective-permute-done((bf16[15,16,128]{2,1,0:T(8,128)(2,1)S(1)}, bf16[15,16,128]{2,1,0:T(8,128)(2,1)S(1)}, u32[]{:S(2)}, u32[]{:S(2)}) %collective-permute-start.29) | collective-permute-done | bytes 61472 | tf_op jit(solution)/shard_map/ppermute | solution.py:282
  123.8 3.7 %collective-permute-done.30.got = bf16[2,15,16,128]{3,2,1,0:T(8,128)(2,1)S(1)} collective-permute-done((bf16[2,15,16,128]{3,2,1,0:T(8,128)(2,1)S(1)}, bf16[2,15,16,128]{3,2,1,0:T(8,128)(2,1)S(1)}, u32[]{:S(2)}, u32[]{:S(2)}) %collective-permute-start.30) | collective-permute-done | bytes 122912 | tf_op jit(solution)/shard_map/ppermute | solution.py:282
  127.5 8.3 %collective-permute-start.31 = (bf16[15,64,128]{2,1,0:T(8,128)(2,1)S(1)}, bf16[15,64,128]{2,1,0:T(8,128)(2,1)S(1)}, u32[]{:S(2)}, u32[]{:S(2)}) collective-permute-start(bf16[15,64,128]{2,1,0:T(8,128)(2,1)S(1)} %join_quarters.1.own), channel_id=1, source_target_pairs={{0,4},{4,0},{8,12},{12,8},{16,20},{20,16},{24,28},{28,24},{32,36},... | collective-permute-start | bytes 737288 | tf_op jit(solution)/shard_map/ppermute | solution.py:282
  (68 shorter events, 31.4 us)
Async XLA Ops:
  1.7 19.9 %collective-permute-start.4 = (bf16[4,256,128]{2,1,0:T(8,128)(2,1)S(1)}, bf16[4,256,128]{2,1,0:T(8,128)(2,1)S(1)}, u32[]{:S(2)}, u32[]{:S(2)}) collective-permute-start(bf16[4,256,128]{2,1,0:T(8,128)(2,1)S(1)} %fusion.m_ref.own), channel_id=1, source_target_pairs={{0,3},{1,2},{2,1},{3,0},{4,7},{5,6},{6,5},{7,4},{8,11},{9,10},{10,... | collective-permute-start | bytes 786440 | tf_op jit(solution)/shard_map/ppermute | solution.py:282
  5.4 16.3 %collective-permute-start.3 = (bf16[4,256,128]{2,1,0:T(8,128)(2,1)S(1)}, bf16[4,256,128]{2,1,0:T(8,128)(2,1)S(1)}, u32[]{:S(2)}, u32[]{:S(2)}) collective-permute-start(bf16[4,256,128]{2,1,0:T(8,128)(2,1)S(1)} %fusion.m_ref.own), channel_id=1, source_target_pairs={{0,2},{1,3},{2,0},{3,1},{4,6},{5,7},{6,4},{7,5},{8,10},{9,11},{10,... | collective-permute-start | bytes 786440 | tf_op jit(solution)/shard_map/ppermute | solution.py:282
  5.7 15.9 %collective-permute-start.2 = (bf16[4,256,128]{2,1,0:T(8,128)(2,1)S(1)}, bf16[4,256,128]{2,1,0:T(8,128)(2,1)S(1)}, u32[]{:S(2)}, u32[]{:S(2)}) collective-permute-start(bf16[4,256,128]{2,1,0:T(8,128)(2,1)S(1)} %fusion.m_ref.own), channel_id=1, source_target_pairs={{0,1},{1,0},{2,3},{3,2},{4,5},{5,4},{6,7},{7,6},{8,9},{9,8},{10,11... | collective-permute-start | bytes 786440 | tf_op jit(solution)/shard_map/ppermute | solution.py:282
  7.5 12.1 %collective-permute-start.1 = (s32[8]{0:T(128)S(1)}, s32[8]{0:T(128)S(1)}, u32[]{:S(2)}, u32[]{:S(2)}) collective-permute-start(s32[8]{0:T(128)S(1)} %compare_select_fusion.code.code_c), channel_id=1, source_target_pairs={{4,8},{8,4},{12,16},{16,12},{20,24},{24,20},{28,32},{32,28},{36,40... | collective-permute-start | bytes 104 | tf_op jit(solution)/shard_map/ppermute | solution.py:282
  11.8 9.7 %collective-permute-start = (s32[8]{0:T(128)S(1)}, s32[8]{0:T(128)S(1)}, u32[]{:S(2)}, u32[]{:S(2)}) collective-permute-start(s32[8]{0:T(128)S(1)} %compare_select_fusion.code.code_c), channel_id=1, source_target_pairs={{0,4},{4,0},{8,12},{12,8},{16,20},{20,16},{24,28},{28,24},{32,36},... | collective-permute-start | bytes 104 | tf_op jit(solution)/shard_map/ppermute | solution.py:282
  19.6 10.8 %collective-permute-start.7 = (bf16[8,128,256]{2,1,0:T(8,128)(2,1)S(1)}, bf16[8,128,256]{2,1,0:T(8,128)(2,1)S(1)}, u32[]{:S(2)}, u32[]{:S(2)}) collective-permute-start(bf16[8,128,256]{2,1,0:T(8,128)(2,1)S(1)} %get-tuple-element.46.part_c), channel_id=1, source_target_pairs={{4,8},{8,4},{12,16},{16,12},{20,24},{24,20},{28,32},{32,28},{36,40... | collective-permute-start | bytes 1572872 | tf_op jit(solution)/shard_map/ppermute | solution.py:282
  21.5 8.9 %collective-permute-start.6 = (bf16[8,128,256]{2,1,0:T(8,128)(2,1)S(1)}, bf16[8,128,256]{2,1,0:T(8,128)(2,1)S(1)}, u32[]{:S(2)}, u32[]{:S(2)}) collective-permute-start(bf16[8,128,256]{2,1,0:T(8,128)(2,1)S(1)} %get-tuple-element.46.part_c), channel_id=1, source_target_pairs={{0,4},{4,0},{8,12},{12,8},{16,20},{20,16},{24,28},{28,24},{32,36},... | collective-permute-start | bytes 1572872 | tf_op jit(solution)/shard_map/ppermute | solution.py:282
  23.3 12.5 %collective-permute-start.5 = (bf16[8,256,128]{2,1,0:T(8,128)(2,1)S(1)}, bf16[8,256,128]{2,1,0:T(8,128)(2,1)S(1)}, u32[]{:S(2)}, u32[]{:S(2)}) collective-permute-start(bf16[8,256,128]{2,1,0:T(8,128)(2,1)S(1)} %get-tuple-element.44), channel_id=1, source_target_pairs={{0,4},{4,0},{8,12},{12,8},{16,20},{20,16},{24,28},{28,24},{32,36},... | collective-permute-start | bytes 1572872 | tf_op jit(solution)/shard_map/ppermute | solution.py:282
  23.8 12.2 %collective-permute-start.8 = (bf16[8,256,128]{2,1,0:T(8,128)(2,1)S(1)}, bf16[8,256,128]{2,1,0:T(8,128)(2,1)S(1)}, u32[]{:S(2)}, u32[]{:S(2)}) collective-permute-start(bf16[8,256,128]{2,1,0:T(8,128)(2,1)S(1)} %get-tuple-element.49), channel_id=1, source_target_pairs={{4,8},{8,4},{12,16},{16,12},{20,24},{24,20},{28,32},{32,28},{36,40... | collective-permute-start | bytes 1572872 | tf_op jit(solution)/shard_map/ppermute | solution.py:282
  31.7 12.5 %collective-permute-start.9 = (bf16[4,128,256]{2,1,0:T(8,128)(2,1)S(1)}, bf16[4,128,256]{2,1,0:T(8,128)(2,1)S(1)}, u32[]{:S(2)}, u32[]{:S(2)}) collective-permute-start(bf16[4,128,256]{2,1,0:T(8,128)(2,1)S(1)} %get-tuple-element.52), channel_id=1, source_target_pairs={{0,1},{1,0},{2,3},{3,2},{4,5},{5,4},{6,7},{7,6},{8,9},{9,8},{10,11... | collective-permute-start | bytes 786440 | tf_op jit(solution)/shard_map/ppermute | solution.py:282
  31.8 12.4 %collective-permute-start.10 = (bf16[4,128,256]{2,1,0:T(8,128)(2,1)S(1)}, bf16[4,128,256]{2,1,0:T(8,128)(2,1)S(1)}, u32[]{:S(2)}, u32[]{:S(2)}) collective-permute-start(bf16[4,128,256]{2,1,0:T(8,128)(2,1)S(1)} %get-tuple-element.53), channel_id=1, source_target_pairs={{0,2},{1,3},{2,0},{3,1},{4,6},{5,7},{6,4},{7,5},{8,10},{9,11},{10,... | collective-permute-start | bytes 786440 | tf_op jit(solution)/shard_map/ppermute | solution.py:282
  35.8 9.6 %collective-permute-start.11 = (bf16[4,128,256]{2,1,0:T(8,128)(2,1)S(1)}, bf16[4,128,256]{2,1,0:T(8,128)(2,1)S(1)}, u32[]{:S(2)}, u32[]{:S(2)}) collective-permute-start(bf16[4,128,256]{2,1,0:T(8,128)(2,1)S(1)} %get-tuple-element.54), channel_id=1, source_target_pairs={{0,3},{1,2},{2,1},{3,0},{4,7},{5,6},{6,5},{7,4},{8,11},{9,10},{10,... | collective-permute-start | bytes 786440 | tf_op jit(solution)/shard_map/ppermute | solution.py:282
  47.1 15.3 %collective-permute-start.14 = (bf16[4,256,128]{2,1,0:T(8,128)(2,1)S(1)}, bf16[4,256,128]{2,1,0:T(8,128)(2,1)S(1)}, u32[]{:S(2)}, u32[]{:S(2)}) collective-permute-start(bf16[4,256,128]{2,1,0:T(8,128)(2,1)S(1)} %get-tuple-element.60.own), channel_id=1, source_target_pairs={{0,3},{1,2},{2,1},{3,0},{4,7},{5,6},{6,5},{7,4},{8,11},{9,10},{10,... | collective-permute-start | bytes 786440 | tf_op jit(solution)/shard_map/ppermute | solution.py:282
  48.8 13.7 %collective-permute-start.13 = (bf16[4,256,128]{2,1,0:T(8,128)(2,1)S(1)}, bf16[4,256,128]{2,1,0:T(8,128)(2,1)S(1)}, u32[]{:S(2)}, u32[]{:S(2)}) collective-permute-start(bf16[4,256,128]{2,1,0:T(8,128)(2,1)S(1)} %get-tuple-element.60.own), channel_id=1, source_target_pairs={{0,2},{1,3},{2,0},{3,1},{4,6},{5,7},{6,4},{7,5},{8,10},{9,11},{10,... | collective-permute-start | bytes 786440 | tf_op jit(solution)/shard_map/ppermute | solution.py:282
  48.8 13.7 %collective-permute-start.12 = (bf16[4,256,128]{2,1,0:T(8,128)(2,1)S(1)}, bf16[4,256,128]{2,1,0:T(8,128)(2,1)S(1)}, u32[]{:S(2)}, u32[]{:S(2)}) collective-permute-start(bf16[4,256,128]{2,1,0:T(8,128)(2,1)S(1)} %get-tuple-element.60.own), channel_id=1, source_target_pairs={{0,1},{1,0},{2,3},{3,2},{4,5},{5,4},{6,7},{7,6},{8,9},{9,8},{10,11... | collective-permute-start | bytes 786440 | tf_op jit(solution)/shard_map/ppermute | solution.py:282
  56.9 13.1 %collective-permute-start.17 = (bf16[8,128,256]{2,1,0:T(8,128)(2,1)S(1)}, bf16[8,128,256]{2,1,0:T(8,128)(2,1)S(1)}, u32[]{:S(2)}, u32[]{:S(2)}) collective-permute-start(bf16[8,128,256]{2,1,0:T(8,128)(2,1)S(1)} %get-tuple-element.63.part_c), channel_id=1, source_target_pairs={{4,8},{8,4},{12,16},{16,12},{20,24},{24,20},{28,32},{32,28},{36,40... | collective-permute-start | bytes 1572872 | tf_op jit(solution)/shard_map/ppermute | solution.py:282
  62.3 7.7 %collective-permute-start.16 = (bf16[8,128,256]{2,1,0:T(8,128)(2,1)S(1)}, bf16[8,128,256]{2,1,0:T(8,128)(2,1)S(1)}, u32[]{:S(2)}, u32[]{:S(2)}) collective-permute-start(bf16[8,128,256]{2,1,0:T(8,128)(2,1)S(1)} %get-tuple-element.63.part_c), channel_id=1, source_target_pairs={{0,4},{4,0},{8,12},{12,8},{16,20},{20,16},{24,28},{28,24},{32,36},... | collective-permute-start | bytes 1572872 | tf_op jit(solution)/shard_map/ppermute | solution.py:282
  64.3 11.1 %collective-permute-start.15 = (bf16[8,256,128]{2,1,0:T(8,128)(2,1)S(1)}, bf16[8,256,128]{2,1,0:T(8,128)(2,1)S(1)}, u32[]{:S(2)}, u32[]{:S(2)}) collective-permute-start(bf16[8,256,128]{2,1,0:T(8,128)(2,1)S(1)} %get-tuple-element.61), channel_id=1, source_target_pairs={{0,4},{4,0},{8,12},{12,8},{16,20},{20,16},{24,28},{28,24},{32,36},... | collective-permute-start | bytes 1572872 | tf_op jit(solution)/shard_map/ppermute | solution.py:282
  64.8 12.4 %collective-permute-start.18 = (bf16[8,256,128]{2,1,0:T(8,128)(2,1)S(1)}, bf16[8,256,128]{2,1,0:T(8,128)(2,1)S(1)}, u32[]{:S(2)}, u32[]{:S(2)}) collective-permute-start(bf16[8,256,128]{2,1,0:T(8,128)(2,1)S(1)} %get-tuple-element.66), channel_id=1, source_target_pairs={{4,8},{8,4},{12,16},{16,12},{20,24},{24,20},{28,32},{32,28},{36,40... | collective-permute-start | bytes 1572872 | tf_op jit(solution)/shard_map/ppermute | solution.py:282
  71.4 15.6 %collective-permute-start.19 = (bf16[4,128,256]{2,1,0:T(8,128)(2,1)S(1)}, bf16[4,128,256]{2,1,0:T(8,128)(2,1)S(1)}, u32[]{:S(2)}, u32[]{:S(2)}) collective-permute-start(bf16[4,128,256]{2,1,0:T(8,128)(2,1)S(1)} %get-tuple-element.71), channel_id=1, source_target_pairs={{0,1},{1,0},{2,3},{3,2},{4,5},{5,4},{6,7},{7,6},{8,9},{9,8},{10,11... | collective-permute-start | bytes 786440 | tf_op jit(solution)/shard_map/ppermute | solution.py:282
  72.1 14.9 %collective-permute-start.20 = (bf16[4,128,256]{2,1,0:T(8,128)(2,1)S(1)}, bf16[4,128,256]{2,1,0:T(8,128)(2,1)S(1)}, u32[]{:S(2)}, u32[]{:S(2)}) collective-permute-start(bf16[4,128,256]{2,1,0:T(8,128)(2,1)S(1)} %get-tuple-element.72), channel_id=1, source_target_pairs={{0,2},{1,3},{2,0},{3,1},{4,6},{5,7},{6,4},{7,5},{8,10},{9,11},{10,... | collective-permute-start | bytes 786440 | tf_op jit(solution)/shard_map/ppermute | solution.py:282
  73.2 13.8 %collective-permute-start.21 = (bf16[4,128,256]{2,1,0:T(8,128)(2,1)S(1)}, bf16[4,128,256]{2,1,0:T(8,128)(2,1)S(1)}, u32[]{:S(2)}, u32[]{:S(2)}) collective-permute-start(bf16[4,128,256]{2,1,0:T(8,128)(2,1)S(1)} %get-tuple-element.73), channel_id=1, source_target_pairs={{0,3},{1,2},{2,1},{3,0},{4,7},{5,6},{6,5},{7,4},{8,11},{9,10},{10,... | collective-permute-start | bytes 786440 | tf_op jit(solution)/shard_map/ppermute | solution.py:282
  102.3 7.2 %collective-permute-start.26 = (bf16[15,16,128]{2,1,0:T(8,128)(2,1)S(1)}, bf16[15,16,128]{2,1,0:T(8,128)(2,1)S(1)}, u32[]{:S(2)}, u32[]{:S(2)}) collective-permute-start(bf16[15,16,128]{2,1,0:T(8,128)(2,1)S(1)} %add.21.own), channel_id=1, source_target_pairs={{0,24},{4,28},{8,16},{12,20},{16,8},{20,12},{24,0},{28,4},{32,56},... | collective-permute-start | bytes 184328 | tf_op jit(solution)/shard_map/ppermute | solution.py:282
  127.5 9.8 %collective-permute-start.31 = (bf16[15,64,128]{2,1,0:T(8,128)(2,1)S(1)}, bf16[15,64,128]{2,1,0:T(8,128)(2,1)S(1)}, u32[]{:S(2)}, u32[]{:S(2)}) collective-permute-start(bf16[15,64,128]{2,1,0:T(8,128)(2,1)S(1)} %join_quarters.1.own), channel_id=1, source_target_pairs={{0,4},{4,0},{8,12},{12,8},{16,20},{20,16},{24,28},{28,24},{32,36},... | collective-permute-start | bytes 737288 | tf_op jit(solution)/shard_map/ppermute | solution.py:282
  (11 other events, 105.2 us)

commit v3 on v2

--- a/solution.py
+++ b/solution.py
@@ -121,34 +121,19 @@
 
 
 def back_own_kernel(
-    per_column,
-    code,
-    chip_ref,
-    here_ref,
-    far_ref,
-    mt_ref,
-    wmt_ref,
-    gd_ref,
-    h_ref,
-    total_ref,
-    keep_ref,
-    send_ref,
-    z,
-    gm,
+    per_column, code, chip_ref, here_ref, far_ref, mt_ref, gd_ref, h_ref, z_ref, keep_ref, send_ref, gm
 ):
-    kernels, width = wmt_ref.shape[0], wmt_ref.shape[1]
+    kernels, width = h_ref.shape[1], here_ref.shape[2]
     half = width // 2
-    total_ref[...] = jnp.zeros_like(total_ref)
     gm[...] = jnp.zeros_like(gm)
 
     def work(s, first, second):
         x = second_rows(s, second, per_column, chip_ref, here_ref, far_ref)
         for k in range(kernels):
-            z[:, k * width : (k + 1) * width] = dot(h_ref[s, k], x).astype(BF16)
-        total_ref[first] += dot(z[...], wmt_ref[...].reshape(kernels * width, width))
-        gm[...] += dot(mt_ref[first], z[...])
-
-    each_slot(code, total_ref.shape[0], work)
+            z_ref[s, :, k * width : (k + 1) * width] = dot(h_ref[s, k], x).astype(BF16)
+        gm[...] += dot(mt_ref[first], z_ref[s])
+
+    each_slot(code, mt_ref.shape[0], work)
     core = lax.axis_index("block") % 2
     for k in range(kernels):
         at = (kernels - 1 - k) * width
@@ -158,6 +143,16 @@
         send_ref[k] = jnp.where(core == 0, high, low).astype(BF16)
 
 
+def to_first_kernel(code, z_ref, wmt_ref, total_ref):
+    kernels, width = wmt_ref.shape[0], wmt_ref.shape[1]
+    total_ref[...] = jnp.zeros_like(total_ref)
+
+    def work(s, first, second):
+        total_ref[first] += dot(z_ref[s], wmt_ref[...].reshape(kernels * width, width))
+
+    each_slot(code, total_ref.shape[0], work)
+
+
 def pick_kernel(per_column, code_p, code_c, code_f, own, one, two, three, to_p, to_c, to_f):
     blocks = own.shape[0]
     regions = per_column // blocks
@@ -165,13 +160,15 @@
     for code, out in ((code_p, to_p), (code_c, to_c), (code_f, to_f)):
         for s in range(out.shape[0]):
             used, _, block = decode(code[s], blocks)
-            here = used & (block // per_column == column)
             away = (block // blocks % regions) ^ me
-            for distance, source in enumerate((own, one, two, three)):
-
-                @pl.when(here & (away == distance))
-                def _(source=source, out=out, s=s, block=block):
-                    out[s] = source[block % blocks]
+
+            @pl.when(used & (block // per_column == column))
+            def _(out=out, s=s, block=block, away=away):
+                for distance, source in enumerate((own, one, two, three)):
+
+                    @pl.when(away == distance)
+                    def _(source=source):
+                        out[s] = source[block % blocks]
 
 
 def merge_kernel(
@@ -228,41 +225,35 @@
     return pl.ds(pl.multiple_of(index * rows, rows), rows)
 
 
-def halve_kernel(keep, got, kept, sent):
-    rows = kept.shape[2]
+def split_kernel(keep, got, own, one, two, three):
+    rows = own.shape[1]
     me = lax.axis_index("grp")
 
-    def piece(index):
-        at = quarter_at(index, rows)
+    def piece(bits):
+        at = quarter_at(me ^ bits, rows)
         return keep[:, at] + got[:, at].astype(F32)
 
-    kept[0] = piece(me)
-    kept[1] = piece(me ^ 3)
-    sent[0] = piece(me ^ 1).astype(BF16)
-    sent[1] = piece(me ^ 2).astype(BF16)
-
-
-def quarter_kernel(pair, got, kept, sent):
-    kept[...] = pair[0] + got[0].astype(F32)
-    sent[...] = (pair[1] + got[1].astype(F32)).astype(BF16)
-
-
-def add_kernel(scale, own, got, out):
-    out[...] = ((own[...].astype(F32) + got[...].astype(F32)) * scale).astype(out.dtype)
-
-
-def pair_kernel(own, got, out):
-    out[0] = own[...]
-    out[1] = got[...]
-
-
-def join_kernel(own, got, out):
-    rows = own.shape[2]
+    own[...] = piece(0)
+    for bits, out in ((1, one), (2, two), (3, three)):
+        out[...] = piece(bits).astype(BF16)
+
+
+def add_kernel(own, one, two, three, out):
+    total = own[...] + one[...].astype(F32) + two[...].astype(F32) + three[...].astype(F32)
+    out[...] = total.astype(BF16)
+
+
+def ordered_kernel(stride, scale, own, one, two, three, out, held):
+    me = lax.axis_index("block") // stride % 4
+    for bits, part in enumerate((own, one, two, three)):
+        held[me ^ bits] = part[...].astype(F32)
+    out[...] = ((held[0] + held[1] + held[2] + held[3]) * scale).astype(BF16)
+
+
+def join_kernel(own, one, two, three, out):
     me = lax.axis_index("grp")
-    out[:, quarter_at(me, rows)] = own[0]
-    out[:, quarter_at(me ^ 3, rows)] = own[1]
-    out[:, quarter_at(me ^ 1, rows)] = got[0]
-    out[:, quarter_at(me ^ 2, rows)] = got[1]
+    for bits, part in enumerate((own, one, two, three)):
+        out[:, quarter_at(me ^ bits, own.shape[1])] = part[...]
 
 
 def widen_kernel(own, other, out):
@@ -378,49 +369,45 @@
     )
     near_upstream, scattered = exchange(upstream, received, to_second)
     half = (kernels, width // 2, width)
-    total, keep, send = run(
+    piece = (kernels, width // 2 // regions, width)
+    store = struct((slots, points, flat), BF16)
+    z_store, keep, send = run(
         functools.partial(back_own_kernel, per_column),
-        (code, *near_upstream, masked_t, mirrored_t, grad_direct, influence),
-        [total_b, struct(half, F32), struct(half, BF16)],
+        (code, *near_upstream, masked_t, grad_direct, influence),
+        [store, struct(half, F32), struct(half, BF16)],
         "back_to_first",
-        [pltpu.VMEM((points, flat), BF16), pltpu.VMEM((width, flat), F32)],
+        [pltpu.VMEM((width, flat), F32)],
         2 * pair_flops,
     )
 
-    piece = (kernels, width // 2 // regions, width)
-    pair = (2,) + piece
     got = swap_core(after(send, *scattered))
-    kept, sent = run(halve_kernel, (keep, got), [struct(pair, F32), struct(pair, BF16)], "halve")
-    kept, sent = run(
-        quarter_kernel,
-        (kept, swap_grp(sent, 1)),
-        [struct(piece, F32), struct(piece, BF16)],
-        "quarter",
-    )
-
-    def add(own, got, dtype, scale=1.0):
-        return run(functools.partial(add_kernel, scale), (own, got), struct(piece, dtype), "add")
-
-    summed = add(kept, swap_grp(sent, 3), BF16)
+    own, *parts = run(
+        split_kernel, (keep, got), [struct(piece, F32)] + [struct(piece, BF16)] * 3, "split_half"
+    )
+    total = run(to_first_kernel, (after(code, own), z_store, mirrored_t), total_b, "to_first")
+    grad_features = run(
+        finish_kernel, (point_counts, total, *scattered), own_b, "finish_features"
+    )
+    got = [swap_grp(part, bits) for bits, part in enumerate(parts, 1)]
+    summed = run(add_kernel, (after(own, total), *got), struct(piece, BF16), "add_quarters")
     everywhere = lax.axis_size("block") * regions * blocks * points
-    for stride, bits, dtype, scale in (
-        (2, 1, BF16, 1.0),
-        (2, 3, F32, 1.0),
-        (8, 1, F32, 1.0),
-        (8, 3, BF16, 1.0 / math.sqrt(everywhere)),
-    ):
-        got = swap(summed, "block", lambda i, n=stride * bits: i ^ n)
-        summed = add(summed, got, dtype, scale)
-    two = run(pair_kernel, (summed, swap_grp(summed, 3)), struct(pair, BF16), "pair_up")
-    joined = run(join_kernel, (two, swap_grp(two, 1)), struct(half, BF16), "join_quarters")
+    for stride, scale in ((2, 1.0), (8, 1.0 / math.sqrt(everywhere))):
+        got = [swap(summed, "block", lambda i, n=stride * b: i ^ n) for b in (1, 2, 3)]
+        if stride == 2:
+            summed = after(summed, grad_features)
+        summed = run(
+            functools.partial(ordered_kernel, stride, scale),
+            (summed, *got),
+            struct(piece, BF16),
+            "add_in_order",
+            [pltpu.VMEM((4,) + piece, F32)],
+        )
+    joined = run(join_kernel, (summed, *around(summed)), struct(half, BF16), "join_quarters")
     grad_weights = run(
         widen_kernel,
         (joined, swap_core(joined)),
         struct((kernels, width, width), F32),
         "join_halves",
-    )
-    grad_features = run(
-        finish_kernel, (point_counts, total, *scattered), own_b, "finish_features"
     )
     return (activated, grad_features, grad_weights)
 

time: 139 us -> 129 us (0.928)
  Pallas kernels: 41.7 us -> 26.4 us
  starting transfers between devices: 62.1 us -> 70.4 us
  waiting for transfers between devices: 30.1 us -> 27.8 us
    pallas_call x20 -> x17, Pallas kernels: 41.7 us -> 26.4 us  [run(): pl.pallas_call(kernel, in_specs=[hbm if i in outside else smem if a.dtype...]
    ppermute x32 -> x36, starting transfers between devices: 62.1 us -> 70.4 us  [swap(): lax.ppermute(x, axis, [(i, partner(i)) for i in peers if partner(i) in pe...]
    ppermute x32 -> x36, waiting for transfers between devices: 30.1 us -> 27.8 us  [swap(): lax.ppermute(x, axis, [(i, partner(i)) for i in peers if partner(i) in pe...]
  transfers between devices with their start and end apart: 32 -> 36, of which waited for: 13 -> 15; matrix products, arithmetic and copies ran while one was open for 1% -> 1% of each run, Pallas kernels for 28% -> 18%
where the time goes in v3:
time: 129 us
  starting transfers between devices  70.4 us (55%)
  waiting for transfers between devices  27.8 us (22%)
  Pallas kernels  26.4 us (20%)
  other arithmetic  1.87 us (1%)
  between operations  1.61 us (1%)
    ppermute x36, starting transfers between devices, swap(): lax.ppermute(x, axis, [(i, partner(i)) for i in peers if partner(i) in pe...  70.4 us
    ppermute x36, waiting for transfers between devices, swap(): lax.ppermute(x, axis, [(i, partner(i)) for i in peers if partner(i) in pe...  27.8 us
    pallas_call x17, Pallas kernels, run(): pl.pallas_call(kernel, in_specs=[hbm if i in outside else smem if a.dtype...  26.4 us
  transfers between devices with their start and end apart: 36, of which 15 were waited for; matrix products, arithmetic and copies ran while one was open for 1% of the time, Pallas kernels for 18%

profile of v3, /device:TPU:1, one launch (start us, length us, event | category | flops | bytes accessed | tf_op | source)
XLA Modules:
  0.0 129.0 jit_solution(12624905045272921793)
XLA Ops:
  1.7 3.6 %collective-permute-start.4 = (bf16[4,256,128]{2,1,0:T(8,128)(2,1)S(1)}, bf16[4,256,128]{2,1,0:T(8,128)(2,1)S(1)}, u32[]{:S(2)}, u32[]{:S(2)}) collective-permute-start(bf16[4,256,128]{2,1,0:T(8,128)(2,1)S(1)} %fusion.m_ref.own), channel_id=1, source_target_pairs={{0,3},{1,2},{2,1},{3,0},{4,7},{5,6},{6,5},{7,4},{8,11},{9,10},{10,... | collective-permute-start | bytes 786440 | tf_op jit(solution)/shard_map/ppermute | solution.py:273
  7.5 4.4 %collective-permute-start.1 = (s32[8]{0:T(128)S(1)}, s32[8]{0:T(128)S(1)}, u32[]{:S(2)}, u32[]{:S(2)}) collective-permute-start(s32[8]{0:T(128)S(1)} %compare_select_fusion.code.code_c), channel_id=1, source_target_pairs={{4,8},{8,4},{12,16},{16,12},{20,24},{24,20},{28,32},{32,28},{36,40... | collective-permute-start | bytes 104 | tf_op jit(solution)/shard_map/ppermute | solution.py:273
  13.0 3.9 %own_to_second.1 = (bf16[8,128,256]{2,1,0:T(8,128)(2,1)S(1)}, bf16[4,128,256]{2,1,0:T(8,128)(2,1)S(1)}, bf16[15,128,128]{2,1,0:T(8,128)(2,1)S(1)}, bf16[8,15,256,256]{3,2,1,0:T(8,128)(2,1)S(1)}) custom-call(s32[8]{0:T(128)S(1)} %compare_select_fusion.code.code_c, bf16[4,256,128]{2,1,0:T(8,128)(2,1)S(1)} %fusion.m_ref.own, bf16[15,128,128]{2,1,0:T(8,128)(2,1)S(1)} %copy-done, ...), custom_call_target="tpu_custom_call" | custom-call | flops 2013265920 | bytes 33488928 | tf_op jit(solution)/shard_map/own_to_second/pallas_call | solution.py:31
  16.9 5.2 %collective-permute-start.7 = (bf16[8,128,256]{2,1,0:T(8,128)(2,1)S(1)}, bf16[8,128,256]{2,1,0:T(8,128)(2,1)S(1)}, u32[]{:S(2)}, u32[]{:S(2)}) collective-permute-start(bf16[8,128,256]{2,1,0:T(8,128)(2,1)S(1)} %get-tuple-element.49.part_c), channel_id=1, source_target_pairs={{4,8},{8,4},{12,16},{16,12},{20,24},{24,20},{28,32},{32,28},{36,40... | collective-permute-start | bytes 1572872 | tf_op jit(solution)/shard_map/ppermute | solution.py:273
  23.8 2.3 %collective-permute-start.8 = (bf16[8,256,128]{2,1,0:T(8,128)(2,1)S(1)}, bf16[8,256,128]{2,1,0:T(8,128)(2,1)S(1)}, u32[]{:S(2)}, u32[]{:S(2)}) collective-permute-start(bf16[8,256,128]{2,1,0:T(8,128)(2,1)S(1)} %get-tuple-element.52), channel_id=1, source_target_pairs={{4,8},{8,4},{12,16},{16,12},{20,24},{24,20},{28,32},{32,28},{36,40... | collective-permute-start | bytes 1572872 | tf_op jit(solution)/shard_map/ppermute | solution.py:273
  26.1 2.8 %collective-permute-done.7.part_f = bf16[8,128,256]{2,1,0:T(8,128)(2,1)S(1)} collective-permute-done((bf16[8,128,256]{2,1,0:T(8,128)(2,1)S(1)}, bf16[8,128,256]{2,1,0:T(8,128)(2,1)S(1)}, u32[]{:S(2)}, u32[]{:S(2)}) %collective-permute-start.7) | collective-permute-done | bytes 524320 | tf_op jit(solution)/shard_map/ppermute | solution.py:273
  31.6 2.1 %collective-permute-start.10 = (bf16[4,128,256]{2,1,0:T(8,128)(2,1)S(1)}, bf16[4,128,256]{2,1,0:T(8,128)(2,1)S(1)}, u32[]{:S(2)}, u32[]{:S(2)}) collective-permute-start(bf16[4,128,256]{2,1,0:T(8,128)(2,1)S(1)} %get-tuple-element.56), channel_id=1, source_target_pairs={{0,2},{1,3},{2,0},{3,1},{4,6},{5,7},{6,4},{7,5},{8,10},{9,11},{10,... | collective-permute-start | bytes 786440 | tf_op jit(solution)/shard_map/ppermute | solution.py:273
  34.8 3.5 %near_to_first.1 = (f32[4,256,128]{2,1,0:T(8,128)S(1)}, bf16[8,256,1920]{2,1,0:T(8,128)(2,1)S(1)}) custom-call(s32[8]{0:T(128)S(1)} %compare_select_fusion.code.code_c, bf16[8,256,128]{2,1,0:T(8,128)(2,1)S(1)} %collective-permute-done.5.chip_ref, bf16[8,256,128]{2,1,0:T(8,128)(2,1)S(1)} %get-tuple-element.51.here_ref, ...), custom_call_target="tpu_custom_call" | custom-call | flops 4026531840 | bytes 26181664 | tf_op jit(solution)/shard_map/near_to_first/pallas_call | solution.py:31
  38.3 3.8 %collective-permute-done.10.two = bf16[4,128,256]{2,1,0:T(8,128)(2,1)S(1)} collective-permute-done((bf16[4,128,256]{2,1,0:T(8,128)(2,1)S(1)}, bf16[4,128,256]{2,1,0:T(8,128)(2,1)S(1)}, u32[]{:S(2)}, u32[]{:S(2)}) %collective-permute-start.10) | collective-permute-done | bytes 262176 | tf_op jit(solution)/shard_map/ppermute | solution.py:273
  42.1 2.7 %collective-permute-done.11.three = bf16[4,128,256]{2,1,0:T(8,128)(2,1)S(1)} collective-permute-done((bf16[4,128,256]{2,1,0:T(8,128)(2,1)S(1)}, bf16[4,128,256]{2,1,0:T(8,128)(2,1)S(1)}, u32[]{:S(2)}, u32[]{:S(2)}) %collective-permute-start.11) | collective-permute-done | bytes 262176 | tf_op jit(solution)/shard_map/ppermute | solution.py:273
  47.5 2.3 %collective-permute-start.12 = (bf16[4,256,128]{2,1,0:T(8,128)(2,1)S(1)}, bf16[4,256,128]{2,1,0:T(8,128)(2,1)S(1)}, u32[]{:S(2)}, u32[]{:S(2)}) collective-permute-start(bf16[4,256,128]{2,1,0:T(8,128)(2,1)S(1)} %get-tuple-element.63.own), channel_id=1, source_target_pairs={{0,1},{1,0},{2,3},{3,2},{4,5},{5,4},{6,7},{7,6},{8,9},{9,8},{10,11... | collective-permute-start | bytes 786440 | tf_op jit(solution)/shard_map/ppermute | solution.py:273
  49.8 3.6 %back_to_second.1 = (bf16[8,128,256]{2,1,0:T(8,128)(2,1)S(1)}, f32[128,1920]{1,0:T(8,128)S(1)}) custom-call(s32[8]{0:T(128)S(1)} %compare_select_fusion.code.code_c, bf16[4,128,256]{2,1,0:T(8,128)(2,1)S(1)} %get-tuple-element.60.ut_ref, bf16[15,128,128]{2,1,0:T(8,128)(2,1)S(1)} %copy-done, bf16[8,256,1920]{2,1,0:T(8,128)(2,1)S(1)} %get-tuple-element.61.near_ref, ...), custom_call_target="tpu_custom_call" | custom-call | flops 4026531840 | bytes 25853984 | tf_op jit(solution)/shard_map/back_to_second/pallas_call | solution.py:31
  53.4 10.8 %collective-permute-start.17 = (bf16[8,128,256]{2,1,0:T(8,128)(2,1)S(1)}, bf16[8,128,256]{2,1,0:T(8,128)(2,1)S(1)}, u32[]{:S(2)}, u32[]{:S(2)}) collective-permute-start(bf16[8,128,256]{2,1,0:T(8,128)(2,1)S(1)} %get-tuple-element.66.part_c), channel_id=1, source_target_pairs={{4,8},{8,4},{12,16},{16,12},{20,24},{24,20},{28,32},{32,28},{36,40... | collective-permute-start | bytes 1572872 | tf_op jit(solution)/shard_map/ppermute | solution.py:273
  66.2 4.9 %collective-permute-start.18 = (bf16[8,256,128]{2,1,0:T(8,128)(2,1)S(1)}, bf16[8,256,128]{2,1,0:T(8,128)(2,1)S(1)}, u32[]{:S(2)}, u32[]{:S(2)}) collective-permute-start(bf16[8,256,128]{2,1,0:T(8,128)(2,1)S(1)} %get-tuple-element.69), channel_id=1, source_target_pairs={{4,8},{8,4},{12,16},{16,12},{20,24},{24,20},{28,32},{32,28},{36,40... | collective-permute-start | bytes 1572872 | tf_op jit(solution)/shard_map/ppermute | solution.py:273
  74.0 2.5 %collective-permute-start.21 = (bf16[4,128,256]{2,1,0:T(8,128)(2,1)S(1)}, bf16[4,128,256]{2,1,0:T(8,128)(2,1)S(1)}, u32[]{:S(2)}, u32[]{:S(2)}) collective-permute-start(bf16[4,128,256]{2,1,0:T(8,128)(2,1)S(1)} %get-tuple-element.76), channel_id=1, source_target_pairs={{0,3},{1,2},{2,1},{3,0},{4,7},{5,6},{6,5},{7,4},{8,11},{9,10},{10,... | collective-permute-start | bytes 786440 | tf_op jit(solution)/shard_map/ppermute | solution.py:273
  78.2 3.7 %back_to_first.1 = (bf16[8,256,1920]{2,1,0:T(8,128)(2,1)S(1)}, f32[15,64,128]{2,1,0:T(8,128)S(1)}, bf16[15,64,128]{2,1,0:T(8,128)(2,1)S(1)}) custom-call(s32[8]{0:T(128)S(1)} %compare_select_fusion.code.code_c, bf16[8,256,128]{2,1,0:T(8,128)(2,1)S(1)} %collective-permute-done.15.chip_ref, bf16[8,256,128]{2,1,0:T(8,128)(2,1)S(1)} %get-tuple-element.68.here_ref, ...), custom_call_target="tpu_custom_call" | custom-call | flops 4026531840 | bytes 27148320 | tf_op jit(solution)/shard_map/back_to_first/pallas_call | solution.py:31
  82.0 2.6 %collective-permute-done.21.three = bf16[4,128,256]{2,1,0:T(8,128)(2,1)S(1)} collective-permute-done((bf16[4,128,256]{2,1,0:T(8,128)(2,1)S(1)}, bf16[4,128,256]{2,1,0:T(8,128)(2,1)S(1)}, u32[]{:S(2)}, u32[]{:S(2)}) %collective-permute-start.21) | collective-permute-done | bytes 262176 | tf_op jit(solution)/shard_map/ppermute | solution.py:273
  86.3 4.3 %collective-permute-start.24 = (bf16[15,16,128]{2,1,0:T(8,128)(2,1)S(1)}, bf16[15,16,128]{2,1,0:T(8,128)(2,1)S(1)}, u32[]{:S(2)}, u32[]{:S(2)}) collective-permute-start(bf16[15,16,128]{2,1,0:T(8,128)(2,1)S(1)} %get-tuple-element.84), channel_id=1, source_target_pairs={{0,2},{1,3},{2,0},{3,1},{4,6},{5,7},{6,4},{7,5},{8,10},{9,11},{10,... | collective-permute-start | bytes 184328 | tf_op jit(solution)/shard_map/ppermute | solution.py:273
  90.6 1.9 %to_first.1.total = f32[4,256,128]{2,1,0:T(8,128)S(1)} custom-call(s32[8]{0:T(128)S(1)} %compare_select_fusion.code.code_c, bf16[8,256,1920]{2,1,0:T(8,128)(2,1)S(1)} %get-tuple-element.80.z_ref, bf16[15,128,128]{2,1,0:T(8,128)(2,1)S(1)} %get-tuple-element.81.wmt_ref), custom_call_target="tpu_custom_call" | custom-call | bytes 8880160 | tf_op jit(solution)/shard_map/to_first/pallas_call | solution.py:31
  94.9 8.3 %collective-permute-start.28 = (bf16[15,16,128]{2,1,0:T(8,128)(2,1)S(1)}, bf16[15,16,128]{2,1,0:T(8,128)(2,1)S(1)}, u32[]{:S(2)}, u32[]{:S(2)}) collective-permute-start(bf16[15,16,128]{2,1,0:T(8,128)(2,1)S(1)} %add_quarters.1.own), channel_id=1, source_target_pairs={{0,24},{4,28},{8,16},{12,20},{16,8},{20,12},{24,0},{28,4},{32,56},... | collective-permute-start | bytes 184328 | tf_op jit(solution)/shard_map/ppermute | solution.py:273
  105.4 2.4 %collective-permute-done.27.two = bf16[15,16,128]{2,1,0:T(8,128)(2,1)S(1)} collective-permute-done((bf16[15,16,128]{2,1,0:T(8,128)(2,1)S(1)}, bf16[15,16,128]{2,1,0:T(8,128)(2,1)S(1)}, u32[]{:S(2)}, u32[]{:S(2)}) %collective-permute-start.27) | collective-permute-done | bytes 61472 | tf_op jit(solution)/shard_map/ppermute | solution.py:273
  107.9 2.0 %collective-permute-start.31 = (bf16[15,16,128]{2,1,0:T(8,128)(2,1)S(1)}, bf16[15,16,128]{2,1,0:T(8,128)(2,1)S(1)}, u32[]{:S(2)}, u32[]{:S(2)}) collective-permute-start(bf16[15,16,128]{2,1,0:T(8,128)(2,1)S(1)} %add_in_order.2.own), channel_id=1, source_target_pairs={{0,96},{4,100},{8,104},{12,108},{16,112},{20,116},{24,120},{28,124... | collective-permute-start | bytes 184328 | tf_op jit(solution)/shard_map/ppermute | solution.py:273
  112.2 2.2 %collective-permute-done.30.two = bf16[15,16,128]{2,1,0:T(8,128)(2,1)S(1)} collective-permute-done((bf16[15,16,128]{2,1,0:T(8,128)(2,1)S(1)}, bf16[15,16,128]{2,1,0:T(8,128)(2,1)S(1)}, u32[]{:S(2)}, u32[]{:S(2)}) %collective-permute-start.30) | collective-permute-done | bytes 61472 | tf_op jit(solution)/shard_map/ppermute | solution.py:273
  120.7 6.1 %collective-permute-start.35 = (bf16[15,64,128]{2,1,0:T(8,128)(2,1)S(1)}, bf16[15,64,128]{2,1,0:T(8,128)(2,1)S(1)}, u32[]{:S(2)}, u32[]{:S(2)}) collective-permute-start(bf16[15,64,128]{2,1,0:T(8,128)(2,1)S(1)} %join_quarters.1.own), channel_id=1, source_target_pairs={{0,4},{4,0},{8,12},{12,8},{16,20},{20,16},{24,28},{28,24},{32,36},... | collective-permute-start | bytes 737288 | tf_op jit(solution)/shard_map/ppermute | solution.py:273
  (73 shorter events, 35.6 us)
Async XLA Ops:
  1.7 20.4 %collective-permute-start.4 = (bf16[4,256,128]{2,1,0:T(8,128)(2,1)S(1)}, bf16[4,256,128]{2,1,0:T(8,128)(2,1)S(1)}, u32[]{:S(2)}, u32[]{:S(2)}) collective-permute-start(bf16[4,256,128]{2,1,0:T(8,128)(2,1)S(1)} %fusion.m_ref.own), channel_id=1, source_target_pairs={{0,3},{1,2},{2,1},{3,0},{4,7},{5,6},{6,5},{7,4},{8,11},{9,10},{10,... | collective-permute-start | bytes 786440 | tf_op jit(solution)/shard_map/ppermute | solution.py:273
  5.4 16.8 %collective-permute-start.3 = (bf16[4,256,128]{2,1,0:T(8,128)(2,1)S(1)}, bf16[4,256,128]{2,1,0:T(8,128)(2,1)S(1)}, u32[]{:S(2)}, u32[]{:S(2)}) collective-permute-start(bf16[4,256,128]{2,1,0:T(8,128)(2,1)S(1)} %fusion.m_ref.own), channel_id=1, source_target_pairs={{0,2},{1,3},{2,0},{3,1},{4,6},{5,7},{6,4},{7,5},{8,10},{9,11},{10,... | collective-permute-start | bytes 786440 | tf_op jit(solution)/shard_map/ppermute | solution.py:273
  5.7 16.4 %collective-permute-start.2 = (bf16[4,256,128]{2,1,0:T(8,128)(2,1)S(1)}, bf16[4,256,128]{2,1,0:T(8,128)(2,1)S(1)}, u32[]{:S(2)}, u32[]{:S(2)}) collective-permute-start(bf16[4,256,128]{2,1,0:T(8,128)(2,1)S(1)} %fusion.m_ref.own), channel_id=1, source_target_pairs={{0,1},{1,0},{2,3},{3,2},{4,5},{5,4},{6,7},{7,6},{8,9},{9,8},{10,11... | collective-permute-start | bytes 786440 | tf_op jit(solution)/shard_map/ppermute | solution.py:273
  7.5 9.4 %collective-permute-start.1 = (s32[8]{0:T(128)S(1)}, s32[8]{0:T(128)S(1)}, u32[]{:S(2)}, u32[]{:S(2)}) collective-permute-start(s32[8]{0:T(128)S(1)} %compare_select_fusion.code.code_c), channel_id=1, source_target_pairs={{4,8},{8,4},{12,16},{16,12},{20,24},{24,20},{28,32},{32,28},{36,40... | collective-permute-start | bytes 104 | tf_op jit(solution)/shard_map/ppermute | solution.py:273
  11.8 10.2 %collective-permute-start = (s32[8]{0:T(128)S(1)}, s32[8]{0:T(128)S(1)}, u32[]{:S(2)}, u32[]{:S(2)}) collective-permute-start(s32[8]{0:T(128)S(1)} %compare_select_fusion.code.code_c), channel_id=1, source_target_pairs={{0,4},{4,0},{8,12},{12,8},{16,20},{20,16},{24,28},{28,24},{32,36},... | collective-permute-start | bytes 104 | tf_op jit(solution)/shard_map/ppermute | solution.py:273
  16.9 12.0 %collective-permute-start.7 = (bf16[8,128,256]{2,1,0:T(8,128)(2,1)S(1)}, bf16[8,128,256]{2,1,0:T(8,128)(2,1)S(1)}, u32[]{:S(2)}, u32[]{:S(2)}) collective-permute-start(bf16[8,128,256]{2,1,0:T(8,128)(2,1)S(1)} %get-tuple-element.49.part_c), channel_id=1, source_target_pairs={{4,8},{8,4},{12,16},{16,12},{20,24},{24,20},{28,32},{32,28},{36,40... | collective-permute-start | bytes 1572872 | tf_op jit(solution)/shard_map/ppermute | solution.py:273
  23.3 10.8 %collective-permute-start.5 = (bf16[8,256,128]{2,1,0:T(8,128)(2,1)S(1)}, bf16[8,256,128]{2,1,0:T(8,128)(2,1)S(1)}, u32[]{:S(2)}, u32[]{:S(2)}) collective-permute-start(bf16[8,256,128]{2,1,0:T(8,128)(2,1)S(1)} %get-tuple-element.47), channel_id=1, source_target_pairs={{0,4},{4,0},{8,12},{12,8},{16,20},{20,16},{24,28},{28,24},{32,36},... | collective-permute-start | bytes 1572872 | tf_op jit(solution)/shard_map/ppermute | solution.py:273
  23.8 10.9 %collective-permute-start.8 = (bf16[8,256,128]{2,1,0:T(8,128)(2,1)S(1)}, bf16[8,256,128]{2,1,0:T(8,128)(2,1)S(1)}, u32[]{:S(2)}, u32[]{:S(2)}) collective-permute-start(bf16[8,256,128]{2,1,0:T(8,128)(2,1)S(1)} %get-tuple-element.52), channel_id=1, source_target_pairs={{4,8},{8,4},{12,16},{16,12},{20,24},{24,20},{28,32},{32,28},{36,40... | collective-permute-start | bytes 1572872 | tf_op jit(solution)/shard_map/ppermute | solution.py:273
  30.2 8.1 %collective-permute-start.9 = (bf16[4,128,256]{2,1,0:T(8,128)(2,1)S(1)}, bf16[4,128,256]{2,1,0:T(8,128)(2,1)S(1)}, u32[]{:S(2)}, u32[]{:S(2)}) collective-permute-start(bf16[4,128,256]{2,1,0:T(8,128)(2,1)S(1)} %get-tuple-element.55), channel_id=1, source_target_pairs={{0,1},{1,0},{2,3},{3,2},{4,5},{5,4},{6,7},{7,6},{8,9},{9,8},{10,11... | collective-permute-start | bytes 786440 | tf_op jit(solution)/shard_map/ppermute | solution.py:273
  31.6 10.5 %collective-permute-start.10 = (bf16[4,128,256]{2,1,0:T(8,128)(2,1)S(1)}, bf16[4,128,256]{2,1,0:T(8,128)(2,1)S(1)}, u32[]{:S(2)}, u32[]{:S(2)}) collective-permute-start(bf16[4,128,256]{2,1,0:T(8,128)(2,1)S(1)} %get-tuple-element.56), channel_id=1, source_target_pairs={{0,2},{1,3},{2,0},{3,1},{4,6},{5,7},{6,4},{7,5},{8,10},{9,11},{10,... | collective-permute-start | bytes 786440 | tf_op jit(solution)/shard_map/ppermute | solution.py:273
  33.7 11.2 %collective-permute-start.11 = (bf16[4,128,256]{2,1,0:T(8,128)(2,1)S(1)}, bf16[4,128,256]{2,1,0:T(8,128)(2,1)S(1)}, u32[]{:S(2)}, u32[]{:S(2)}) collective-permute-start(bf16[4,128,256]{2,1,0:T(8,128)(2,1)S(1)} %get-tuple-element.57), channel_id=1, source_target_pairs={{0,3},{1,2},{2,1},{3,0},{4,7},{5,6},{6,5},{7,4},{8,11},{9,10},{10,... | collective-permute-start | bytes 786440 | tf_op jit(solution)/shard_map/ppermute | solution.py:273
  46.6 17.7 %collective-permute-start.14 = (bf16[4,256,128]{2,1,0:T(8,128)(2,1)S(1)}, bf16[4,256,128]{2,1,0:T(8,128)(2,1)S(1)}, u32[]{:S(2)}, u32[]{:S(2)}) collective-permute-start(bf16[4,256,128]{2,1,0:T(8,128)(2,1)S(1)} %get-tuple-element.63.own), channel_id=1, source_target_pairs={{0,3},{1,2},{2,1},{3,0},{4,7},{5,6},{6,5},{7,4},{8,11},{9,10},{10,... | collective-permute-start | bytes 786440 | tf_op jit(solution)/shard_map/ppermute | solution.py:273
  47.1 17.2 %collective-permute-start.13 = (bf16[4,256,128]{2,1,0:T(8,128)(2,1)S(1)}, bf16[4,256,128]{2,1,0:T(8,128)(2,1)S(1)}, u32[]{:S(2)}, u32[]{:S(2)}) collective-permute-start(bf16[4,256,128]{2,1,0:T(8,128)(2,1)S(1)} %get-tuple-element.63.own), channel_id=1, source_target_pairs={{0,2},{1,3},{2,0},{3,1},{4,6},{5,7},{6,4},{7,5},{8,10},{9,11},{10,... | collective-permute-start | bytes 786440 | tf_op jit(solution)/shard_map/ppermute | solution.py:273
  47.5 16.8 %collective-permute-start.12 = (bf16[4,256,128]{2,1,0:T(8,128)(2,1)S(1)}, bf16[4,256,128]{2,1,0:T(8,128)(2,1)S(1)}, u32[]{:S(2)}, u32[]{:S(2)}) collective-permute-start(bf16[4,256,128]{2,1,0:T(8,128)(2,1)S(1)} %get-tuple-element.63.own), channel_id=1, source_target_pairs={{0,1},{1,0},{2,3},{3,2},{4,5},{5,4},{6,7},{7,6},{8,9},{9,8},{10,11... | collective-permute-start | bytes 786440 | tf_op jit(solution)/shard_map/ppermute | solution.py:273
  53.4 17.7 %collective-permute-start.17 = (bf16[8,128,256]{2,1,0:T(8,128)(2,1)S(1)}, bf16[8,128,256]{2,1,0:T(8,128)(2,1)S(1)}, u32[]{:S(2)}, u32[]{:S(2)}) collective-permute-start(bf16[8,128,256]{2,1,0:T(8,128)(2,1)S(1)} %get-tuple-element.66.part_c), channel_id=1, source_target_pairs={{4,8},{8,4},{12,16},{16,12},{20,24},{24,20},{28,32},{32,28},{36,40... | collective-permute-start | bytes 1572872 | tf_op jit(solution)/shard_map/ppermute | solution.py:273
  64.2 6.9 %collective-permute-start.16 = (bf16[8,128,256]{2,1,0:T(8,128)(2,1)S(1)}, bf16[8,128,256]{2,1,0:T(8,128)(2,1)S(1)}, u32[]{:S(2)}, u32[]{:S(2)}) collective-permute-start(bf16[8,128,256]{2,1,0:T(8,128)(2,1)S(1)} %get-tuple-element.66.part_c), channel_id=1, source_target_pairs={{0,4},{4,0},{8,12},{12,8},{16,20},{20,16},{24,28},{28,24},{32,36},... | collective-permute-start | bytes 1572872 | tf_op jit(solution)/shard_map/ppermute | solution.py:273
  65.7 10.7 %collective-permute-start.15 = (bf16[8,256,128]{2,1,0:T(8,128)(2,1)S(1)}, bf16[8,256,128]{2,1,0:T(8,128)(2,1)S(1)}, u32[]{:S(2)}, u32[]{:S(2)}) collective-permute-start(bf16[8,256,128]{2,1,0:T(8,128)(2,1)S(1)} %get-tuple-element.64), channel_id=1, source_target_pairs={{0,4},{4,0},{8,12},{12,8},{16,20},{20,16},{24,28},{28,24},{32,36},... | collective-permute-start | bytes 1572872 | tf_op jit(solution)/shard_map/ppermute | solution.py:273
  66.2 12.1 %collective-permute-start.18 = (bf16[8,256,128]{2,1,0:T(8,128)(2,1)S(1)}, bf16[8,256,128]{2,1,0:T(8,128)(2,1)S(1)}, u32[]{:S(2)}, u32[]{:S(2)}) collective-permute-start(bf16[8,256,128]{2,1,0:T(8,128)(2,1)S(1)} %get-tuple-element.69), channel_id=1, source_target_pairs={{4,8},{8,4},{12,16},{16,12},{20,24},{24,20},{28,32},{32,28},{36,40... | collective-permute-start | bytes 1572872 | tf_op jit(solution)/shard_map/ppermute | solution.py:273
  72.5 9.5 %collective-permute-start.19 = (bf16[4,128,256]{2,1,0:T(8,128)(2,1)S(1)}, bf16[4,128,256]{2,1,0:T(8,128)(2,1)S(1)}, u32[]{:S(2)}, u32[]{:S(2)}) collective-permute-start(bf16[4,128,256]{2,1,0:T(8,128)(2,1)S(1)} %get-tuple-element.74), channel_id=1, source_target_pairs={{0,1},{1,0},{2,3},{3,2},{4,5},{5,4},{6,7},{7,6},{8,9},{9,8},{10,11... | collective-permute-start | bytes 786440 | tf_op jit(solution)/shard_map/ppermute | solution.py:273
  72.9 9.1 %collective-permute-start.20 = (bf16[4,128,256]{2,1,0:T(8,128)(2,1)S(1)}, bf16[4,128,256]{2,1,0:T(8,128)(2,1)S(1)}, u32[]{:S(2)}, u32[]{:S(2)}) collective-permute-start(bf16[4,128,256]{2,1,0:T(8,128)(2,1)S(1)} %get-tuple-element.75), channel_id=1, source_target_pairs={{0,2},{1,3},{2,0},{3,1},{4,6},{5,7},{6,4},{7,5},{8,10},{9,11},{10,... | collective-permute-start | bytes 786440 | tf_op jit(solution)/shard_map/ppermute | solution.py:273
  74.0 10.6 %collective-permute-start.21 = (bf16[4,128,256]{2,1,0:T(8,128)(2,1)S(1)}, bf16[4,128,256]{2,1,0:T(8,128)(2,1)S(1)}, u32[]{:S(2)}, u32[]{:S(2)}) collective-permute-start(bf16[4,128,256]{2,1,0:T(8,128)(2,1)S(1)} %get-tuple-element.76), channel_id=1, source_target_pairs={{0,3},{1,2},{2,1},{3,0},{4,7},{5,6},{6,5},{7,4},{8,11},{9,10},{10,... | collective-permute-start | bytes 786440 | tf_op jit(solution)/shard_map/ppermute | solution.py:273
  86.3 7.6 %collective-permute-start.24 = (bf16[15,16,128]{2,1,0:T(8,128)(2,1)S(1)}, bf16[15,16,128]{2,1,0:T(8,128)(2,1)S(1)}, u32[]{:S(2)}, u32[]{:S(2)}) collective-permute-start(bf16[15,16,128]{2,1,0:T(8,128)(2,1)S(1)} %get-tuple-element.84), channel_id=1, source_target_pairs={{0,2},{1,3},{2,0},{3,1},{4,6},{5,7},{6,4},{7,5},{8,10},{9,11},{10,... | collective-permute-start | bytes 184328 | tf_op jit(solution)/shard_map/ppermute | solution.py:273
  94.9 10.5 %collective-permute-start.28 = (bf16[15,16,128]{2,1,0:T(8,128)(2,1)S(1)}, bf16[15,16,128]{2,1,0:T(8,128)(2,1)S(1)}, u32[]{:S(2)}, u32[]{:S(2)}) collective-permute-start(bf16[15,16,128]{2,1,0:T(8,128)(2,1)S(1)} %add_quarters.1.own), channel_id=1, source_target_pairs={{0,24},{4,28},{8,16},{12,20},{16,8},{20,12},{24,0},{28,4},{32,56},... | collective-permute-start | bytes 184328 | tf_op jit(solution)/shard_map/ppermute | solution.py:273
  120.7 7.3 %collective-permute-start.35 = (bf16[15,64,128]{2,1,0:T(8,128)(2,1)S(1)}, bf16[15,64,128]{2,1,0:T(8,128)(2,1)S(1)}, u32[]{:S(2)}, u32[]{:S(2)}) collective-permute-start(bf16[15,64,128]{2,1,0:T(8,128)(2,1)S(1)} %join_quarters.1.own), channel_id=1, source_target_pairs={{0,4},{4,0},{8,12},{12,8},{16,20},{20,16},{24,28},{28,24},{32,36},... | collective-permute-start | bytes 737288 | tf_op jit(solution)/shard_map/ppermute | solution.py:273
  (15 other events, 124.7 us)

commit v4 on v3

--- a/solution.py
+++ b/solution.py
@@ -21,13 +21,14 @@
     return jax.ShapeDtypeStruct(shape, dtype)
 
 
-def run(kernel, args, outs, name, scratch=(), flops=0, outside=(), limit=20):
+def run(kernel, args, outs, name, scratch=(), flops=0, outside=(), limit=20, size=None):
     single = not isinstance(outs, (list, tuple))
     outs = [outs] if single else outs
     vmem = pl.BlockSpec(memory_space=pltpu.VMEM)
     smem = pl.BlockSpec(memory_space=pltpu.SMEM)
     hbm = pl.BlockSpec(memory_space=pltpu.HBM)
-    size = sum(a.size * a.dtype.itemsize for a in list(args) + list(outs))
+    if size is None:
+        size = sum(a.size * a.dtype.itemsize for a in list(args) + list(outs))
     result = pl.pallas_call(
         kernel,
         in_specs=[
@@ -61,14 +62,19 @@
     lax.fori_loop(0, code.shape[0], step, 0)
 
 
-def own_kernel(code, m_ref, w_ref, far_h, out_ref, mt_ref, wmt_ref, h_ref, yt, arrived):
+def own_kernel(
+    code, m_ref, far_w, far_h, out_ref, mt_ref, wmt_ref, h_ref, yt, w_ref, w_arrived, arrived
+):
     kernels, points = h_ref.shape[1], h_ref.shape[2]
     blocks = m_ref.shape[0]
 
     def fetch(s):
         return pltpu.make_async_copy(far_h.at[s], h_ref.at[s], arrived.at[s])
 
+    weights = pltpu.make_async_copy(far_w, w_ref, w_arrived)
+    weights.start()
     each_slot(code, blocks, lambda s, first, second: fetch(s).start())
+    weights.wait()
     for k in range(kernels):
         wmt_ref[k] = w_ref[kernels - 1 - k].T
     for a in range(blocks):
@@ -308,9 +314,8 @@
         return tuple(swap_grp(values, bits) for bits in (1, 2, 3))
 
     received = around(masked)
-    codes = (swap_core(code), code, swap_far(code))
-
-    def exchange(values, received, part):
+
+    def exchange(codes, values, received, part):
         part_p, part_f = swap_core(part), swap_far(part)
         to_p, to_c, to_f = run(
             functools.partial(pick_kernel, per_column),
@@ -336,13 +341,17 @@
         "own_to_second",
         [
             pltpu.VMEM((blocks, width, kernels * points), BF16),
+            pltpu.VMEM((kernels, width, width), BF16),
+            pltpu.SemaphoreType.DMA,
             pltpu.SemaphoreType.DMA((slots,)),
         ],
         pair_flops,
-        outside=(3,),
+        outside=(2, 3),
         limit=31,
     )
-    near_rows, scattered = exchange(masked, received, to_second)
+    late = after(code, to_second)
+    codes = (swap_core(late), code, swap_far(late))
+    near_rows, scattered = exchange(codes, masked, received, to_second)
     total, near_store = run(
         functools.partial(near_kernel, per_column),
         (code, *near_rows, kernel_weights, influence),
@@ -367,7 +376,7 @@
         [pltpu.VMEM((blocks, width, kernels * points), BF16)],
         2 * pair_flops,
     )
-    near_upstream, scattered = exchange(upstream, received, to_second)
+    near_upstream, scattered = exchange(codes, upstream, received, to_second)
     half = (kernels, width // 2, width)
     piece = (kernels, width // 2 // regions, width)
     store = struct((slots, points, flat), BF16)
@@ -377,19 +386,22 @@
         [store, struct(half, F32), struct(half, BF16)],
         "back_to_first",
         [pltpu.VMEM((width, flat), F32)],
-        2 * pair_flops,
-    )
-
-    got = swap_core(after(send, *scattered))
+        size=0,
+    )
+
+    got = swap_core(send)
+    total = run(to_first_kernel, (code, z_store, mirrored_t), total_b, "to_first", size=0)
     own, *parts = run(
-        split_kernel, (keep, got), [struct(piece, F32)] + [struct(piece, BF16)] * 3, "split_half"
-    )
-    total = run(to_first_kernel, (after(code, own), z_store, mirrored_t), total_b, "to_first")
+        split_kernel,
+        (keep, after(got, total)),
+        [struct(piece, F32)] + [struct(piece, BF16)] * 3,
+        "split_half",
+    )
     grad_features = run(
         finish_kernel, (point_counts, total, *scattered), own_b, "finish_features"
     )
-    got = [swap_grp(part, bits) for bits, part in enumerate(parts, 1)]
-    summed = run(add_kernel, (after(own, total), *got), struct(piece, BF16), "add_quarters")
+    got = [swap_grp(after(part, *scattered), bits) for bits, part in enumerate(parts, 1)]
+    summed = run(add_kernel, (own, *got), struct(piece, BF16), "add_quarters")
     everywhere = lax.axis_size("block") * regions * blocks * points
     for stride, scale in ((2, 1.0), (8, 1.0 / math.sqrt(everywhere))):
         got = [swap(summed, "block", lambda i, n=stride * b: i ^ n) for b in (1, 2, 3)]

time: 129 us -> 133 us (1.031)
  Pallas kernels: 26.4 us -> 33.4 us
  waiting for transfers between devices: 27.8 us -> 25.1 us
  starting transfers between devices: 70.4 us -> 68.8 us
    pallas_call x17, Pallas kernels: 26.4 us -> 33.4 us  [run(): pl.pallas_call(kernel, in_specs=[hbm if i in outside else smem if a.dtype...]
    ppermute x36, waiting for transfers between devices: 27.8 us -> 25.1 us  [swap(): lax.ppermute(x, axis, [(i, partner(i)) for i in peers if partner(i) in pe...]
    ppermute x36, starting transfers between devices: 70.4 us -> 68.8 us  [swap(): lax.ppermute(x, axis, [(i, partner(i)) for i in peers if partner(i) in pe...]
  transfers between devices with their start and end apart: 36 -> 36, of which waited for: 15 -> 16; matrix products, arithmetic and copies ran while one was open for 1% -> 1% of each run, Pallas kernels for 18% -> 23%
where the time goes in v4:
time: 133 us; the launch traced here: 132 us
  starting transfers between devices  68.8 us (52%)
  Pallas kernels  33.4 us (25%)
  waiting for transfers between devices  25.1 us (19%)
  other arithmetic  1.87 us (1%)
  between operations  1.62 us (1%)
    ppermute x36, starting transfers between devices, swap(): lax.ppermute(x, axis, [(i, partner(i)) for i in peers if partner(i) in pe...  68.8 us
    pallas_call x17, Pallas kernels, run(): pl.pallas_call(kernel, in_specs=[hbm if i in outside else smem if a.dtype...  33.4 us
    ppermute x36, waiting for transfers between devices, swap(): lax.ppermute(x, axis, [(i, partner(i)) for i in peers if partner(i) in pe...  25.1 us
  transfers between devices with their start and end apart: 36, of which 16 were waited for; matrix products, arithmetic and copies ran while one was open for 1% of the time, Pallas kernels for 23%

profile of v4, /device:TPU:1, one launch (start us, length us, event | category | flops | bytes accessed | tf_op | source)
XLA Modules:
  0.0 131.8 jit_solution(18434792132168899408)
XLA Ops:
  1.7 3.6 %collective-permute-start.4 = (bf16[4,256,128]{2,1,0:T(8,128)(2,1)S(1)}, bf16[4,256,128]{2,1,0:T(8,128)(2,1)S(1)}, u32[]{:S(2)}, u32[]{:S(2)}) collective-permute-start(bf16[4,256,128]{2,1,0:T(8,128)(2,1)S(1)} %fusion.m_ref.own), channel_id=1, source_target_pairs={{0,3},{1,2},{2,1},{3,0},{4,7},{5,6},{6,5},{7,4},{8,11},{9,10},{10,... | collective-permute-start | bytes 786440 | tf_op jit(solution)/shard_map/ppermute | solution.py:279
  8.5 5.3 %own_to_second.1 = (bf16[8,128,256]{2,1,0:T(8,128)(2,1)S(1)}, bf16[4,128,256]{2,1,0:T(8,128)(2,1)S(1)}, bf16[15,128,128]{2,1,0:T(8,128)(2,1)S(1)}, bf16[8,15,256,256]{3,2,1,0:T(8,128)(2,1)S(1)}) custom-call(s32[8]{0:T(128)S(1)} %compare_select_fusion.code.code_c, bf16[4,256,128]{2,1,0:T(8,128)(2,1)S(1)} %fusion.m_ref.own, bf16[15,128,128]{2,1,0:T(8,128)(2,1)S(1)} %copy-done, ...), custom_call_target="tpu_custom_call" | custom-call | flops 2013265920 | bytes 33488928 | tf_op jit(solution)/shard_map/own_to_second/pallas_call | solution.py:32
  13.8 6.0 %collective-permute-start.1 = (s32[8]{0:T(128)S(1)}, s32[8]{0:T(128)S(1)}, u32[]{:S(2)}, u32[]{:S(2)}) collective-permute-start(s32[8]{0:T(128)S(1)} %compare_select_fusion.code.code_c), channel_id=1, source_target_pairs={{4,8},{8,4},{12,16},{16,12},{20,24},{24,20},{28,32},{32,28},{36,40... | collective-permute-start | bytes 104 | tf_op jit(solution)/shard_map/ppermute | solution.py:279
  21.0 3.6 %collective-permute-start.7 = (bf16[8,128,256]{2,1,0:T(8,128)(2,1)S(1)}, bf16[8,128,256]{2,1,0:T(8,128)(2,1)S(1)}, u32[]{:S(2)}, u32[]{:S(2)}) collective-permute-start(bf16[8,128,256]{2,1,0:T(8,128)(2,1)S(1)} %get-tuple-element.52.part_c), channel_id=1, source_target_pairs={{4,8},{8,4},{12,16},{16,12},{20,24},{24,20},{28,32},{32,28},{36,40... | collective-permute-start | bytes 1572872 | tf_op jit(solution)/shard_map/ppermute | solution.py:279
  26.5 1.9 %collective-permute-start.8 = (bf16[8,256,128]{2,1,0:T(8,128)(2,1)S(1)}, bf16[8,256,128]{2,1,0:T(8,128)(2,1)S(1)}, u32[]{:S(2)}, u32[]{:S(2)}) collective-permute-start(bf16[8,256,128]{2,1,0:T(8,128)(2,1)S(1)} %get-tuple-element.55), channel_id=1, source_target_pairs={{4,8},{8,4},{12,16},{16,12},{20,24},{24,20},{28,32},{32,28},{36,40... | collective-permute-start | bytes 1572872 | tf_op jit(solution)/shard_map/ppermute | solution.py:279
  28.4 3.1 %collective-permute-done.7.part_f = bf16[8,128,256]{2,1,0:T(8,128)(2,1)S(1)} collective-permute-done((bf16[8,128,256]{2,1,0:T(8,128)(2,1)S(1)}, bf16[8,128,256]{2,1,0:T(8,128)(2,1)S(1)}, u32[]{:S(2)}, u32[]{:S(2)}) %collective-permute-start.7) | collective-permute-done | bytes 524320 | tf_op jit(solution)/shard_map/ppermute | solution.py:279
  33.0 1.9 %collective-permute-start.10 = (bf16[4,128,256]{2,1,0:T(8,128)(2,1)S(1)}, bf16[4,128,256]{2,1,0:T(8,128)(2,1)S(1)}, u32[]{:S(2)}, u32[]{:S(2)}) collective-permute-start(bf16[4,128,256]{2,1,0:T(8,128)(2,1)S(1)} %get-tuple-element.59), channel_id=1, source_target_pairs={{0,2},{1,3},{2,0},{3,1},{4,6},{5,7},{6,4},{7,5},{8,10},{9,11},{10,... | collective-permute-start | bytes 786440 | tf_op jit(solution)/shard_map/ppermute | solution.py:279
  37.4 5.4 %near_to_first.1 = (f32[4,256,128]{2,1,0:T(8,128)S(1)}, bf16[8,256,1920]{2,1,0:T(8,128)(2,1)S(1)}) custom-call(s32[8]{0:T(128)S(1)} %compare_select_fusion.code.code_c, bf16[8,256,128]{2,1,0:T(8,128)(2,1)S(1)} %collective-permute-done.5.chip_ref, bf16[8,256,128]{2,1,0:T(8,128)(2,1)S(1)} %get-tuple-element.54.here_ref, ...), custom_call_target="tpu_custom_call" | custom-call | flops 4026531840 | bytes 26181664 | tf_op jit(solution)/shard_map/near_to_first/pallas_call | solution.py:32
  43.1 2.7 %collective-permute-done.11.three = bf16[4,128,256]{2,1,0:T(8,128)(2,1)S(1)} collective-permute-done((bf16[4,128,256]{2,1,0:T(8,128)(2,1)S(1)}, bf16[4,128,256]{2,1,0:T(8,128)(2,1)S(1)}, u32[]{:S(2)}, u32[]{:S(2)}) %collective-permute-start.11) | collective-permute-done | bytes 262176 | tf_op jit(solution)/shard_map/ppermute | solution.py:279
  47.5 2.2 %collective-permute-start.14 = (bf16[4,256,128]{2,1,0:T(8,128)(2,1)S(1)}, bf16[4,256,128]{2,1,0:T(8,128)(2,1)S(1)}, u32[]{:S(2)}, u32[]{:S(2)}) collective-permute-start(bf16[4,256,128]{2,1,0:T(8,128)(2,1)S(1)} %get-tuple-element.66.own), channel_id=1, source_target_pairs={{0,3},{1,2},{2,1},{3,0},{4,7},{5,6},{6,5},{7,4},{8,11},{9,10},{10,... | collective-permute-start | bytes 786440 | tf_op jit(solution)/shard_map/ppermute | solution.py:279
  50.8 4.8 %back_to_second.1 = (bf16[8,128,256]{2,1,0:T(8,128)(2,1)S(1)}, f32[128,1920]{1,0:T(8,128)S(1)}) custom-call(s32[8]{0:T(128)S(1)} %compare_select_fusion.code.code_c, bf16[4,128,256]{2,1,0:T(8,128)(2,1)S(1)} %get-tuple-element.63.ut_ref, bf16[15,128,128]{2,1,0:T(8,128)(2,1)S(1)} %copy-done, bf16[8,256,1920]{2,1,0:T(8,128)(2,1)S(1)} %get-tuple-element.64.near_ref, ...), custom_call_target="tpu_custom_call" | custom-call | flops 4026531840 | bytes 25853984 | tf_op jit(solution)/shard_map/back_to_second/pallas_call | solution.py:32
  55.5 10.1 %collective-permute-start.17 = (bf16[8,128,256]{2,1,0:T(8,128)(2,1)S(1)}, bf16[8,128,256]{2,1,0:T(8,128)(2,1)S(1)}, u32[]{:S(2)}, u32[]{:S(2)}) collective-permute-start(bf16[8,128,256]{2,1,0:T(8,128)(2,1)S(1)} %get-tuple-element.69.part_c), channel_id=1, source_target_pairs={{4,8},{8,4},{12,16},{16,12},{20,24},{24,20},{28,32},{32,28},{36,40... | collective-permute-start | bytes 1572872 | tf_op jit(solution)/shard_map/ppermute | solution.py:279
  67.7 3.0 %collective-permute-start.18 = (bf16[8,256,128]{2,1,0:T(8,128)(2,1)S(1)}, bf16[8,256,128]{2,1,0:T(8,128)(2,1)S(1)}, u32[]{:S(2)}, u32[]{:S(2)}) collective-permute-start(bf16[8,256,128]{2,1,0:T(8,128)(2,1)S(1)} %get-tuple-element.72), channel_id=1, source_target_pairs={{4,8},{8,4},{12,16},{16,12},{20,24},{24,20},{28,32},{32,28},{36,40... | collective-permute-start | bytes 1572872 | tf_op jit(solution)/shard_map/ppermute | solution.py:279
  74.1 3.8 %collective-permute-start.21 = (bf16[4,128,256]{2,1,0:T(8,128)(2,1)S(1)}, bf16[4,128,256]{2,1,0:T(8,128)(2,1)S(1)}, u32[]{:S(2)}, u32[]{:S(2)}) collective-permute-start(bf16[4,128,256]{2,1,0:T(8,128)(2,1)S(1)} %get-tuple-element.79), channel_id=1, source_target_pairs={{0,3},{1,2},{2,1},{3,0},{4,7},{5,6},{6,5},{7,4},{8,11},{9,10},{10,... | collective-permute-start | bytes 786440 | tf_op jit(solution)/shard_map/ppermute | solution.py:279
  78.4 5.4 %back_to_first.1 = (bf16[8,256,1920]{2,1,0:T(8,128)(2,1)S(1)}, f32[15,64,128]{2,1,0:T(8,128)S(1)}, bf16[15,64,128]{2,1,0:T(8,128)(2,1)S(1)}) custom-call(s32[8]{0:T(128)S(1)} %compare_select_fusion.code.code_c, bf16[8,256,128]{2,1,0:T(8,128)(2,1)S(1)} %collective-permute-done.15.chip_ref, bf16[8,256,128]{2,1,0:T(8,128)(2,1)S(1)} %get-tuple-element.71.here_ref, ...), custom_call_target="tpu_custom_call" | custom-call | tf_op jit(solution)/shard_map/back_to_first/pallas_call | solution.py:32
  84.0 2.7 %to_first.1.total = f32[4,256,128]{2,1,0:T(8,128)S(1)} custom-call(s32[8]{0:T(128)S(1)} %compare_select_fusion.code.code_c, bf16[8,256,1920]{2,1,0:T(8,128)(2,1)S(1)} %get-tuple-element.75.z_ref, bf16[15,128,128]{2,1,0:T(8,128)(2,1)S(1)} %get-tuple-element.76.wmt_ref), custom_call_target="tpu_custom_call" | custom-call | tf_op jit(solution)/shard_map/to_first/pallas_call | solution.py:32
  86.9 3.5 %collective-permute-start.24 = (bf16[15,16,128]{2,1,0:T(8,128)(2,1)S(1)}, bf16[15,16,128]{2,1,0:T(8,128)(2,1)S(1)}, u32[]{:S(2)}, u32[]{:S(2)}) collective-permute-start(bf16[15,16,128]{2,1,0:T(8,128)(2,1)S(1)} %get-tuple-element.87), channel_id=1, source_target_pairs={{0,2},{1,3},{2,0},{3,1},{4,6},{5,7},{6,4},{7,5},{8,10},{9,11},{10,... | collective-permute-start | bytes 184328 | tf_op jit(solution)/shard_map/ppermute | solution.py:279
  90.8 3.0 %collective-permute-done.24.two = bf16[15,16,128]{2,1,0:T(8,128)(2,1)S(1)} collective-permute-done((bf16[15,16,128]{2,1,0:T(8,128)(2,1)S(1)}, bf16[15,16,128]{2,1,0:T(8,128)(2,1)S(1)}, u32[]{:S(2)}, u32[]{:S(2)}) %collective-permute-start.24) | collective-permute-done | bytes 61472 | tf_op jit(solution)/shard_map/ppermute | solution.py:279
  95.3 10.2 %collective-permute-start.28 = (bf16[15,16,128]{2,1,0:T(8,128)(2,1)S(1)}, bf16[15,16,128]{2,1,0:T(8,128)(2,1)S(1)}, u32[]{:S(2)}, u32[]{:S(2)}) collective-permute-start(bf16[15,16,128]{2,1,0:T(8,128)(2,1)S(1)} %add_quarters.1.own), channel_id=1, source_target_pairs={{0,24},{4,28},{8,16},{12,20},{16,8},{20,12},{24,0},{28,4},{32,56},... | collective-permute-start | bytes 184328 | tf_op jit(solution)/shard_map/ppermute | solution.py:279
  107.6 2.4 %collective-permute-done.27.two = bf16[15,16,128]{2,1,0:T(8,128)(2,1)S(1)} collective-permute-done((bf16[15,16,128]{2,1,0:T(8,128)(2,1)S(1)}, bf16[15,16,128]{2,1,0:T(8,128)(2,1)S(1)}, u32[]{:S(2)}, u32[]{:S(2)}) %collective-permute-start.27) | collective-permute-done | bytes 61472 | tf_op jit(solution)/shard_map/ppermute | solution.py:279
  110.2 4.0 %collective-permute-start.30 = (bf16[15,16,128]{2,1,0:T(8,128)(2,1)S(1)}, bf16[15,16,128]{2,1,0:T(8,128)(2,1)S(1)}, u32[]{:S(2)}, u32[]{:S(2)}) collective-permute-start(bf16[15,16,128]{2,1,0:T(8,128)(2,1)S(1)} %add_in_order.2.own), channel_id=1, source_target_pairs={{0,64},{4,68},{8,72},{12,76},{16,80},{20,84},{24,88},{28,92},{32,9... | collective-permute-start | bytes 184328 | tf_op jit(solution)/shard_map/ppermute | solution.py:279
  117.4 2.5 %collective-permute-start.34 = (bf16[15,16,128]{2,1,0:T(8,128)(2,1)S(1)}, bf16[15,16,128]{2,1,0:T(8,128)(2,1)S(1)}, u32[]{:S(2)}, u32[]{:S(2)}) collective-permute-start(bf16[15,16,128]{2,1,0:T(8,128)(2,1)S(1)} %add_in_order.3.own), channel_id=1, source_target_pairs={{0,3},{1,2},{2,1},{3,0},{4,7},{5,6},{6,5},{7,4},{8,11},{9,10},{10,... | collective-permute-start | bytes 184328 | tf_op jit(solution)/shard_map/ppermute | solution.py:279
  121.8 2.7 %collective-permute-done.33.two = bf16[15,16,128]{2,1,0:T(8,128)(2,1)S(1)} collective-permute-done((bf16[15,16,128]{2,1,0:T(8,128)(2,1)S(1)}, bf16[15,16,128]{2,1,0:T(8,128)(2,1)S(1)}, u32[]{:S(2)}, u32[]{:S(2)}) %collective-permute-start.33) | collective-permute-done | bytes 61472 | tf_op jit(solution)/shard_map/ppermute | solution.py:279
  124.5 5.1 %collective-permute-start.35 = (bf16[15,64,128]{2,1,0:T(8,128)(2,1)S(1)}, bf16[15,64,128]{2,1,0:T(8,128)(2,1)S(1)}, u32[]{:S(2)}, u32[]{:S(2)}) collective-permute-start(bf16[15,64,128]{2,1,0:T(8,128)(2,1)S(1)} %join_quarters.1.own), channel_id=1, source_target_pairs={{0,4},{4,0},{8,12},{12,8},{16,20},{20,16},{24,28},{28,24},{32,36},... | collective-permute-start | bytes 737288 | tf_op jit(solution)/shard_map/ppermute | solution.py:279
  (73 shorter events, 31.1 us)
Async XLA Ops:
  1.7 23.0 %collective-permute-start.4 = (bf16[4,256,128]{2,1,0:T(8,128)(2,1)S(1)}, bf16[4,256,128]{2,1,0:T(8,128)(2,1)S(1)}, u32[]{:S(2)}, u32[]{:S(2)}) collective-permute-start(bf16[4,256,128]{2,1,0:T(8,128)(2,1)S(1)} %fusion.m_ref.own), channel_id=1, source_target_pairs={{0,3},{1,2},{2,1},{3,0},{4,7},{5,6},{6,5},{7,4},{8,11},{9,10},{10,... | collective-permute-start | bytes 786440 | tf_op jit(solution)/shard_map/ppermute | solution.py:279
  5.4 19.4 %collective-permute-start.3 = (bf16[4,256,128]{2,1,0:T(8,128)(2,1)S(1)}, bf16[4,256,128]{2,1,0:T(8,128)(2,1)S(1)}, u32[]{:S(2)}, u32[]{:S(2)}) collective-permute-start(bf16[4,256,128]{2,1,0:T(8,128)(2,1)S(1)} %fusion.m_ref.own), channel_id=1, source_target_pairs={{0,2},{1,3},{2,0},{3,1},{4,6},{5,7},{6,4},{7,5},{8,10},{9,11},{10,... | collective-permute-start | bytes 786440 | tf_op jit(solution)/shard_map/ppermute | solution.py:279
  5.7 19.1 %collective-permute-start.2 = (bf16[4,256,128]{2,1,0:T(8,128)(2,1)S(1)}, bf16[4,256,128]{2,1,0:T(8,128)(2,1)S(1)}, u32[]{:S(2)}, u32[]{:S(2)}) collective-permute-start(bf16[4,256,128]{2,1,0:T(8,128)(2,1)S(1)} %fusion.m_ref.own), channel_id=1, source_target_pairs={{0,1},{1,0},{2,3},{3,2},{4,5},{5,4},{6,7},{7,6},{8,9},{9,8},{10,11... | collective-permute-start | bytes 786440 | tf_op jit(solution)/shard_map/ppermute | solution.py:279
  13.8 7.2 %collective-permute-start.1 = (s32[8]{0:T(128)S(1)}, s32[8]{0:T(128)S(1)}, u32[]{:S(2)}, u32[]{:S(2)}) collective-permute-start(s32[8]{0:T(128)S(1)} %compare_select_fusion.code.code_c), channel_id=1, source_target_pairs={{4,8},{8,4},{12,16},{16,12},{20,24},{24,20},{28,32},{32,28},{36,40... | collective-permute-start | bytes 104 | tf_op jit(solution)/shard_map/ppermute | solution.py:279
  21.0 10.5 %collective-permute-start.7 = (bf16[8,128,256]{2,1,0:T(8,128)(2,1)S(1)}, bf16[8,128,256]{2,1,0:T(8,128)(2,1)S(1)}, u32[]{:S(2)}, u32[]{:S(2)}) collective-permute-start(bf16[8,128,256]{2,1,0:T(8,128)(2,1)S(1)} %get-tuple-element.52.part_c), channel_id=1, source_target_pairs={{4,8},{8,4},{12,16},{16,12},{20,24},{24,20},{28,32},{32,28},{36,40... | collective-permute-start | bytes 1572872 | tf_op jit(solution)/shard_map/ppermute | solution.py:279
  24.7 6.8 %collective-permute-start.6 = (bf16[8,128,256]{2,1,0:T(8,128)(2,1)S(1)}, bf16[8,128,256]{2,1,0:T(8,128)(2,1)S(1)}, u32[]{:S(2)}, u32[]{:S(2)}) collective-permute-start(bf16[8,128,256]{2,1,0:T(8,128)(2,1)S(1)} %get-tuple-element.52.part_c), channel_id=1, source_target_pairs={{0,4},{4,0},{8,12},{12,8},{16,20},{20,16},{24,28},{28,24},{32,36},... | collective-permute-start | bytes 1572872 | tf_op jit(solution)/shard_map/ppermute | solution.py:279
  26.0 10.8 %collective-permute-start.5 = (bf16[8,256,128]{2,1,0:T(8,128)(2,1)S(1)}, bf16[8,256,128]{2,1,0:T(8,128)(2,1)S(1)}, u32[]{:S(2)}, u32[]{:S(2)}) collective-permute-start(bf16[8,256,128]{2,1,0:T(8,128)(2,1)S(1)} %get-tuple-element.50), channel_id=1, source_target_pairs={{0,4},{4,0},{8,12},{12,8},{16,20},{20,16},{24,28},{28,24},{32,36},... | collective-permute-start | bytes 1572872 | tf_op jit(solution)/shard_map/ppermute | solution.py:279
  26.5 10.9 %collective-permute-start.8 = (bf16[8,256,128]{2,1,0:T(8,128)(2,1)S(1)}, bf16[8,256,128]{2,1,0:T(8,128)(2,1)S(1)}, u32[]{:S(2)}, u32[]{:S(2)}) collective-permute-start(bf16[8,256,128]{2,1,0:T(8,128)(2,1)S(1)} %get-tuple-element.55), channel_id=1, source_target_pairs={{4,8},{8,4},{12,16},{16,12},{20,24},{24,20},{28,32},{32,28},{36,40... | collective-permute-start | bytes 1572872 | tf_op jit(solution)/shard_map/ppermute | solution.py:279
  32.9 10.0 %collective-permute-start.9 = (bf16[4,128,256]{2,1,0:T(8,128)(2,1)S(1)}, bf16[4,128,256]{2,1,0:T(8,128)(2,1)S(1)}, u32[]{:S(2)}, u32[]{:S(2)}) collective-permute-start(bf16[4,128,256]{2,1,0:T(8,128)(2,1)S(1)} %get-tuple-element.58), channel_id=1, source_target_pairs={{0,1},{1,0},{2,3},{3,2},{4,5},{5,4},{6,7},{7,6},{8,9},{9,8},{10,11... | collective-permute-start | bytes 786440 | tf_op jit(solution)/shard_map/ppermute | solution.py:279
  33.0 10.1 %collective-permute-start.10 = (bf16[4,128,256]{2,1,0:T(8,128)(2,1)S(1)}, bf16[4,128,256]{2,1,0:T(8,128)(2,1)S(1)}, u32[]{:S(2)}, u32[]{:S(2)}) collective-permute-start(bf16[4,128,256]{2,1,0:T(8,128)(2,1)S(1)} %get-tuple-element.59), channel_id=1, source_target_pairs={{0,2},{1,3},{2,0},{3,1},{4,6},{5,7},{6,4},{7,5},{8,10},{9,11},{10,... | collective-permute-start | bytes 786440 | tf_op jit(solution)/shard_map/ppermute | solution.py:279
  34.9 10.9 %collective-permute-start.11 = (bf16[4,128,256]{2,1,0:T(8,128)(2,1)S(1)}, bf16[4,128,256]{2,1,0:T(8,128)(2,1)S(1)}, u32[]{:S(2)}, u32[]{:S(2)}) collective-permute-start(bf16[4,128,256]{2,1,0:T(8,128)(2,1)S(1)} %get-tuple-element.60), channel_id=1, source_target_pairs={{0,3},{1,2},{2,1},{3,0},{4,7},{5,6},{6,5},{7,4},{8,11},{9,10},{10,... | collective-permute-start | bytes 786440 | tf_op jit(solution)/shard_map/ppermute | solution.py:279
  47.5 18.2 %collective-permute-start.14 = (bf16[4,256,128]{2,1,0:T(8,128)(2,1)S(1)}, bf16[4,256,128]{2,1,0:T(8,128)(2,1)S(1)}, u32[]{:S(2)}, u32[]{:S(2)}) collective-permute-start(bf16[4,256,128]{2,1,0:T(8,128)(2,1)S(1)} %get-tuple-element.66.own), channel_id=1, source_target_pairs={{0,3},{1,2},{2,1},{3,0},{4,7},{5,6},{6,5},{7,4},{8,11},{9,10},{10,... | collective-permute-start | bytes 786440 | tf_op jit(solution)/shard_map/ppermute | solution.py:279
  49.8 16.0 %collective-permute-start.13 = (bf16[4,256,128]{2,1,0:T(8,128)(2,1)S(1)}, bf16[4,256,128]{2,1,0:T(8,128)(2,1)S(1)}, u32[]{:S(2)}, u32[]{:S(2)}) collective-permute-start(bf16[4,256,128]{2,1,0:T(8,128)(2,1)S(1)} %get-tuple-element.66.own), channel_id=1, source_target_pairs={{0,2},{1,3},{2,0},{3,1},{4,6},{5,7},{6,4},{7,5},{8,10},{9,11},{10,... | collective-permute-start | bytes 786440 | tf_op jit(solution)/shard_map/ppermute | solution.py:279
  49.8 16.0 %collective-permute-start.12 = (bf16[4,256,128]{2,1,0:T(8,128)(2,1)S(1)}, bf16[4,256,128]{2,1,0:T(8,128)(2,1)S(1)}, u32[]{:S(2)}, u32[]{:S(2)}) collective-permute-start(bf16[4,256,128]{2,1,0:T(8,128)(2,1)S(1)} %get-tuple-element.66.own), channel_id=1, source_target_pairs={{0,1},{1,0},{2,3},{3,2},{4,5},{5,4},{6,7},{7,6},{8,9},{9,8},{10,11... | collective-permute-start | bytes 786440 | tf_op jit(solution)/shard_map/ppermute | solution.py:279
  55.5 17.0 %collective-permute-start.17 = (bf16[8,128,256]{2,1,0:T(8,128)(2,1)S(1)}, bf16[8,128,256]{2,1,0:T(8,128)(2,1)S(1)}, u32[]{:S(2)}, u32[]{:S(2)}) collective-permute-start(bf16[8,128,256]{2,1,0:T(8,128)(2,1)S(1)} %get-tuple-element.69.part_c), channel_id=1, source_target_pairs={{4,8},{8,4},{12,16},{16,12},{20,24},{24,20},{28,32},{32,28},{36,40... | collective-permute-start | bytes 1572872 | tf_op jit(solution)/shard_map/ppermute | solution.py:279
  65.7 6.9 %collective-permute-start.16 = (bf16[8,128,256]{2,1,0:T(8,128)(2,1)S(1)}, bf16[8,128,256]{2,1,0:T(8,128)(2,1)S(1)}, u32[]{:S(2)}, u32[]{:S(2)}) collective-permute-start(bf16[8,128,256]{2,1,0:T(8,128)(2,1)S(1)} %get-tuple-element.69.part_c), channel_id=1, source_target_pairs={{0,4},{4,0},{8,12},{12,8},{16,20},{20,16},{24,28},{28,24},{32,36},... | collective-permute-start | bytes 1572872 | tf_op jit(solution)/shard_map/ppermute | solution.py:279
  67.2 10.7 %collective-permute-start.15 = (bf16[8,256,128]{2,1,0:T(8,128)(2,1)S(1)}, bf16[8,256,128]{2,1,0:T(8,128)(2,1)S(1)}, u32[]{:S(2)}, u32[]{:S(2)}) collective-permute-start(bf16[8,256,128]{2,1,0:T(8,128)(2,1)S(1)} %get-tuple-element.67), channel_id=1, source_target_pairs={{0,4},{4,0},{8,12},{12,8},{16,20},{20,16},{24,28},{28,24},{32,36},... | collective-permute-start | bytes 1572872 | tf_op jit(solution)/shard_map/ppermute | solution.py:279
  67.7 10.8 %collective-permute-start.18 = (bf16[8,256,128]{2,1,0:T(8,128)(2,1)S(1)}, bf16[8,256,128]{2,1,0:T(8,128)(2,1)S(1)}, u32[]{:S(2)}, u32[]{:S(2)}) collective-permute-start(bf16[8,256,128]{2,1,0:T(8,128)(2,1)S(1)} %get-tuple-element.72), channel_id=1, source_target_pairs={{4,8},{8,4},{12,16},{16,12},{20,24},{24,20},{28,32},{32,28},{36,40... | collective-permute-start | bytes 1572872 | tf_op jit(solution)/shard_map/ppermute | solution.py:279
  73.9 12.9 %collective-permute-start.19 = (bf16[4,128,256]{2,1,0:T(8,128)(2,1)S(1)}, bf16[4,128,256]{2,1,0:T(8,128)(2,1)S(1)}, u32[]{:S(2)}, u32[]{:S(2)}) collective-permute-start(bf16[4,128,256]{2,1,0:T(8,128)(2,1)S(1)} %get-tuple-element.77), channel_id=1, source_target_pairs={{0,1},{1,0},{2,3},{3,2},{4,5},{5,4},{6,7},{7,6},{8,9},{9,8},{10,11... | collective-permute-start | bytes 786440 | tf_op jit(solution)/shard_map/ppermute | solution.py:279
  74.0 12.8 %collective-permute-start.20 = (bf16[4,128,256]{2,1,0:T(8,128)(2,1)S(1)}, bf16[4,128,256]{2,1,0:T(8,128)(2,1)S(1)}, u32[]{:S(2)}, u32[]{:S(2)}) collective-permute-start(bf16[4,128,256]{2,1,0:T(8,128)(2,1)S(1)} %get-tuple-element.78), channel_id=1, source_target_pairs={{0,2},{1,3},{2,0},{3,1},{4,6},{5,7},{6,4},{7,5},{8,10},{9,11},{10,... | collective-permute-start | bytes 786440 | tf_op jit(solution)/shard_map/ppermute | solution.py:279
  74.1 12.7 %collective-permute-start.21 = (bf16[4,128,256]{2,1,0:T(8,128)(2,1)S(1)}, bf16[4,128,256]{2,1,0:T(8,128)(2,1)S(1)}, u32[]{:S(2)}, u32[]{:S(2)}) collective-permute-start(bf16[4,128,256]{2,1,0:T(8,128)(2,1)S(1)} %get-tuple-element.79), channel_id=1, source_target_pairs={{0,3},{1,2},{2,1},{3,0},{4,7},{5,6},{6,5},{7,4},{8,11},{9,10},{10,... | collective-permute-start | bytes 786440 | tf_op jit(solution)/shard_map/ppermute | solution.py:279
  86.9 6.9 %collective-permute-start.24 = (bf16[15,16,128]{2,1,0:T(8,128)(2,1)S(1)}, bf16[15,16,128]{2,1,0:T(8,128)(2,1)S(1)}, u32[]{:S(2)}, u32[]{:S(2)}) collective-permute-start(bf16[15,16,128]{2,1,0:T(8,128)(2,1)S(1)} %get-tuple-element.87), channel_id=1, source_target_pairs={{0,2},{1,3},{2,0},{3,1},{4,6},{5,7},{6,4},{7,5},{8,10},{9,11},{10,... | collective-permute-start | bytes 184328 | tf_op jit(solution)/shard_map/ppermute | solution.py:279
  95.3 12.3 %collective-permute-start.28 = (bf16[15,16,128]{2,1,0:T(8,128)(2,1)S(1)}, bf16[15,16,128]{2,1,0:T(8,128)(2,1)S(1)}, u32[]{:S(2)}, u32[]{:S(2)}) collective-permute-start(bf16[15,16,128]{2,1,0:T(8,128)(2,1)S(1)} %add_quarters.1.own), channel_id=1, source_target_pairs={{0,24},{4,28},{8,16},{12,20},{16,8},{20,12},{24,0},{28,4},{32,56},... | collective-permute-start | bytes 184328 | tf_op jit(solution)/shard_map/ppermute | solution.py:279
  124.5 6.2 %collective-permute-start.35 = (bf16[15,64,128]{2,1,0:T(8,128)(2,1)S(1)}, bf16[15,64,128]{2,1,0:T(8,128)(2,1)S(1)}, u32[]{:S(2)}, u32[]{:S(2)}) collective-permute-start(bf16[15,64,128]{2,1,0:T(8,128)(2,1)S(1)} %join_quarters.1.own), channel_id=1, source_target_pairs={{0,4},{4,0},{8,12},{12,8},{16,20},{20,16},{24,28},{28,24},{32,36},... | collective-permute-start | bytes 737288 | tf_op jit(solution)/shard_map/ppermute | solution.py:279
  (15 other events, 127.8 us)

commit v5 on v4

--- a/solution.py
+++ b/solution.py
@@ -49,7 +49,7 @@
     return code > 0, code % blocks, jnp.maximum(code // blocks - 1, 0)
 
 
-def each_slot(code, blocks, work):
+def each_slot(code, blocks, work, unused=None):
     def step(s, carry):
         used, first, second = decode(code[s], blocks)
 
@@ -57,24 +57,25 @@
         def _():
             work(s, first, second)
 
+        if unused is not None:
+
+            @pl.when(jnp.logical_not(used))
+            def _():
+                unused(s)
+
         return carry
 
     lax.fori_loop(0, code.shape[0], step, 0)
 
 
-def own_kernel(
-    code, m_ref, far_w, far_h, out_ref, mt_ref, wmt_ref, h_ref, yt, w_ref, w_arrived, arrived
-):
+def own_kernel(code, m_ref, w_ref, far_h, out_ref, mt_ref, wmt_ref, h_ref, yt, arrived):
     kernels, points = h_ref.shape[1], h_ref.shape[2]
     blocks = m_ref.shape[0]
 
     def fetch(s):
         return pltpu.make_async_copy(far_h.at[s], h_ref.at[s], arrived.at[s])
 
-    weights = pltpu.make_async_copy(far_w, w_ref, w_arrived)
-    weights.start()
     each_slot(code, blocks, lambda s, first, second: fetch(s).start())
-    weights.wait()
     for k in range(kernels):
         wmt_ref[k] = w_ref[kernels - 1 - k].T
     for a in range(blocks):
@@ -95,6 +96,23 @@
     column = second // per_column - here
     beside = jnp.where(column == 1 - 2 * (here % 2), chip_ref[s], far_ref[s])
     return jnp.where(column == 0, here_ref[s], beside)
+
+
+def clear(ref, s):
+    ref[s] = jnp.zeros(ref.shape[1:], ref.dtype)
+
+
+def add_rows(code, terms_ref, w_ref, total_ref):
+    blocks = total_ref.shape[0]
+    w = w_ref[...].reshape(terms_ref.shape[2], total_ref.shape[2])
+    for s in range(terms_ref.shape[0]):
+        total_ref[code[s] % blocks] += dot(terms_ref[s], w)
+
+
+def line_up(code, blocks_ref, line):
+    blocks, _, points = blocks_ref.shape
+    for s in range(code.shape[0]):
+        line[:, s * points : (s + 1) * points] = blocks_ref[code[s] % blocks]
 
 
 def near_kernel(per_column, code, chip_ref, here_ref, far_ref, w_ref, h_ref, total_ref, near_ref):
@@ -127,19 +145,31 @@
 
 
 def back_own_kernel(
-    per_column, code, chip_ref, here_ref, far_ref, mt_ref, gd_ref, h_ref, z_ref, keep_ref, send_ref, gm
+    per_column,
+    code,
+    chip_ref,
+    here_ref,
+    far_ref,
+    mt_ref,
+    gd_ref,
+    h_ref,
+    z_ref,
+    keep_ref,
+    send_ref,
+    gm,
+    line,
 ):
     kernels, width = h_ref.shape[1], here_ref.shape[2]
     half = width // 2
-    gm[...] = jnp.zeros_like(gm)
 
     def work(s, first, second):
         x = second_rows(s, second, per_column, chip_ref, here_ref, far_ref)
         for k in range(kernels):
             z_ref[s, :, k * width : (k + 1) * width] = dot(h_ref[s, k], x).astype(BF16)
-        gm[...] += dot(mt_ref[first], z_ref[s])
-
-    each_slot(code, mt_ref.shape[0], work)
+
+    each_slot(code, mt_ref.shape[0], work, functools.partial(clear, z_ref))
+    line_up(code, mt_ref, line)
+    gm[...] = dot(line[...], z_ref[...].reshape(-1, kernels * width))
     core = lax.axis_index("block") % 2
     for k in range(kernels):
         at = (kernels - 1 - k) * width
@@ -150,13 +180,8 @@
 
 
 def to_first_kernel(code, z_ref, wmt_ref, total_ref):
-    kernels, width = wmt_ref.shape[0], wmt_ref.shape[1]
     total_ref[...] = jnp.zeros_like(total_ref)
-
-    def work(s, first, second):
-        total_ref[first] += dot(z_ref[s], wmt_ref[...].reshape(kernels * width, width))
-
-    each_slot(code, total_ref.shape[0], work)
+    add_rows(code, z_ref, wmt_ref, total_ref)
 
 
 def pick_kernel(per_column, code_p, code_c, code_f, own, one, two, three, to_p, to_c, to_f):
@@ -311,11 +336,13 @@
     total_b = struct((blocks, points, width), F32)
 
     def around(values):
-        return tuple(swap_grp(values, bits) for bits in (1, 2, 3))
+        three, one, two = (swap_grp(values, bits) for bits in (3, 1, 2))
+        return one, two, three
 
     received = around(masked)
-
-    def exchange(codes, values, received, part):
+    codes = (swap_core(code), code, swap_far(code))
+
+    def exchange(values, received, part):
         part_p, part_f = swap_core(part), swap_far(part)
         to_p, to_c, to_f = run(
             functools.partial(pick_kernel, per_column),
@@ -334,6 +361,8 @@
         scattered = (own, *(swap_grp(parts[bits - 1], bits) for bits in (1, 2, 3)))
         return (from_p, after(to_c, own), from_f), scattered
 
+    line = pltpu.VMEM((width, slots * points), BF16)
+
     to_second, masked_t, mirrored_t, influence = run(
         own_kernel,
         (code, masked, kernel_weights, influence),
@@ -341,17 +370,13 @@
         "own_to_second",
         [
             pltpu.VMEM((blocks, width, kernels * points), BF16),
-            pltpu.VMEM((kernels, width, width), BF16),
-            pltpu.SemaphoreType.DMA,
             pltpu.SemaphoreType.DMA((slots,)),
         ],
         pair_flops,
-        outside=(2, 3),
+        outside=(3,),
         limit=31,
     )
-    late = after(code, to_second)
-    codes = (swap_core(late), code, swap_far(late))
-    near_rows, scattered = exchange(codes, masked, received, to_second)
+    near_rows, scattered = exchange(masked, received, to_second)
     total, near_store = run(
         functools.partial(near_kernel, per_column),
         (code, *near_rows, kernel_weights, influence),
@@ -376,7 +401,7 @@
         [pltpu.VMEM((blocks, width, kernels * points), BF16)],
         2 * pair_flops,
     )
-    near_upstream, scattered = exchange(codes, upstream, received, to_second)
+    near_upstream, scattered = exchange(upstream, received, to_second)
     half = (kernels, width // 2, width)
     piece = (kernels, width // 2 // regions, width)
     store = struct((slots, points, flat), BF16)
@@ -385,7 +410,7 @@
         (code, *near_upstream, masked_t, grad_direct, influence),
         [store, struct(half, F32), struct(half, BF16)],
         "back_to_first",
-        [pltpu.VMEM((width, flat), F32)],
+        [pltpu.VMEM((width, flat), F32), line],
         size=0,
     )
 

time: 133 us -> 128 us (0.962); the launches traced: 132 us -> 128 us
  Pallas kernels: 33.4 us -> 41.2 us
  waiting for transfers between devices: 25.1 us -> 18.1 us
  starting transfers between devices: 68.8 us -> 64.3 us
    pallas_call x17, Pallas kernels: 33.4 us -> 41.2 us  [run(): pl.pallas_call(kernel, in_specs=[hbm if i in outside else smem if a.dtype...]
    ppermute x36, waiting for transfers between devices: 25.1 us -> 18.1 us  [swap(): lax.ppermute(x, axis, [(i, partner(i)) for i in peers if partner(i) in pe...]
    ppermute x36, starting transfers between devices: 68.8 us -> 64.3 us  [swap(): lax.ppermute(x, axis, [(i, partner(i)) for i in peers if partner(i) in pe...]
  transfers between devices with their start and end apart: 36 -> 36, of which waited for: 16 -> 12; matrix products, arithmetic and copies ran while one was open for 1% -> 1% of each run, Pallas kernels for 23% -> 30%
where the time goes in v5:
time: 128 us
  starting transfers between devices  64.3 us (50%)
  Pallas kernels  41.2 us (32%)
  waiting for transfers between devices  18.1 us (14%)
  other arithmetic  1.87 us (1%)
  between operations  1.65 us (1%)
    ppermute x36, starting transfers between devices, swap(): lax.ppermute(x, axis, [(i, partner(i)) for i in peers if partner(i) in pe...  64.3 us
    pallas_call x17, Pallas kernels, run(): pl.pallas_call(kernel, in_specs=[hbm if i in outside else smem if a.dtype...  41.2 us
    ppermute x36, waiting for transfers between devices, swap(): lax.ppermute(x, axis, [(i, partner(i)) for i in peers if partner(i) in pe...  18.1 us
  transfers between devices with their start and end apart: 36, of which 12 were waited for; matrix products, arithmetic and copies ran while one was open for 1% of the time, Pallas kernels for 30%

profile of v5, /device:TPU:1, one launch (start us, length us, event | category | flops | bytes accessed | tf_op | source)
XLA Modules:
  0.0 128.2 jit_solution(1846269886854230462)
XLA Ops:
  1.7 3.6 %collective-permute-start.4 = (bf16[4,256,128]{2,1,0:T(8,128)(2,1)S(1)}, bf16[4,256,128]{2,1,0:T(8,128)(2,1)S(1)}, u32[]{:S(2)}, u32[]{:S(2)}) collective-permute-start(bf16[4,256,128]{2,1,0:T(8,128)(2,1)S(1)} %fusion.m_ref.own), channel_id=1, source_target_pairs={{0,3},{1,2},{2,1},{3,0},{4,7},{5,6},{6,5},{7,4},{8,11},{9,10},{10,... | collective-permute-start | bytes 786440 | tf_op jit(solution)/shard_map/ppermute | solution.py:304
  7.5 4.4 %collective-permute-start.1 = (s32[8]{0:T(128)S(1)}, s32[8]{0:T(128)S(1)}, u32[]{:S(2)}, u32[]{:S(2)}) collective-permute-start(s32[8]{0:T(128)S(1)} %compare_select_fusion.code.code_c), channel_id=1, source_target_pairs={{4,8},{8,4},{12,16},{16,12},{20,24},{24,20},{28,32},{32,28},{36,40... | collective-permute-start | bytes 104 | tf_op jit(solution)/shard_map/ppermute | solution.py:304
  13.0 6.6 %own_to_second.1 = (bf16[8,128,256]{2,1,0:T(8,128)(2,1)S(1)}, bf16[4,128,256]{2,1,0:T(8,128)(2,1)S(1)}, bf16[15,128,128]{2,1,0:T(8,128)(2,1)S(1)}, bf16[8,15,256,256]{3,2,1,0:T(8,128)(2,1)S(1)}) custom-call(s32[8]{0:T(128)S(1)} %compare_select_fusion.code.code_c, bf16[4,256,128]{2,1,0:T(8,128)(2,1)S(1)} %fusion.m_ref.own, bf16[15,128,128]{2,1,0:T(8,128)(2,1)S(1)} %copy-done, ...), custom_call_target="tpu_custom_call" | custom-call | flops 2013265920 | bytes 33488928 | tf_op jit(solution)/shard_map/own_to_second/pallas_call | solution.py:32
  19.6 1.9 %collective-permute-start.7 = (bf16[8,128,256]{2,1,0:T(8,128)(2,1)S(1)}, bf16[8,128,256]{2,1,0:T(8,128)(2,1)S(1)}, u32[]{:S(2)}, u32[]{:S(2)}) collective-permute-start(bf16[8,128,256]{2,1,0:T(8,128)(2,1)S(1)} %get-tuple-element.50.part_c), channel_id=1, source_target_pairs={{4,8},{8,4},{12,16},{16,12},{20,24},{24,20},{28,32},{32,28},{36,40... | collective-permute-start | bytes 1572872 | tf_op jit(solution)/shard_map/ppermute | solution.py:304
  23.5 4.3 %collective-permute-start.8 = (bf16[8,256,128]{2,1,0:T(8,128)(2,1)S(1)}, bf16[8,256,128]{2,1,0:T(8,128)(2,1)S(1)}, u32[]{:S(2)}, u32[]{:S(2)}) collective-permute-start(bf16[8,256,128]{2,1,0:T(8,128)(2,1)S(1)} %get-tuple-element.53), channel_id=1, source_target_pairs={{4,8},{8,4},{12,16},{16,12},{20,24},{24,20},{28,32},{32,28},{36,40... | collective-permute-start | bytes 1572872 | tf_op jit(solution)/shard_map/ppermute | solution.py:304
  27.7 2.7 %collective-permute-done.7.part_f = bf16[8,128,256]{2,1,0:T(8,128)(2,1)S(1)} collective-permute-done((bf16[8,128,256]{2,1,0:T(8,128)(2,1)S(1)}, bf16[8,128,256]{2,1,0:T(8,128)(2,1)S(1)}, u32[]{:S(2)}, u32[]{:S(2)}) %collective-permute-start.7) | collective-permute-done | bytes 524320 | tf_op jit(solution)/shard_map/ppermute | solution.py:304
  31.8 2.6 %collective-permute-start.10 = (bf16[4,128,256]{2,1,0:T(8,128)(2,1)S(1)}, bf16[4,128,256]{2,1,0:T(8,128)(2,1)S(1)}, u32[]{:S(2)}, u32[]{:S(2)}) collective-permute-start(bf16[4,128,256]{2,1,0:T(8,128)(2,1)S(1)} %get-tuple-element.57), channel_id=1, source_target_pairs={{0,2},{1,3},{2,0},{3,1},{4,6},{5,7},{6,4},{7,5},{8,10},{9,11},{10,... | collective-permute-start | bytes 786440 | tf_op jit(solution)/shard_map/ppermute | solution.py:304
  36.0 8.2 %near_to_first.1 = (f32[4,256,128]{2,1,0:T(8,128)S(1)}, bf16[8,256,1920]{2,1,0:T(8,128)(2,1)S(1)}) custom-call(s32[8]{0:T(128)S(1)} %compare_select_fusion.code.code_c, bf16[8,256,128]{2,1,0:T(8,128)(2,1)S(1)} %collective-permute-done.5.chip_ref, bf16[8,256,128]{2,1,0:T(8,128)(2,1)S(1)} %get-tuple-element.52.here_ref, ...), custom_call_target="tpu_custom_call" | custom-call | flops 4026531840 | bytes 26181664 | tf_op jit(solution)/shard_map/near_to_first/pallas_call | solution.py:32
  45.3 1.7 %activate.1 = (bf16[4,256,128]{2,1,0:T(8,128)(2,1)}, bf16[4,256,128]{2,1,0:T(8,128)(2,1)S(1)}, bf16[4,128,256]{2,1,0:T(8,128)(2,1)S(1)}) custom-call(s32[4]{0:T(128)S(1)} %copy-done.2, f32[4,256,128]{2,1,0:T(8,128)S(1)} %get-tuple-element.55.total, f32[4,128,256]{2,1,0:T(8,128)S(1)} %get-tuple-element.51.own, ...), custom_call_target="tpu_custom_call" | custom-call | bytes 2883600 | tf_op jit(solution)/shard_map/activate/pallas_call | solution.py:32
  50.3 6.5 %back_to_second.1 = (bf16[8,128,256]{2,1,0:T(8,128)(2,1)S(1)}, f32[128,1920]{1,0:T(8,128)S(1)}) custom-call(s32[8]{0:T(128)S(1)} %compare_select_fusion.code.code_c, bf16[4,128,256]{2,1,0:T(8,128)(2,1)S(1)} %get-tuple-element.61.ut_ref, bf16[15,128,128]{2,1,0:T(8,128)(2,1)S(1)} %copy-done, bf16[8,256,1920]{2,1,0:T(8,128)(2,1)S(1)} %get-tuple-element.62.near_ref, ...), custom_call_target="tpu_custom_call" | custom-call | flops 4026531840 | bytes 25853984 | tf_op jit(solution)/shard_map/back_to_second/pallas_call | solution.py:32
  56.9 6.2 %collective-permute-start.17 = (bf16[8,128,256]{2,1,0:T(8,128)(2,1)S(1)}, bf16[8,128,256]{2,1,0:T(8,128)(2,1)S(1)}, u32[]{:S(2)}, u32[]{:S(2)}) collective-permute-start(bf16[8,128,256]{2,1,0:T(8,128)(2,1)S(1)} %get-tuple-element.67.part_c), channel_id=1, source_target_pairs={{4,8},{8,4},{12,16},{16,12},{20,24},{24,20},{28,32},{32,28},{36,40... | collective-permute-start | bytes 1572872 | tf_op jit(solution)/shard_map/ppermute | solution.py:304
  65.1 6.3 %collective-permute-start.18 = (bf16[8,256,128]{2,1,0:T(8,128)(2,1)S(1)}, bf16[8,256,128]{2,1,0:T(8,128)(2,1)S(1)}, u32[]{:S(2)}, u32[]{:S(2)}) collective-permute-start(bf16[8,256,128]{2,1,0:T(8,128)(2,1)S(1)} %get-tuple-element.70), channel_id=1, source_target_pairs={{4,8},{8,4},{12,16},{16,12},{20,24},{24,20},{28,32},{32,28},{36,40... | collective-permute-start | bytes 1572872 | tf_op jit(solution)/shard_map/ppermute | solution.py:304
  72.9 2.6 %collective-permute-start.20 = (bf16[4,128,256]{2,1,0:T(8,128)(2,1)S(1)}, bf16[4,128,256]{2,1,0:T(8,128)(2,1)S(1)}, u32[]{:S(2)}, u32[]{:S(2)}) collective-permute-start(bf16[4,128,256]{2,1,0:T(8,128)(2,1)S(1)} %get-tuple-element.76), channel_id=1, source_target_pairs={{0,2},{1,3},{2,0},{3,1},{4,6},{5,7},{6,4},{7,5},{8,10},{9,11},{10,... | collective-permute-start | bytes 786440 | tf_op jit(solution)/shard_map/ppermute | solution.py:304
  76.8 1.8 %collective-permute-done.18.far_ref = bf16[8,256,128]{2,1,0:T(8,128)(2,1)S(1)} collective-permute-done((bf16[8,256,128]{2,1,0:T(8,128)(2,1)S(1)}, bf16[8,256,128]{2,1,0:T(8,128)(2,1)S(1)}, u32[]{:S(2)}, u32[]{:S(2)}) %collective-permute-start.18) | collective-permute-done | bytes 524320 | tf_op jit(solution)/shard_map/ppermute | solution.py:304
  78.6 7.4 %back_to_first.1 = (bf16[8,256,1920]{2,1,0:T(8,128)(2,1)S(1)}, f32[15,64,128]{2,1,0:T(8,128)S(1)}, bf16[15,64,128]{2,1,0:T(8,128)(2,1)S(1)}) custom-call(s32[8]{0:T(128)S(1)} %compare_select_fusion.code.code_c, bf16[8,256,128]{2,1,0:T(8,128)(2,1)S(1)} %collective-permute-done.15.chip_ref, bf16[8,256,128]{2,1,0:T(8,128)(2,1)S(1)} %get-tuple-element.69.here_ref, ...), custom_call_target="tpu_custom_call" | custom-call | tf_op jit(solution)/shard_map/back_to_first/pallas_call | solution.py:32
  86.1 2.8 %to_first.1.total = f32[4,256,128]{2,1,0:T(8,128)S(1)} custom-call(s32[8]{0:T(128)S(1)} %compare_select_fusion.code.code_c, bf16[8,256,1920]{2,1,0:T(8,128)(2,1)S(1)} %get-tuple-element.73.z_ref, bf16[15,128,128]{2,1,0:T(8,128)(2,1)S(1)} %get-tuple-element.74.wmt_ref), custom_call_target="tpu_custom_call" | custom-call | tf_op jit(solution)/shard_map/to_first/pallas_call | solution.py:32
  89.9 3.0 %collective-permute-start.25 = (bf16[15,16,128]{2,1,0:T(8,128)(2,1)S(1)}, bf16[15,16,128]{2,1,0:T(8,128)(2,1)S(1)}, u32[]{:S(2)}, u32[]{:S(2)}) collective-permute-start(bf16[15,16,128]{2,1,0:T(8,128)(2,1)S(1)} %get-tuple-element.87), channel_id=1, source_target_pairs={{0,3},{1,2},{2,1},{3,0},{4,7},{5,6},{6,5},{7,4},{8,11},{9,10},{10,... | collective-permute-start | bytes 184328 | tf_op jit(solution)/shard_map/ppermute | solution.py:304
  93.8 1.8 %collective-permute-done.25.three = bf16[15,16,128]{2,1,0:T(8,128)(2,1)S(1)} collective-permute-done((bf16[15,16,128]{2,1,0:T(8,128)(2,1)S(1)}, bf16[15,16,128]{2,1,0:T(8,128)(2,1)S(1)}, u32[]{:S(2)}, u32[]{:S(2)}) %collective-permute-start.25) | collective-permute-done | bytes 61472 | tf_op jit(solution)/shard_map/ppermute | solution.py:304
  95.6 4.4 %collective-permute-start.28 = (bf16[15,16,128]{2,1,0:T(8,128)(2,1)S(1)}, bf16[15,16,128]{2,1,0:T(8,128)(2,1)S(1)}, u32[]{:S(2)}, u32[]{:S(2)}) collective-permute-start(bf16[15,16,128]{2,1,0:T(8,128)(2,1)S(1)} %add_quarters.1.own), channel_id=1, source_target_pairs={{0,24},{4,28},{8,16},{12,20},{16,8},{20,12},{24,0},{28,4},{32,56},... | collective-permute-start | bytes 184328 | tf_op jit(solution)/shard_map/ppermute | solution.py:304
  102.1 2.4 %collective-permute-done.27.two = bf16[15,16,128]{2,1,0:T(8,128)(2,1)S(1)} collective-permute-done((bf16[15,16,128]{2,1,0:T(8,128)(2,1)S(1)}, bf16[15,16,128]{2,1,0:T(8,128)(2,1)S(1)}, u32[]{:S(2)}, u32[]{:S(2)}) %collective-permute-start.27) | collective-permute-done | bytes 61472 | tf_op jit(solution)/shard_map/ppermute | solution.py:304
  105.9 4.5 %collective-permute-start.30 = (bf16[15,16,128]{2,1,0:T(8,128)(2,1)S(1)}, bf16[15,16,128]{2,1,0:T(8,128)(2,1)S(1)}, u32[]{:S(2)}, u32[]{:S(2)}) collective-permute-start(bf16[15,16,128]{2,1,0:T(8,128)(2,1)S(1)} %add_in_order.2.own), channel_id=1, source_target_pairs={{0,64},{4,68},{8,72},{12,76},{16,80},{20,84},{24,88},{28,92},{32,9... | collective-permute-start | bytes 184328 | tf_op jit(solution)/shard_map/ppermute | solution.py:304
  110.4 1.6 %collective-permute-done.30.two = bf16[15,16,128]{2,1,0:T(8,128)(2,1)S(1)} collective-permute-done((bf16[15,16,128]{2,1,0:T(8,128)(2,1)S(1)}, bf16[15,16,128]{2,1,0:T(8,128)(2,1)S(1)}, u32[]{:S(2)}, u32[]{:S(2)}) %collective-permute-start.30) | collective-permute-done | bytes 61472 | tf_op jit(solution)/shard_map/ppermute | solution.py:304
  118.1 1.7 %collective-permute-done.33.two = bf16[15,16,128]{2,1,0:T(8,128)(2,1)S(1)} collective-permute-done((bf16[15,16,128]{2,1,0:T(8,128)(2,1)S(1)}, bf16[15,16,128]{2,1,0:T(8,128)(2,1)S(1)}, u32[]{:S(2)}, u32[]{:S(2)}) %collective-permute-start.33) | collective-permute-done | bytes 61472 | tf_op jit(solution)/shard_map/ppermute | solution.py:304
  119.9 6.1 %collective-permute-start.35 = (bf16[15,64,128]{2,1,0:T(8,128)(2,1)S(1)}, bf16[15,64,128]{2,1,0:T(8,128)(2,1)S(1)}, u32[]{:S(2)}, u32[]{:S(2)}) collective-permute-start(bf16[15,64,128]{2,1,0:T(8,128)(2,1)S(1)} %join_quarters.1.own), channel_id=1, source_target_pairs={{0,4},{4,0},{8,12},{12,8},{16,20},{20,16},{24,28},{28,24},{32,36},... | collective-permute-start | bytes 737288 | tf_op jit(solution)/shard_map/ppermute | solution.py:304
  (73 shorter events, 31.2 us)
Async XLA Ops:
  1.7 19.9 %collective-permute-start.4 = (bf16[4,256,128]{2,1,0:T(8,128)(2,1)S(1)}, bf16[4,256,128]{2,1,0:T(8,128)(2,1)S(1)}, u32[]{:S(2)}, u32[]{:S(2)}) collective-permute-start(bf16[4,256,128]{2,1,0:T(8,128)(2,1)S(1)} %fusion.m_ref.own), channel_id=1, source_target_pairs={{0,3},{1,2},{2,1},{3,0},{4,7},{5,6},{6,5},{7,4},{8,11},{9,10},{10,... | collective-permute-start | bytes 786440 | tf_op jit(solution)/shard_map/ppermute | solution.py:304
  5.4 16.3 %collective-permute-start.3 = (bf16[4,256,128]{2,1,0:T(8,128)(2,1)S(1)}, bf16[4,256,128]{2,1,0:T(8,128)(2,1)S(1)}, u32[]{:S(2)}, u32[]{:S(2)}) collective-permute-start(bf16[4,256,128]{2,1,0:T(8,128)(2,1)S(1)} %fusion.m_ref.own), channel_id=1, source_target_pairs={{0,2},{1,3},{2,0},{3,1},{4,6},{5,7},{6,4},{7,5},{8,10},{9,11},{10,... | collective-permute-start | bytes 786440 | tf_op jit(solution)/shard_map/ppermute | solution.py:304
  5.7 15.9 %collective-permute-start.2 = (bf16[4,256,128]{2,1,0:T(8,128)(2,1)S(1)}, bf16[4,256,128]{2,1,0:T(8,128)(2,1)S(1)}, u32[]{:S(2)}, u32[]{:S(2)}) collective-permute-start(bf16[4,256,128]{2,1,0:T(8,128)(2,1)S(1)} %fusion.m_ref.own), channel_id=1, source_target_pairs={{0,1},{1,0},{2,3},{3,2},{4,5},{5,4},{6,7},{7,6},{8,9},{9,8},{10,11... | collective-permute-start | bytes 786440 | tf_op jit(solution)/shard_map/ppermute | solution.py:304
  7.5 12.1 %collective-permute-start.1 = (s32[8]{0:T(128)S(1)}, s32[8]{0:T(128)S(1)}, u32[]{:S(2)}, u32[]{:S(2)}) collective-permute-start(s32[8]{0:T(128)S(1)} %compare_select_fusion.code.code_c), channel_id=1, source_target_pairs={{4,8},{8,4},{12,16},{16,12},{20,24},{24,20},{28,32},{32,28},{36,40... | collective-permute-start | bytes 104 | tf_op jit(solution)/shard_map/ppermute | solution.py:304
  11.8 9.7 %collective-permute-start = (s32[8]{0:T(128)S(1)}, s32[8]{0:T(128)S(1)}, u32[]{:S(2)}, u32[]{:S(2)}) collective-permute-start(s32[8]{0:T(128)S(1)} %compare_select_fusion.code.code_c), channel_id=1, source_target_pairs={{0,4},{4,0},{8,12},{12,8},{16,20},{20,16},{24,28},{28,24},{32,36},... | collective-permute-start | bytes 104 | tf_op jit(solution)/shard_map/ppermute | solution.py:304
  19.6 10.8 %collective-permute-start.7 = (bf16[8,128,256]{2,1,0:T(8,128)(2,1)S(1)}, bf16[8,128,256]{2,1,0:T(8,128)(2,1)S(1)}, u32[]{:S(2)}, u32[]{:S(2)}) collective-permute-start(bf16[8,128,256]{2,1,0:T(8,128)(2,1)S(1)} %get-tuple-element.50.part_c), channel_id=1, source_target_pairs={{4,8},{8,4},{12,16},{16,12},{20,24},{24,20},{28,32},{32,28},{36,40... | collective-permute-start | bytes 1572872 | tf_op jit(solution)/shard_map/ppermute | solution.py:304
  21.5 8.9 %collective-permute-start.6 = (bf16[8,128,256]{2,1,0:T(8,128)(2,1)S(1)}, bf16[8,128,256]{2,1,0:T(8,128)(2,1)S(1)}, u32[]{:S(2)}, u32[]{:S(2)}) collective-permute-start(bf16[8,128,256]{2,1,0:T(8,128)(2,1)S(1)} %get-tuple-element.50.part_c), channel_id=1, source_target_pairs={{0,4},{4,0},{8,12},{12,8},{16,20},{20,16},{24,28},{28,24},{32,36},... | collective-permute-start | bytes 1572872 | tf_op jit(solution)/shard_map/ppermute | solution.py:304
  22.8 12.9 %collective-permute-start.5 = (bf16[8,256,128]{2,1,0:T(8,128)(2,1)S(1)}, bf16[8,256,128]{2,1,0:T(8,128)(2,1)S(1)}, u32[]{:S(2)}, u32[]{:S(2)}) collective-permute-start(bf16[8,256,128]{2,1,0:T(8,128)(2,1)S(1)} %get-tuple-element.48), channel_id=1, source_target_pairs={{0,4},{4,0},{8,12},{12,8},{16,20},{20,16},{24,28},{28,24},{32,36},... | collective-permute-start | bytes 1572872 | tf_op jit(solution)/shard_map/ppermute | solution.py:304
  23.5 12.6 %collective-permute-start.8 = (bf16[8,256,128]{2,1,0:T(8,128)(2,1)S(1)}, bf16[8,256,128]{2,1,0:T(8,128)(2,1)S(1)}, u32[]{:S(2)}, u32[]{:S(2)}) collective-permute-start(bf16[8,256,128]{2,1,0:T(8,128)(2,1)S(1)} %get-tuple-element.53), channel_id=1, source_target_pairs={{4,8},{8,4},{12,16},{16,12},{20,24},{24,20},{28,32},{32,28},{36,40... | collective-permute-start | bytes 1572872 | tf_op jit(solution)/shard_map/ppermute | solution.py:304
  31.7 12.5 %collective-permute-start.9 = (bf16[4,128,256]{2,1,0:T(8,128)(2,1)S(1)}, bf16[4,128,256]{2,1,0:T(8,128)(2,1)S(1)}, u32[]{:S(2)}, u32[]{:S(2)}) collective-permute-start(bf16[4,128,256]{2,1,0:T(8,128)(2,1)S(1)} %get-tuple-element.56), channel_id=1, source_target_pairs={{0,1},{1,0},{2,3},{3,2},{4,5},{5,4},{6,7},{7,6},{8,9},{9,8},{10,11... | collective-permute-start | bytes 786440 | tf_op jit(solution)/shard_map/ppermute | solution.py:304
  31.8 12.4 %collective-permute-start.10 = (bf16[4,128,256]{2,1,0:T(8,128)(2,1)S(1)}, bf16[4,128,256]{2,1,0:T(8,128)(2,1)S(1)}, u32[]{:S(2)}, u32[]{:S(2)}) collective-permute-start(bf16[4,128,256]{2,1,0:T(8,128)(2,1)S(1)} %get-tuple-element.57), channel_id=1, source_target_pairs={{0,2},{1,3},{2,0},{3,1},{4,6},{5,7},{6,4},{7,5},{8,10},{9,11},{10,... | collective-permute-start | bytes 786440 | tf_op jit(solution)/shard_map/ppermute | solution.py:304
  34.4 10.9 %collective-permute-start.11 = (bf16[4,128,256]{2,1,0:T(8,128)(2,1)S(1)}, bf16[4,128,256]{2,1,0:T(8,128)(2,1)S(1)}, u32[]{:S(2)}, u32[]{:S(2)}) collective-permute-start(bf16[4,128,256]{2,1,0:T(8,128)(2,1)S(1)} %get-tuple-element.58), channel_id=1, source_target_pairs={{0,3},{1,2},{2,1},{3,0},{4,7},{5,6},{6,5},{7,4},{8,11},{9,10},{10,... | collective-permute-start | bytes 786440 | tf_op jit(solution)/shard_map/ppermute | solution.py:304
  47.1 16.1 %collective-permute-start.14 = (bf16[4,256,128]{2,1,0:T(8,128)(2,1)S(1)}, bf16[4,256,128]{2,1,0:T(8,128)(2,1)S(1)}, u32[]{:S(2)}, u32[]{:S(2)}) collective-permute-start(bf16[4,256,128]{2,1,0:T(8,128)(2,1)S(1)} %get-tuple-element.64.own), channel_id=1, source_target_pairs={{0,3},{1,2},{2,1},{3,0},{4,7},{5,6},{6,5},{7,4},{8,11},{9,10},{10,... | collective-permute-start | bytes 786440 | tf_op jit(solution)/shard_map/ppermute | solution.py:304
  47.8 15.4 %collective-permute-start.13 = (bf16[4,256,128]{2,1,0:T(8,128)(2,1)S(1)}, bf16[4,256,128]{2,1,0:T(8,128)(2,1)S(1)}, u32[]{:S(2)}, u32[]{:S(2)}) collective-permute-start(bf16[4,256,128]{2,1,0:T(8,128)(2,1)S(1)} %get-tuple-element.64.own), channel_id=1, source_target_pairs={{0,2},{1,3},{2,0},{3,1},{4,6},{5,7},{6,4},{7,5},{8,10},{9,11},{10,... | collective-permute-start | bytes 786440 | tf_op jit(solution)/shard_map/ppermute | solution.py:304
  49.2 14.0 %collective-permute-start.12 = (bf16[4,256,128]{2,1,0:T(8,128)(2,1)S(1)}, bf16[4,256,128]{2,1,0:T(8,128)(2,1)S(1)}, u32[]{:S(2)}, u32[]{:S(2)}) collective-permute-start(bf16[4,256,128]{2,1,0:T(8,128)(2,1)S(1)} %get-tuple-element.64.own), channel_id=1, source_target_pairs={{0,1},{1,0},{2,3},{3,2},{4,5},{5,4},{6,7},{7,6},{8,9},{9,8},{10,11... | collective-permute-start | bytes 786440 | tf_op jit(solution)/shard_map/ppermute | solution.py:304
  56.9 14.6 %collective-permute-start.17 = (bf16[8,128,256]{2,1,0:T(8,128)(2,1)S(1)}, bf16[8,128,256]{2,1,0:T(8,128)(2,1)S(1)}, u32[]{:S(2)}, u32[]{:S(2)}) collective-permute-start(bf16[8,128,256]{2,1,0:T(8,128)(2,1)S(1)} %get-tuple-element.67.part_c), channel_id=1, source_target_pairs={{4,8},{8,4},{12,16},{16,12},{20,24},{24,20},{28,32},{32,28},{36,40... | collective-permute-start | bytes 1572872 | tf_op jit(solution)/shard_map/ppermute | solution.py:304
  63.0 8.5 %collective-permute-start.16 = (bf16[8,128,256]{2,1,0:T(8,128)(2,1)S(1)}, bf16[8,128,256]{2,1,0:T(8,128)(2,1)S(1)}, u32[]{:S(2)}, u32[]{:S(2)}) collective-permute-start(bf16[8,128,256]{2,1,0:T(8,128)(2,1)S(1)} %get-tuple-element.67.part_c), channel_id=1, source_target_pairs={{0,4},{4,0},{8,12},{12,8},{16,20},{20,16},{24,28},{28,24},{32,36},... | collective-permute-start | bytes 1572872 | tf_op jit(solution)/shard_map/ppermute | solution.py:304
  64.5 12.3 %collective-permute-start.15 = (bf16[8,256,128]{2,1,0:T(8,128)(2,1)S(1)}, bf16[8,256,128]{2,1,0:T(8,128)(2,1)S(1)}, u32[]{:S(2)}, u32[]{:S(2)}) collective-permute-start(bf16[8,256,128]{2,1,0:T(8,128)(2,1)S(1)} %get-tuple-element.65), channel_id=1, source_target_pairs={{0,4},{4,0},{8,12},{12,8},{16,20},{20,16},{24,28},{28,24},{32,36},... | collective-permute-start | bytes 1572872 | tf_op jit(solution)/shard_map/ppermute | solution.py:304
  65.1 13.5 %collective-permute-start.18 = (bf16[8,256,128]{2,1,0:T(8,128)(2,1)S(1)}, bf16[8,256,128]{2,1,0:T(8,128)(2,1)S(1)}, u32[]{:S(2)}, u32[]{:S(2)}) collective-permute-start(bf16[8,256,128]{2,1,0:T(8,128)(2,1)S(1)} %get-tuple-element.70), channel_id=1, source_target_pairs={{4,8},{8,4},{12,16},{16,12},{20,24},{24,20},{28,32},{32,28},{36,40... | collective-permute-start | bytes 1572872 | tf_op jit(solution)/shard_map/ppermute | solution.py:304
  72.8 16.1 %collective-permute-start.19 = (bf16[4,128,256]{2,1,0:T(8,128)(2,1)S(1)}, bf16[4,128,256]{2,1,0:T(8,128)(2,1)S(1)}, u32[]{:S(2)}, u32[]{:S(2)}) collective-permute-start(bf16[4,128,256]{2,1,0:T(8,128)(2,1)S(1)} %get-tuple-element.75), channel_id=1, source_target_pairs={{0,1},{1,0},{2,3},{3,2},{4,5},{5,4},{6,7},{7,6},{8,9},{9,8},{10,11... | collective-permute-start | bytes 786440 | tf_op jit(solution)/shard_map/ppermute | solution.py:304
  72.9 16.1 %collective-permute-start.20 = (bf16[4,128,256]{2,1,0:T(8,128)(2,1)S(1)}, bf16[4,128,256]{2,1,0:T(8,128)(2,1)S(1)}, u32[]{:S(2)}, u32[]{:S(2)}) collective-permute-start(bf16[4,128,256]{2,1,0:T(8,128)(2,1)S(1)} %get-tuple-element.76), channel_id=1, source_target_pairs={{0,2},{1,3},{2,0},{3,1},{4,6},{5,7},{6,4},{7,5},{8,10},{9,11},{10,... | collective-permute-start | bytes 786440 | tf_op jit(solution)/shard_map/ppermute | solution.py:304
  75.6 13.4 %collective-permute-start.21 = (bf16[4,128,256]{2,1,0:T(8,128)(2,1)S(1)}, bf16[4,128,256]{2,1,0:T(8,128)(2,1)S(1)}, u32[]{:S(2)}, u32[]{:S(2)}) collective-permute-start(bf16[4,128,256]{2,1,0:T(8,128)(2,1)S(1)} %get-tuple-element.77), channel_id=1, source_target_pairs={{0,3},{1,2},{2,1},{3,0},{4,7},{5,6},{6,5},{7,4},{8,11},{9,10},{10,... | collective-permute-start | bytes 786440 | tf_op jit(solution)/shard_map/ppermute | solution.py:304
  95.6 6.5 %collective-permute-start.28 = (bf16[15,16,128]{2,1,0:T(8,128)(2,1)S(1)}, bf16[15,16,128]{2,1,0:T(8,128)(2,1)S(1)}, u32[]{:S(2)}, u32[]{:S(2)}) collective-permute-start(bf16[15,16,128]{2,1,0:T(8,128)(2,1)S(1)} %add_quarters.1.own), channel_id=1, source_target_pairs={{0,24},{4,28},{8,16},{12,20},{16,8},{20,12},{24,0},{28,4},{32,56},... | collective-permute-start | bytes 184328 | tf_op jit(solution)/shard_map/ppermute | solution.py:304
  119.9 7.3 %collective-permute-start.35 = (bf16[15,64,128]{2,1,0:T(8,128)(2,1)S(1)}, bf16[15,64,128]{2,1,0:T(8,128)(2,1)S(1)}, u32[]{:S(2)}, u32[]{:S(2)}) collective-permute-start(bf16[15,64,128]{2,1,0:T(8,128)(2,1)S(1)} %join_quarters.1.own), channel_id=1, source_target_pairs={{0,4},{4,0},{8,12},{12,8},{16,20},{20,16},{24,28},{28,24},{32,36},... | collective-permute-start | bytes 737288 | tf_op jit(solution)/shard_map/ppermute | solution.py:304
  (15 other events, 125.1 us)

commit v6 on v5

--- a/solution.py
+++ b/solution.py
@@ -128,10 +128,10 @@
     each_slot(code, total_ref.shape[0], work)
 
 
-def back_near_kernel(code, ut_ref, w_ref, near_ref, h_ref, out_ref, gd_ref, vt):
+def back_near_kernel(code, ut_ref, w_ref, near_ref, h_ref, out_ref, gd_ref, vt, gdt):
     kernels, points, width = h_ref.shape[1], h_ref.shape[2], w_ref.shape[1]
     blocks = ut_ref.shape[0]
-    gd_ref[...] = jnp.zeros_like(gd_ref)
+    gdt[...] = jnp.zeros_like(gdt)
     for a in range(blocks):
         u = ut_ref[a]
         for k in range(kernels):
@@ -139,9 +139,11 @@
 
     def work(s, first, second):
         out_ref[s] = dot(vt[first], h_ref[s].reshape(kernels * points, points)).astype(BF16)
-        gd_ref[...] += dot(ut_ref[first], near_ref[s])
+        gdt[...] += dot(ut_ref[first], near_ref[s])
 
     each_slot(code, blocks, work)
+    for k in range(kernels):
+        gd_ref[k] = gdt[:, k * width : (k + 1) * width].T
 
 
 def back_own_kernel(
@@ -173,7 +175,7 @@
     core = lax.axis_index("block") % 2
     for k in range(kernels):
         at = (kernels - 1 - k) * width
-        both = gd_ref[:, k * width : (k + 1) * width].T + gm[:, at : at + width]
+        both = gd_ref[k] + gm[:, at : at + width]
         low, high = both[:half], both[half:]
         keep_ref[k] = jnp.where(core == 0, low, high)
         send_ref[k] = jnp.where(core == 0, high, low).astype(BF16)
@@ -184,18 +186,20 @@
     add_rows(code, z_ref, wmt_ref, total_ref)
 
 
-def pick_kernel(per_column, code_p, code_c, code_f, own, one, two, three, to_p, to_c, to_f):
-    blocks = own.shape[0]
+def pick_kernel(per_column, *refs):
+    count = (len(refs) - 4) // 2
+    codes, sources, outs = refs[:count], refs[count : count + 4], refs[count + 4 :]
+    blocks = sources[0].shape[0]
     regions = per_column // blocks
     me, column = lax.axis_index("grp"), lax.axis_index("block")
-    for code, out in ((code_p, to_p), (code_c, to_c), (code_f, to_f)):
+    for code, out in zip(codes, outs):
         for s in range(out.shape[0]):
             used, _, block = decode(code[s], blocks)
             away = (block // blocks % regions) ^ me
 
             @pl.when(used & (block // per_column == column))
             def _(out=out, s=s, block=block, away=away):
-                for distance, source in enumerate((own, one, two, three)):
+                for distance, source in enumerate(sources):
 
                     @pl.when(away == distance)
                     def _(source=source):
@@ -344,22 +348,29 @@
 
     def exchange(values, received, part):
         part_p, part_f = swap_core(part), swap_far(part)
-        to_p, to_c, to_f = run(
-            functools.partial(pick_kernel, per_column),
-            (*codes, after(values, part), *received),
-            [rows_b] * 3,
-            "pick_requested",
-        )
-        from_p, from_f = swap_core(to_p), swap_far(to_f)
+        values = after(values, part)
+        code_p, code_c, code_f = codes
+
+        def pick(*asked):
+            return run(
+                functools.partial(pick_kernel, per_column),
+                (*asked, values, *received),
+                [rows_b] * len(asked),
+                "pick_requested",
+            )
+
+        to_f, to_p = pick(code_f, code_p)
+        from_f, from_p = swap_far(to_f), swap_core(to_p)
         own, *parts = run(
             functools.partial(merge_kernel, per_column),
-            (*codes, part_p, after(part, to_c), part_f),
+            (*codes, part_p, after(part, to_f), part_f),
             [struct((blocks, width, points), F32)] + [own_t] * 3,
             "merge_partials",
             scratch=[pltpu.VMEM((per_column, width, points), F32)],
         )
         scattered = (own, *(swap_grp(parts[bits - 1], bits) for bits in (1, 2, 3)))
-        return (from_p, after(to_c, own), from_f), scattered
+        (to_c,) = pick(after(code_c, own))
+        return (from_p, to_c, from_f), scattered
 
     line = pltpu.VMEM((width, slots * points), BF16)
 
@@ -396,9 +407,9 @@
     to_second, grad_direct = run(
         back_near_kernel,
         (code, upstream_t, kernel_weights, near_store, influence),
-        [rows_t, struct((width, flat), F32)],
+        [rows_t, struct((kernels, width, width), F32)],
         "back_to_second",
-        [pltpu.VMEM((blocks, width, kernels * points), BF16)],
+        [pltpu.VMEM((blocks, width, kernels * points), BF16), pltpu.VMEM((width, flat), F32)],
         2 * pair_flops,
     )
     near_upstream, scattered = exchange(upstream, received, to_second)
@@ -415,18 +426,20 @@
     )
 
     got = swap_core(send)
-    total = run(to_first_kernel, (code, z_store, mirrored_t), total_b, "to_first", size=0)
     own, *parts = run(
         split_kernel,
-        (keep, after(got, total)),
+        (keep, got),
         [struct(piece, F32)] + [struct(piece, BF16)] * 3,
         "split_half",
     )
+    total = run(
+        to_first_kernel, (after(code, own), z_store, mirrored_t), total_b, "to_first", size=0
+    )
     grad_features = run(
         finish_kernel, (point_counts, total, *scattered), own_b, "finish_features"
     )
     got = [swap_grp(after(part, *scattered), bits) for bits, part in enumerate(parts, 1)]
-    summed = run(add_kernel, (own, *got), struct(piece, BF16), "add_quarters")
+    summed = run(add_kernel, (after(own, total), *got), struct(piece, BF16), "add_quarters")
     everywhere = lax.axis_size("block") * regions * blocks * points
     for stride, scale in ((2, 1.0), (8, 1.0 / math.sqrt(everywhere))):
         got = [swap(summed, "block", lambda i, n=stride * b: i ^ n) for b in (1, 2, 3)]

time: 128 us -> 128 us (level)
  waiting for transfers between devices: 18.1 us -> 15.8 us
  Pallas kernels: 41.2 us -> 42.7 us
    ppermute x36, waiting for transfers between devices: 18.1 us -> 15.8 us  [swap(): lax.ppermute(x, axis, [(i, partner(i)) for i in peers if partner(i) in pe...]
    pallas_call x17 -> x19, Pallas kernels: 41.2 us -> 42.7 us  [run(): pl.pallas_call(kernel, in_specs=[hbm if i in outside else smem if a.dtype...]
  transfers between devices with their start and end apart: 36 -> 36, of which waited for: 12 -> 11; matrix products, arithmetic and copies ran while one was open for 1% -> 1% of each run, Pallas kernels for 30% -> 31%
where the time goes in v6:
time: 128 us
  starting transfers between devices  64.5 us (50%)
  Pallas kernels  42.7 us (33%)
  waiting for transfers between devices  15.8 us (12%)
  other arithmetic  1.87 us (1%)
  between operations  1.69 us (1%)
    ppermute x36, starting transfers between devices, swap(): lax.ppermute(x, axis, [(i, partner(i)) for i in peers if partner(i) in pe...  64.5 us
    pallas_call x19, Pallas kernels, run(): pl.pallas_call(kernel, in_specs=[hbm if i in outside else smem if a.dtype...  42.7 us
    ppermute x36, waiting for transfers between devices, swap(): lax.ppermute(x, axis, [(i, partner(i)) for i in peers if partner(i) in pe...  15.8 us
  transfers between devices with their start and end apart: 36, of which 11 were waited for; matrix products, arithmetic and copies ran while one was open for 1% of the time, Pallas kernels for 31%

profile of v6, /device:TPU:1, one launch (start us, length us, event | category | flops | bytes accessed | tf_op | source)
XLA Modules:
  0.0 127.5 jit_solution(8383250865321361849)
XLA Ops:
  1.7 3.6 %collective-permute-start.4 = (bf16[4,256,128]{2,1,0:T(8,128)(2,1)S(1)}, bf16[4,256,128]{2,1,0:T(8,128)(2,1)S(1)}, u32[]{:S(2)}, u32[]{:S(2)}) collective-permute-start(bf16[4,256,128]{2,1,0:T(8,128)(2,1)S(1)} %fusion.m_ref.refs_2_.refs_1_), channel_id=1, source_target_pairs={{0,3},{1,2},{2,1},{3,0},{4,7},{5,6},{6,5},{7,4},{8,11},{9,10},{10,... | collective-permute-start | bytes 786440 | tf_op jit(solution)/shard_map/ppermute | solution.py:308
  8.8 3.1 %collective-permute-start = (s32[8]{0:T(128)S(1)}, s32[8]{0:T(128)S(1)}, u32[]{:S(2)}, u32[]{:S(2)}) collective-permute-start(s32[8]{0:T(128)S(1)} %compare_select_fusion.code.code_c.refs_0_), channel_id=1, source_target_pairs={{4,8},{8,4},{12,16},{16,12},{20,24},{24,20},{28,32},{32,28},{36,40... | collective-permute-start | bytes 104 | tf_op jit(solution)/shard_map/ppermute | solution.py:308
  12.9 6.6 %own_to_second.1 = (bf16[8,128,256]{2,1,0:T(8,128)(2,1)S(1)}, bf16[4,128,256]{2,1,0:T(8,128)(2,1)S(1)}, bf16[15,128,128]{2,1,0:T(8,128)(2,1)S(1)}, bf16[8,15,256,256]{3,2,1,0:T(8,128)(2,1)S(1)}) custom-call(s32[8]{0:T(128)S(1)} %compare_select_fusion.code.code_c.refs_0_, bf16[4,256,128]{2,1,0:T(8,128)(2,1)S(1)} %fusion.m_ref.refs_2_.refs_1_, ...), custom_call_target="tpu_custom_call" | custom-call | flops 2013265920 | bytes 33488928 | tf_op jit(solution)/shard_map/own_to_second/pallas_call | solution.py:32
  19.5 1.9 %collective-permute-start.7 = (bf16[8,128,256]{2,1,0:T(8,128)(2,1)S(1)}, bf16[8,128,256]{2,1,0:T(8,128)(2,1)S(1)}, u32[]{:S(2)}, u32[]{:S(2)}) collective-permute-start(bf16[8,128,256]{2,1,0:T(8,128)(2,1)S(1)} %get-tuple-element.49.part_c), channel_id=1, source_target_pairs={{4,8},{8,4},{12,16},{16,12},{20,24},{24,20},{28,32},{32,28},{36,40... | collective-permute-start | bytes 1572872 | tf_op jit(solution)/shard_map/ppermute | solution.py:308
  23.1 3.8 %collective-permute-start.8 = (bf16[8,256,128]{2,1,0:T(8,128)(2,1)S(1)}, bf16[8,256,128]{2,1,0:T(8,128)(2,1)S(1)}, u32[]{:S(2)}, u32[]{:S(2)}) collective-permute-start(bf16[8,256,128]{2,1,0:T(8,128)(2,1)S(1)} %get-tuple-element.48), channel_id=1, source_target_pairs={{4,8},{8,4},{12,16},{16,12},{20,24},{24,20},{28,32},{32,28},{36,40... | collective-permute-start | bytes 1572872 | tf_op jit(solution)/shard_map/ppermute | solution.py:308
  26.8 3.5 %collective-permute-done.7.part_f = bf16[8,128,256]{2,1,0:T(8,128)(2,1)S(1)} collective-permute-done((bf16[8,128,256]{2,1,0:T(8,128)(2,1)S(1)}, bf16[8,128,256]{2,1,0:T(8,128)(2,1)S(1)}, u32[]{:S(2)}, u32[]{:S(2)}) %collective-permute-start.7) | collective-permute-done | bytes 524320 | tf_op jit(solution)/shard_map/ppermute | solution.py:308
  32.0 2.8 %collective-permute-start.10 = (bf16[4,128,256]{2,1,0:T(8,128)(2,1)S(1)}, bf16[4,128,256]{2,1,0:T(8,128)(2,1)S(1)}, u32[]{:S(2)}, u32[]{:S(2)}) collective-permute-start(bf16[4,128,256]{2,1,0:T(8,128)(2,1)S(1)} %get-tuple-element.55), channel_id=1, source_target_pairs={{0,2},{1,3},{2,0},{3,1},{4,6},{5,7},{6,4},{7,5},{8,10},{9,11},{10,... | collective-permute-start | bytes 786440 | tf_op jit(solution)/shard_map/ppermute | solution.py:308
  36.5 8.2 %near_to_first.1 = (f32[4,256,128]{2,1,0:T(8,128)S(1)}, bf16[8,256,1920]{2,1,0:T(8,128)(2,1)S(1)}) custom-call(s32[8]{0:T(128)S(1)} %compare_select_fusion.code.code_c.refs_0_, bf16[8,256,128]{2,1,0:T(8,128)(2,1)S(1)} %collective-permute-done.5.chip_ref, bf16[8,256,128]{2,1,0:T(8,128)(2,1)S(1)} %pick_requested.5.here_ref, ...), custom_call_target="tpu_custom_call" | custom-call | flops 4026531840 | bytes 26181664 | tf_op jit(solution)/shard_map/near_to_first/pallas_call | solution.py:32
  44.7 1.7 %activate.1 = (bf16[4,256,128]{2,1,0:T(8,128)(2,1)}, bf16[4,256,128]{2,1,0:T(8,128)(2,1)S(1)}, bf16[4,128,256]{2,1,0:T(8,128)(2,1)S(1)}) custom-call(s32[4]{0:T(128)S(1)} %copy-done.2, f32[4,256,128]{2,1,0:T(8,128)S(1)} %get-tuple-element.53.total, f32[4,128,256]{2,1,0:T(8,128)S(1)} %get-tuple-element.50.own, ...), custom_call_target="tpu_custom_call" | custom-call | bytes 2883600 | tf_op jit(solution)/shard_map/activate/pallas_call | solution.py:32
  46.6 2.2 %collective-permute-start.13 = (bf16[4,256,128]{2,1,0:T(8,128)(2,1)S(1)}, bf16[4,256,128]{2,1,0:T(8,128)(2,1)S(1)}, u32[]{:S(2)}, u32[]{:S(2)}) collective-permute-start(bf16[4,256,128]{2,1,0:T(8,128)(2,1)S(1)} %get-tuple-element.62.refs_2_.refs_1_), channel_id=1, source_target_pairs={{0,2},{1,3},{2,0},{3,1},{4,6},{5,7},{6,4},{7,5},{8,10},{9,11},{10,... | collective-permute-start | bytes 786440 | tf_op jit(solution)/shard_map/ppermute | solution.py:308
  49.7 7.0 %back_to_second.1 = (bf16[8,128,256]{2,1,0:T(8,128)(2,1)S(1)}, f32[15,128,128]{2,1,0:T(8,128)S(1)}) custom-call(s32[8]{0:T(128)S(1)} %compare_select_fusion.code.code_c.refs_0_, bf16[4,128,256]{2,1,0:T(8,128)(2,1)S(1)} %get-tuple-element.59.ut_ref, bf16[15,128,128]{2,1,0:T(8,128)(2,1)S(1)} %copy-done, bf16[8,256,1920]{2,1,0:T(8,128)(2,1)S(1)} %get-tuple-element.60.near_ref, ...), custom_call_target="tpu_custom_call" | custom-call | flops 4026531840 | bytes 25853984 | tf_op jit(solution)/shard_map/back_to_second/pallas_call | solution.py:32
  56.7 5.9 %collective-permute-start.17 = (bf16[8,128,256]{2,1,0:T(8,128)(2,1)S(1)}, bf16[8,128,256]{2,1,0:T(8,128)(2,1)S(1)}, u32[]{:S(2)}, u32[]{:S(2)}) collective-permute-start(bf16[8,128,256]{2,1,0:T(8,128)(2,1)S(1)} %get-tuple-element.65.part_c), channel_id=1, source_target_pairs={{4,8},{8,4},{12,16},{16,12},{20,24},{24,20},{28,32},{32,28},{36,40... | collective-permute-start | bytes 1572872 | tf_op jit(solution)/shard_map/ppermute | solution.py:308
  64.4 6.0 %collective-permute-start.18 = (bf16[8,256,128]{2,1,0:T(8,128)(2,1)S(1)}, bf16[8,256,128]{2,1,0:T(8,128)(2,1)S(1)}, u32[]{:S(2)}, u32[]{:S(2)}) collective-permute-start(bf16[8,256,128]{2,1,0:T(8,128)(2,1)S(1)} %get-tuple-element.64), channel_id=1, source_target_pairs={{4,8},{8,4},{12,16},{16,12},{20,24},{24,20},{28,32},{32,28},{36,40... | collective-permute-start | bytes 1572872 | tf_op jit(solution)/shard_map/ppermute | solution.py:308
  71.8 1.6 %collective-permute-start.20 = (bf16[4,128,256]{2,1,0:T(8,128)(2,1)S(1)}, bf16[4,128,256]{2,1,0:T(8,128)(2,1)S(1)}, u32[]{:S(2)}, u32[]{:S(2)}) collective-permute-start(bf16[4,128,256]{2,1,0:T(8,128)(2,1)S(1)} %get-tuple-element.76), channel_id=1, source_target_pairs={{0,1},{1,0},{2,3},{3,2},{4,5},{5,4},{6,7},{7,6},{8,9},{9,8},{10,11... | collective-permute-start | bytes 786440 | tf_op jit(solution)/shard_map/ppermute | solution.py:308
  73.4 2.0 %collective-permute-start.21 = (bf16[4,128,256]{2,1,0:T(8,128)(2,1)S(1)}, bf16[4,128,256]{2,1,0:T(8,128)(2,1)S(1)}, u32[]{:S(2)}, u32[]{:S(2)}) collective-permute-start(bf16[4,128,256]{2,1,0:T(8,128)(2,1)S(1)} %get-tuple-element.77), channel_id=1, source_target_pairs={{0,2},{1,3},{2,0},{3,1},{4,6},{5,7},{6,4},{7,5},{8,10},{9,11},{10,... | collective-permute-start | bytes 786440 | tf_op jit(solution)/shard_map/ppermute | solution.py:308
  77.5 7.3 %back_to_first.1 = (bf16[8,256,1920]{2,1,0:T(8,128)(2,1)S(1)}, f32[15,64,128]{2,1,0:T(8,128)S(1)}, bf16[15,64,128]{2,1,0:T(8,128)(2,1)S(1)}) custom-call(s32[8]{0:T(128)S(1)} %compare_select_fusion.code.code_c.refs_0_, bf16[8,256,128]{2,1,0:T(8,128)(2,1)S(1)} %collective-permute-done.15.chip_ref, bf16[8,256,128]{2,1,0:T(8,128)(2,1)S(1)} %pick_requested.7.here_ref, ...), custom_call_target="tpu_custom_call" | custom-call | tf_op jit(solution)/shard_map/back_to_first/pallas_call | solution.py:32
  88.1 1.8 %collective-permute-start.23 = (bf16[15,16,128]{2,1,0:T(8,128)(2,1)S(1)}, bf16[15,16,128]{2,1,0:T(8,128)(2,1)S(1)}, u32[]{:S(2)}, u32[]{:S(2)}) collective-permute-start(bf16[15,16,128]{2,1,0:T(8,128)(2,1)S(1)} %get-tuple-element.81), channel_id=1, source_target_pairs={{0,1},{1,0},{2,3},{3,2},{4,5},{5,4},{6,7},{7,6},{8,9},{9,8},{10,11... | collective-permute-start | bytes 184328 | tf_op jit(solution)/shard_map/ppermute | solution.py:308
  89.9 2.8 %to_first.1.total = f32[4,256,128]{2,1,0:T(8,128)S(1)} custom-call(s32[8]{0:T(128)S(1)} %compare_select_fusion.code.code_c.refs_0_, bf16[8,256,1920]{2,1,0:T(8,128)(2,1)S(1)} %get-tuple-element.74.z_ref, bf16[15,128,128]{2,1,0:T(8,128)(2,1)S(1)} %get-tuple-element.75.wmt_ref), custom_call_target="tpu_custom_call" | custom-call | tf_op jit(solution)/shard_map/to_first/pallas_call | solution.py:32
  92.9 8.0 %collective-permute-start.28 = (bf16[15,16,128]{2,1,0:T(8,128)(2,1)S(1)}, bf16[15,16,128]{2,1,0:T(8,128)(2,1)S(1)}, u32[]{:S(2)}, u32[]{:S(2)}) collective-permute-start(bf16[15,16,128]{2,1,0:T(8,128)(2,1)S(1)} %add_quarters.1.own), channel_id=1, source_target_pairs={{0,24},{4,28},{8,16},{12,20},{16,8},{20,12},{24,0},{28,4},{32,56},... | collective-permute-start | bytes 184328 | tf_op jit(solution)/shard_map/ppermute | solution.py:308
  103.1 2.4 %collective-permute-done.27.two = bf16[15,16,128]{2,1,0:T(8,128)(2,1)S(1)} collective-permute-done((bf16[15,16,128]{2,1,0:T(8,128)(2,1)S(1)}, bf16[15,16,128]{2,1,0:T(8,128)(2,1)S(1)}, u32[]{:S(2)}, u32[]{:S(2)}) %collective-permute-start.27) | collective-permute-done | bytes 61472 | tf_op jit(solution)/shard_map/ppermute | solution.py:308
  107.0 2.8 %collective-permute-start.30 = (bf16[15,16,128]{2,1,0:T(8,128)(2,1)S(1)}, bf16[15,16,128]{2,1,0:T(8,128)(2,1)S(1)}, u32[]{:S(2)}, u32[]{:S(2)}) collective-permute-start(bf16[15,16,128]{2,1,0:T(8,128)(2,1)S(1)} %add_in_order.2.own), channel_id=1, source_target_pairs={{0,64},{4,68},{8,72},{12,76},{16,80},{20,84},{24,88},{28,92},{32,9... | collective-permute-start | bytes 184328 | tf_op jit(solution)/shard_map/ppermute | solution.py:308
  113.0 1.8 %collective-permute-start.34 = (bf16[15,16,128]{2,1,0:T(8,128)(2,1)S(1)}, bf16[15,16,128]{2,1,0:T(8,128)(2,1)S(1)}, u32[]{:S(2)}, u32[]{:S(2)}) collective-permute-start(bf16[15,16,128]{2,1,0:T(8,128)(2,1)S(1)} %add_in_order.3.own), channel_id=1, source_target_pairs={{0,3},{1,2},{2,1},{3,0},{4,7},{5,6},{6,5},{7,4},{8,11},{9,10},{10,... | collective-permute-start | bytes 184328 | tf_op jit(solution)/shard_map/ppermute | solution.py:308
  117.3 2.0 %collective-permute-done.33.two = bf16[15,16,128]{2,1,0:T(8,128)(2,1)S(1)} collective-permute-done((bf16[15,16,128]{2,1,0:T(8,128)(2,1)S(1)}, bf16[15,16,128]{2,1,0:T(8,128)(2,1)S(1)}, u32[]{:S(2)}, u32[]{:S(2)}) %collective-permute-start.33) | collective-permute-done | bytes 61472 | tf_op jit(solution)/shard_map/ppermute | solution.py:308
  119.4 5.9 %collective-permute-start.35 = (bf16[15,64,128]{2,1,0:T(8,128)(2,1)S(1)}, bf16[15,64,128]{2,1,0:T(8,128)(2,1)S(1)}, u32[]{:S(2)}, u32[]{:S(2)}) collective-permute-start(bf16[15,64,128]{2,1,0:T(8,128)(2,1)S(1)} %join_quarters.1.own), channel_id=1, source_target_pairs={{0,4},{4,0},{8,12},{12,8},{16,20},{20,16},{24,28},{28,24},{32,36},... | collective-permute-start | bytes 737288 | tf_op jit(solution)/shard_map/ppermute | solution.py:308
  (75 shorter events, 30.9 us)
Async XLA Ops:
  1.7 19.8 %collective-permute-start.4 = (bf16[4,256,128]{2,1,0:T(8,128)(2,1)S(1)}, bf16[4,256,128]{2,1,0:T(8,128)(2,1)S(1)}, u32[]{:S(2)}, u32[]{:S(2)}) collective-permute-start(bf16[4,256,128]{2,1,0:T(8,128)(2,1)S(1)} %fusion.m_ref.refs_2_.refs_1_), channel_id=1, source_target_pairs={{0,3},{1,2},{2,1},{3,0},{4,7},{5,6},{6,5},{7,4},{8,11},{9,10},{10,... | collective-permute-start | bytes 786440 | tf_op jit(solution)/shard_map/ppermute | solution.py:308
  5.4 16.2 %collective-permute-start.3 = (bf16[4,256,128]{2,1,0:T(8,128)(2,1)S(1)}, bf16[4,256,128]{2,1,0:T(8,128)(2,1)S(1)}, u32[]{:S(2)}, u32[]{:S(2)}) collective-permute-start(bf16[4,256,128]{2,1,0:T(8,128)(2,1)S(1)} %fusion.m_ref.refs_2_.refs_1_), channel_id=1, source_target_pairs={{0,2},{1,3},{2,0},{3,1},{4,6},{5,7},{6,4},{7,5},{8,10},{9,11},{10,... | collective-permute-start | bytes 786440 | tf_op jit(solution)/shard_map/ppermute | solution.py:308
  5.7 15.8 %collective-permute-start.2 = (bf16[4,256,128]{2,1,0:T(8,128)(2,1)S(1)}, bf16[4,256,128]{2,1,0:T(8,128)(2,1)S(1)}, u32[]{:S(2)}, u32[]{:S(2)}) collective-permute-start(bf16[4,256,128]{2,1,0:T(8,128)(2,1)S(1)} %fusion.m_ref.refs_2_.refs_1_), channel_id=1, source_target_pairs={{0,1},{1,0},{2,3},{3,2},{4,5},{5,4},{6,7},{7,6},{8,9},{9,8},{10,11... | collective-permute-start | bytes 786440 | tf_op jit(solution)/shard_map/ppermute | solution.py:308
  7.5 12.0 %collective-permute-start.1 = (s32[8]{0:T(128)S(1)}, s32[8]{0:T(128)S(1)}, u32[]{:S(2)}, u32[]{:S(2)}) collective-permute-start(s32[8]{0:T(128)S(1)} %compare_select_fusion.code.code_c.refs_0_), channel_id=1, source_target_pairs={{0,4},{4,0},{8,12},{12,8},{16,20},{20,16},{24,28},{28,24},{32,36},... | collective-permute-start | bytes 104 | tf_op jit(solution)/shard_map/ppermute | solution.py:308
  8.8 12.7 %collective-permute-start = (s32[8]{0:T(128)S(1)}, s32[8]{0:T(128)S(1)}, u32[]{:S(2)}, u32[]{:S(2)}) collective-permute-start(s32[8]{0:T(128)S(1)} %compare_select_fusion.code.code_c.refs_0_), channel_id=1, source_target_pairs={{4,8},{8,4},{12,16},{16,12},{20,24},{24,20},{28,32},{32,28},{36,40... | collective-permute-start | bytes 104 | tf_op jit(solution)/shard_map/ppermute | solution.py:308
  19.5 10.8 %collective-permute-start.7 = (bf16[8,128,256]{2,1,0:T(8,128)(2,1)S(1)}, bf16[8,128,256]{2,1,0:T(8,128)(2,1)S(1)}, u32[]{:S(2)}, u32[]{:S(2)}) collective-permute-start(bf16[8,128,256]{2,1,0:T(8,128)(2,1)S(1)} %get-tuple-element.49.part_c), channel_id=1, source_target_pairs={{4,8},{8,4},{12,16},{16,12},{20,24},{24,20},{28,32},{32,28},{36,40... | collective-permute-start | bytes 1572872 | tf_op jit(solution)/shard_map/ppermute | solution.py:308
  21.5 8.9 %collective-permute-start.6 = (bf16[8,128,256]{2,1,0:T(8,128)(2,1)S(1)}, bf16[8,128,256]{2,1,0:T(8,128)(2,1)S(1)}, u32[]{:S(2)}, u32[]{:S(2)}) collective-permute-start(bf16[8,128,256]{2,1,0:T(8,128)(2,1)S(1)} %get-tuple-element.49.part_c), channel_id=1, source_target_pairs={{0,4},{4,0},{8,12},{12,8},{16,20},{20,16},{24,28},{28,24},{32,36},... | collective-permute-start | bytes 1572872 | tf_op jit(solution)/shard_map/ppermute | solution.py:308
  22.6 13.9 %collective-permute-start.5 = (bf16[8,256,128]{2,1,0:T(8,128)(2,1)S(1)}, bf16[8,256,128]{2,1,0:T(8,128)(2,1)S(1)}, u32[]{:S(2)}, u32[]{:S(2)}) collective-permute-start(bf16[8,256,128]{2,1,0:T(8,128)(2,1)S(1)} %get-tuple-element.47), channel_id=1, source_target_pairs={{0,4},{4,0},{8,12},{12,8},{16,20},{20,16},{24,28},{28,24},{32,36},... | collective-permute-start | bytes 1572872 | tf_op jit(solution)/shard_map/ppermute | solution.py:308
  23.1 13.4 %collective-permute-start.8 = (bf16[8,256,128]{2,1,0:T(8,128)(2,1)S(1)}, bf16[8,256,128]{2,1,0:T(8,128)(2,1)S(1)}, u32[]{:S(2)}, u32[]{:S(2)}) collective-permute-start(bf16[8,256,128]{2,1,0:T(8,128)(2,1)S(1)} %get-tuple-element.48), channel_id=1, source_target_pairs={{4,8},{8,4},{12,16},{16,12},{20,24},{24,20},{28,32},{32,28},{36,40... | collective-permute-start | bytes 1572872 | tf_op jit(solution)/shard_map/ppermute | solution.py:308
  31.7 13.0 %collective-permute-start.9 = (bf16[4,128,256]{2,1,0:T(8,128)(2,1)S(1)}, bf16[4,128,256]{2,1,0:T(8,128)(2,1)S(1)}, u32[]{:S(2)}, u32[]{:S(2)}) collective-permute-start(bf16[4,128,256]{2,1,0:T(8,128)(2,1)S(1)} %get-tuple-element.54), channel_id=1, source_target_pairs={{0,1},{1,0},{2,3},{3,2},{4,5},{5,4},{6,7},{7,6},{8,9},{9,8},{10,11... | collective-permute-start | bytes 786440 | tf_op jit(solution)/shard_map/ppermute | solution.py:308
  32.0 12.7 %collective-permute-start.10 = (bf16[4,128,256]{2,1,0:T(8,128)(2,1)S(1)}, bf16[4,128,256]{2,1,0:T(8,128)(2,1)S(1)}, u32[]{:S(2)}, u32[]{:S(2)}) collective-permute-start(bf16[4,128,256]{2,1,0:T(8,128)(2,1)S(1)} %get-tuple-element.55), channel_id=1, source_target_pairs={{0,2},{1,3},{2,0},{3,1},{4,6},{5,7},{6,4},{7,5},{8,10},{9,11},{10,... | collective-permute-start | bytes 786440 | tf_op jit(solution)/shard_map/ppermute | solution.py:308
  34.8 9.9 %collective-permute-start.11 = (bf16[4,128,256]{2,1,0:T(8,128)(2,1)S(1)}, bf16[4,128,256]{2,1,0:T(8,128)(2,1)S(1)}, u32[]{:S(2)}, u32[]{:S(2)}) collective-permute-start(bf16[4,128,256]{2,1,0:T(8,128)(2,1)S(1)} %get-tuple-element.56), channel_id=1, source_target_pairs={{0,3},{1,2},{2,1},{3,0},{4,7},{5,6},{6,5},{7,4},{8,11},{9,10},{10,... | collective-permute-start | bytes 786440 | tf_op jit(solution)/shard_map/ppermute | solution.py:308
  46.5 16.2 %collective-permute-start.14 = (bf16[4,256,128]{2,1,0:T(8,128)(2,1)S(1)}, bf16[4,256,128]{2,1,0:T(8,128)(2,1)S(1)}, u32[]{:S(2)}, u32[]{:S(2)}) collective-permute-start(bf16[4,256,128]{2,1,0:T(8,128)(2,1)S(1)} %get-tuple-element.62.refs_2_.refs_1_), channel_id=1, source_target_pairs={{0,3},{1,2},{2,1},{3,0},{4,7},{5,6},{6,5},{7,4},{8,11},{9,10},{10,... | collective-permute-start | bytes 786440 | tf_op jit(solution)/shard_map/ppermute | solution.py:308
  46.6 16.1 %collective-permute-start.13 = (bf16[4,256,128]{2,1,0:T(8,128)(2,1)S(1)}, bf16[4,256,128]{2,1,0:T(8,128)(2,1)S(1)}, u32[]{:S(2)}, u32[]{:S(2)}) collective-permute-start(bf16[4,256,128]{2,1,0:T(8,128)(2,1)S(1)} %get-tuple-element.62.refs_2_.refs_1_), channel_id=1, source_target_pairs={{0,2},{1,3},{2,0},{3,1},{4,6},{5,7},{6,4},{7,5},{8,10},{9,11},{10,... | collective-permute-start | bytes 786440 | tf_op jit(solution)/shard_map/ppermute | solution.py:308
  48.9 13.9 %collective-permute-start.12 = (bf16[4,256,128]{2,1,0:T(8,128)(2,1)S(1)}, bf16[4,256,128]{2,1,0:T(8,128)(2,1)S(1)}, u32[]{:S(2)}, u32[]{:S(2)}) collective-permute-start(bf16[4,256,128]{2,1,0:T(8,128)(2,1)S(1)} %get-tuple-element.62.refs_2_.refs_1_), channel_id=1, source_target_pairs={{0,1},{1,0},{2,3},{3,2},{4,5},{5,4},{6,7},{7,6},{8,9},{9,8},{10,11... | collective-permute-start | bytes 786440 | tf_op jit(solution)/shard_map/ppermute | solution.py:308
  56.7 13.7 %collective-permute-start.17 = (bf16[8,128,256]{2,1,0:T(8,128)(2,1)S(1)}, bf16[8,128,256]{2,1,0:T(8,128)(2,1)S(1)}, u32[]{:S(2)}, u32[]{:S(2)}) collective-permute-start(bf16[8,128,256]{2,1,0:T(8,128)(2,1)S(1)} %get-tuple-element.65.part_c), channel_id=1, source_target_pairs={{4,8},{8,4},{12,16},{16,12},{20,24},{24,20},{28,32},{32,28},{36,40... | collective-permute-start | bytes 1572872 | tf_op jit(solution)/shard_map/ppermute | solution.py:308
  62.6 7.8 %collective-permute-start.16 = (bf16[8,128,256]{2,1,0:T(8,128)(2,1)S(1)}, bf16[8,128,256]{2,1,0:T(8,128)(2,1)S(1)}, u32[]{:S(2)}, u32[]{:S(2)}) collective-permute-start(bf16[8,128,256]{2,1,0:T(8,128)(2,1)S(1)} %get-tuple-element.65.part_c), channel_id=1, source_target_pairs={{0,4},{4,0},{8,12},{12,8},{16,20},{20,16},{24,28},{28,24},{32,36},... | collective-permute-start | bytes 1572872 | tf_op jit(solution)/shard_map/ppermute | solution.py:308
  63.7 13.0 %collective-permute-start.15 = (bf16[8,256,128]{2,1,0:T(8,128)(2,1)S(1)}, bf16[8,256,128]{2,1,0:T(8,128)(2,1)S(1)}, u32[]{:S(2)}, u32[]{:S(2)}) collective-permute-start(bf16[8,256,128]{2,1,0:T(8,128)(2,1)S(1)} %get-tuple-element.63), channel_id=1, source_target_pairs={{0,4},{4,0},{8,12},{12,8},{16,20},{20,16},{24,28},{28,24},{32,36},... | collective-permute-start | bytes 1572872 | tf_op jit(solution)/shard_map/ppermute | solution.py:308
  64.4 13.1 %collective-permute-start.18 = (bf16[8,256,128]{2,1,0:T(8,128)(2,1)S(1)}, bf16[8,256,128]{2,1,0:T(8,128)(2,1)S(1)}, u32[]{:S(2)}, u32[]{:S(2)}) collective-permute-start(bf16[8,256,128]{2,1,0:T(8,128)(2,1)S(1)} %get-tuple-element.64), channel_id=1, source_target_pairs={{4,8},{8,4},{12,16},{16,12},{20,24},{24,20},{28,32},{32,28},{36,40... | collective-permute-start | bytes 1572872 | tf_op jit(solution)/shard_map/ppermute | solution.py:308
  71.8 14.8 %collective-permute-start.20 = (bf16[4,128,256]{2,1,0:T(8,128)(2,1)S(1)}, bf16[4,128,256]{2,1,0:T(8,128)(2,1)S(1)}, u32[]{:S(2)}, u32[]{:S(2)}) collective-permute-start(bf16[4,128,256]{2,1,0:T(8,128)(2,1)S(1)} %get-tuple-element.76), channel_id=1, source_target_pairs={{0,1},{1,0},{2,3},{3,2},{4,5},{5,4},{6,7},{7,6},{8,9},{9,8},{10,11... | collective-permute-start | bytes 786440 | tf_op jit(solution)/shard_map/ppermute | solution.py:308
  73.4 13.1 %collective-permute-start.21 = (bf16[4,128,256]{2,1,0:T(8,128)(2,1)S(1)}, bf16[4,128,256]{2,1,0:T(8,128)(2,1)S(1)}, u32[]{:S(2)}, u32[]{:S(2)}) collective-permute-start(bf16[4,128,256]{2,1,0:T(8,128)(2,1)S(1)} %get-tuple-element.77), channel_id=1, source_target_pairs={{0,2},{1,3},{2,0},{3,1},{4,6},{5,7},{6,4},{7,5},{8,10},{9,11},{10,... | collective-permute-start | bytes 786440 | tf_op jit(solution)/shard_map/ppermute | solution.py:308
  75.4 11.1 %collective-permute-start.22 = (bf16[4,128,256]{2,1,0:T(8,128)(2,1)S(1)}, bf16[4,128,256]{2,1,0:T(8,128)(2,1)S(1)}, u32[]{:S(2)}, u32[]{:S(2)}) collective-permute-start(bf16[4,128,256]{2,1,0:T(8,128)(2,1)S(1)} %get-tuple-element.78), channel_id=1, source_target_pairs={{0,3},{1,2},{2,1},{3,0},{4,7},{5,6},{6,5},{7,4},{8,11},{9,10},{10,... | collective-permute-start | bytes 786440 | tf_op jit(solution)/shard_map/ppermute | solution.py:308
  92.9 10.1 %collective-permute-start.28 = (bf16[15,16,128]{2,1,0:T(8,128)(2,1)S(1)}, bf16[15,16,128]{2,1,0:T(8,128)(2,1)S(1)}, u32[]{:S(2)}, u32[]{:S(2)}) collective-permute-start(bf16[15,16,128]{2,1,0:T(8,128)(2,1)S(1)} %add_quarters.1.own), channel_id=1, source_target_pairs={{0,24},{4,28},{8,16},{12,20},{16,8},{20,12},{24,0},{28,4},{32,56},... | collective-permute-start | bytes 184328 | tf_op jit(solution)/shard_map/ppermute | solution.py:308
  119.4 7.1 %collective-permute-start.35 = (bf16[15,64,128]{2,1,0:T(8,128)(2,1)S(1)}, bf16[15,64,128]{2,1,0:T(8,128)(2,1)S(1)}, u32[]{:S(2)}, u32[]{:S(2)}) collective-permute-start(bf16[15,64,128]{2,1,0:T(8,128)(2,1)S(1)} %join_quarters.1.own), channel_id=1, source_target_pairs={{0,4},{4,0},{8,12},{12,8},{16,20},{20,16},{24,28},{28,24},{32,36},... | collective-permute-start | bytes 737288 | tf_op jit(solution)/shard_map/ppermute | solution.py:308
  (15 other events, 123.0 us)

commit v7 on v6

--- a/solution.py
+++ b/solution.py
@@ -361,16 +361,16 @@
 
         to_f, to_p = pick(code_f, code_p)
         from_f, from_p = swap_far(to_f), swap_core(to_p)
+        (to_c,) = pick(after(code_c, to_f))
         own, *parts = run(
             functools.partial(merge_kernel, per_column),
-            (*codes, part_p, after(part, to_f), part_f),
+            (*codes, part_p, after(part, to_c), part_f),
             [struct((blocks, width, points), F32)] + [own_t] * 3,
             "merge_partials",
             scratch=[pltpu.VMEM((per_column, width, points), F32)],
         )
         scattered = (own, *(swap_grp(parts[bits - 1], bits) for bits in (1, 2, 3)))
-        (to_c,) = pick(after(code_c, own))
-        return (from_p, to_c, from_f), scattered
+        return (from_p, after(to_c, own), from_f), scattered
 
     line = pltpu.VMEM((width, slots * points), BF16)
 

time: 128 us -> 128 us (level)
  Pallas kernels: 42.7 us -> 28.9 us
  waiting for transfers between devices: 15.8 us -> 25.2 us
  starting transfers between devices: 64.5 us -> 69.6 us
    pallas_call x19, Pallas kernels: 42.7 us -> 28.9 us  [run(): pl.pallas_call(kernel, in_specs=[hbm if i in outside else smem if a.dtype...]
    ppermute x36, waiting for transfers between devices: 15.8 us -> 25.2 us  [swap(): lax.ppermute(x, axis, [(i, partner(i)) for i in peers if partner(i) in pe...]
    ppermute x36, starting transfers between devices: 64.5 us -> 69.6 us  [swap(): lax.ppermute(x, axis, [(i, partner(i)) for i in peers if partner(i) in pe...]
  transfers between devices with their start and end apart: 36 -> 36, of which waited for: 11 -> 16; matrix products, arithmetic and copies ran while one was open for 1% -> 1% of each run, Pallas kernels for 31% -> 20%
where the time goes in v7:
time: 128 us
  starting transfers between devices  69.6 us (54%)
  Pallas kernels  28.9 us (23%)
  waiting for transfers between devices  25.2 us (20%)
  other arithmetic  1.87 us (1%)
  between operations  1.6 us (1%)
    ppermute x36, starting transfers between devices, swap(): lax.ppermute(x, axis, [(i, partner(i)) for i in peers if partner(i) in pe...  69.6 us
    pallas_call x19, Pallas kernels, run(): pl.pallas_call(kernel, in_specs=[hbm if i in outside else smem if a.dtype...  28.9 us
    ppermute x36, waiting for transfers between devices, swap(): lax.ppermute(x, axis, [(i, partner(i)) for i in peers if partner(i) in pe...  25.2 us
  transfers between devices with their start and end apart: 36, of which 16 were waited for; matrix products, arithmetic and copies ran while one was open for 1% of the time, Pallas kernels for 20%

profile of v7, /device:TPU:1, one launch (start us, length us, event | category | flops | bytes accessed | tf_op | source)
XLA Modules:
  0.0 128.2 jit_solution(11366314368602925497)
XLA Ops:
  1.7 3.6 %collective-permute-start.4 = (bf16[4,256,128]{2,1,0:T(8,128)(2,1)S(1)}, bf16[4,256,128]{2,1,0:T(8,128)(2,1)S(1)}, u32[]{:S(2)}, u32[]{:S(2)}) collective-permute-start(bf16[4,256,128]{2,1,0:T(8,128)(2,1)S(1)} %fusion.m_ref.refs_2_.refs_1_), channel_id=1, source_target_pairs={{0,3},{1,2},{2,1},{3,0},{4,7},{5,6},{6,5},{7,4},{8,11},{9,10},{10,... | collective-permute-start | bytes 786440 | tf_op jit(solution)/shard_map/ppermute | solution.py:308
  8.8 3.1 %collective-permute-start = (s32[8]{0:T(128)S(1)}, s32[8]{0:T(128)S(1)}, u32[]{:S(2)}, u32[]{:S(2)}) collective-permute-start(s32[8]{0:T(128)S(1)} %compare_select_fusion.code.refs_0_.code_c), channel_id=1, source_target_pairs={{4,8},{8,4},{12,16},{16,12},{20,24},{24,20},{28,32},{32,28},{36,40... | collective-permute-start | bytes 104 | tf_op jit(solution)/shard_map/ppermute | solution.py:308
  12.9 3.9 %own_to_second.1 = (bf16[8,128,256]{2,1,0:T(8,128)(2,1)S(1)}, bf16[4,128,256]{2,1,0:T(8,128)(2,1)S(1)}, bf16[15,128,128]{2,1,0:T(8,128)(2,1)S(1)}, bf16[8,15,256,256]{3,2,1,0:T(8,128)(2,1)S(1)}) custom-call(s32[8]{0:T(128)S(1)} %compare_select_fusion.code.refs_0_.code_c, bf16[4,256,128]{2,1,0:T(8,128)(2,1)S(1)} %fusion.m_ref.refs_2_.refs_1_, ...), custom_call_target="tpu_custom_call" | custom-call | flops 2013265920 | bytes 33488928 | tf_op jit(solution)/shard_map/own_to_second/pallas_call | solution.py:32
  16.8 3.6 %collective-permute-start.7 = (bf16[8,128,256]{2,1,0:T(8,128)(2,1)S(1)}, bf16[8,128,256]{2,1,0:T(8,128)(2,1)S(1)}, u32[]{:S(2)}, u32[]{:S(2)}) collective-permute-start(bf16[8,128,256]{2,1,0:T(8,128)(2,1)S(1)} %get-tuple-element.52.part_c), channel_id=1, source_target_pairs={{4,8},{8,4},{12,16},{16,12},{20,24},{24,20},{28,32},{32,28},{36,40... | collective-permute-start | bytes 1572872 | tf_op jit(solution)/shard_map/ppermute | solution.py:308
  22.0 3.1 %collective-permute-start.8 = (bf16[8,256,128]{2,1,0:T(8,128)(2,1)S(1)}, bf16[8,256,128]{2,1,0:T(8,128)(2,1)S(1)}, u32[]{:S(2)}, u32[]{:S(2)}) collective-permute-start(bf16[8,256,128]{2,1,0:T(8,128)(2,1)S(1)} %get-tuple-element.50), channel_id=1, source_target_pairs={{4,8},{8,4},{12,16},{16,12},{20,24},{24,20},{28,32},{32,28},{36,40... | collective-permute-start | bytes 1572872 | tf_op jit(solution)/shard_map/ppermute | solution.py:308
  28.6 4.4 %collective-permute-start.9 = (bf16[4,128,256]{2,1,0:T(8,128)(2,1)S(1)}, bf16[4,128,256]{2,1,0:T(8,128)(2,1)S(1)}, u32[]{:S(2)}, u32[]{:S(2)}) collective-permute-start(bf16[4,128,256]{2,1,0:T(8,128)(2,1)S(1)} %get-tuple-element.57), channel_id=1, source_target_pairs={{0,1},{1,0},{2,3},{3,2},{4,5},{5,4},{6,7},{7,6},{8,9},{9,8},{10,11... | collective-permute-start | bytes 786440 | tf_op jit(solution)/shard_map/ppermute | solution.py:308
  35.5 3.5 %near_to_first.1 = (f32[4,256,128]{2,1,0:T(8,128)S(1)}, bf16[8,256,1920]{2,1,0:T(8,128)(2,1)S(1)}) custom-call(s32[8]{0:T(128)S(1)} %compare_select_fusion.code.refs_0_.code_c, bf16[8,256,128]{2,1,0:T(8,128)(2,1)S(1)} %collective-permute-done.5.chip_ref, bf16[8,256,128]{2,1,0:T(8,128)(2,1)S(1)} %pick_requested.5.here_ref, ...), custom_call_target="tpu_custom_call" | custom-call | flops 4026531840 | bytes 26181664 | tf_op jit(solution)/shard_map/near_to_first/pallas_call | solution.py:32
  39.0 3.2 %collective-permute-done.10.two = bf16[4,128,256]{2,1,0:T(8,128)(2,1)S(1)} collective-permute-done((bf16[4,128,256]{2,1,0:T(8,128)(2,1)S(1)}, bf16[4,128,256]{2,1,0:T(8,128)(2,1)S(1)}, u32[]{:S(2)}, u32[]{:S(2)}) %collective-permute-start.10) | collective-permute-done | bytes 262176 | tf_op jit(solution)/shard_map/ppermute | solution.py:308
  42.3 2.7 %collective-permute-done.11.three = bf16[4,128,256]{2,1,0:T(8,128)(2,1)S(1)} collective-permute-done((bf16[4,128,256]{2,1,0:T(8,128)(2,1)S(1)}, bf16[4,128,256]{2,1,0:T(8,128)(2,1)S(1)}, u32[]{:S(2)}, u32[]{:S(2)}) %collective-permute-start.11) | collective-permute-done | bytes 262176 | tf_op jit(solution)/shard_map/ppermute | solution.py:308
  46.9 2.1 %collective-permute-start.13 = (bf16[4,256,128]{2,1,0:T(8,128)(2,1)S(1)}, bf16[4,256,128]{2,1,0:T(8,128)(2,1)S(1)}, u32[]{:S(2)}, u32[]{:S(2)}) collective-permute-start(bf16[4,256,128]{2,1,0:T(8,128)(2,1)S(1)} %get-tuple-element.65.refs_2_.refs_1_), channel_id=1, source_target_pairs={{0,2},{1,3},{2,0},{3,1},{4,6},{5,7},{6,4},{7,5},{8,10},{9,11},{10,... | collective-permute-start | bytes 786440 | tf_op jit(solution)/shard_map/ppermute | solution.py:308
  50.0 3.9 %back_to_second.1 = (bf16[8,128,256]{2,1,0:T(8,128)(2,1)S(1)}, f32[15,128,128]{2,1,0:T(8,128)S(1)}) custom-call(s32[8]{0:T(128)S(1)} %compare_select_fusion.code.refs_0_.code_c, bf16[4,128,256]{2,1,0:T(8,128)(2,1)S(1)} %get-tuple-element.62.ut_ref, bf16[15,128,128]{2,1,0:T(8,128)(2,1)S(1)} %copy-done, bf16[8,256,1920]{2,1,0:T(8,128)(2,1)S(1)} %get-tuple-element.63.near_ref, ...), custom_call_target="tpu_custom_call" | custom-call | flops 4026531840 | bytes 25853984 | tf_op jit(solution)/shard_map/back_to_second/pallas_call | solution.py:32
  53.9 8.6 %collective-permute-start.17 = (bf16[8,128,256]{2,1,0:T(8,128)(2,1)S(1)}, bf16[8,128,256]{2,1,0:T(8,128)(2,1)S(1)}, u32[]{:S(2)}, u32[]{:S(2)}) collective-permute-start(bf16[8,128,256]{2,1,0:T(8,128)(2,1)S(1)} %get-tuple-element.69.part_c), channel_id=1, source_target_pairs={{4,8},{8,4},{12,16},{16,12},{20,24},{24,20},{28,32},{32,28},{36,40... | collective-permute-start | bytes 1572872 | tf_op jit(solution)/shard_map/ppermute | solution.py:308
  64.3 4.1 %collective-permute-start.18 = (bf16[8,256,128]{2,1,0:T(8,128)(2,1)S(1)}, bf16[8,256,128]{2,1,0:T(8,128)(2,1)S(1)}, u32[]{:S(2)}, u32[]{:S(2)}) collective-permute-start(bf16[8,256,128]{2,1,0:T(8,128)(2,1)S(1)} %get-tuple-element.67), channel_id=1, source_target_pairs={{4,8},{8,4},{12,16},{16,12},{20,24},{24,20},{28,32},{32,28},{36,40... | collective-permute-start | bytes 1572872 | tf_op jit(solution)/shard_map/ppermute | solution.py:308
  71.1 2.6 %collective-permute-start.21 = (bf16[4,128,256]{2,1,0:T(8,128)(2,1)S(1)}, bf16[4,128,256]{2,1,0:T(8,128)(2,1)S(1)}, u32[]{:S(2)}, u32[]{:S(2)}) collective-permute-start(bf16[4,128,256]{2,1,0:T(8,128)(2,1)S(1)} %get-tuple-element.81), channel_id=1, source_target_pairs={{0,2},{1,3},{2,0},{3,1},{4,6},{5,7},{6,4},{7,5},{8,10},{9,11},{10,... | collective-permute-start | bytes 786440 | tf_op jit(solution)/shard_map/ppermute | solution.py:308
  75.6 4.3 %back_to_first.1 = (bf16[8,256,1920]{2,1,0:T(8,128)(2,1)S(1)}, f32[15,64,128]{2,1,0:T(8,128)S(1)}, bf16[15,64,128]{2,1,0:T(8,128)(2,1)S(1)}) custom-call(s32[8]{0:T(128)S(1)} %compare_select_fusion.code.refs_0_.code_c, bf16[8,256,128]{2,1,0:T(8,128)(2,1)S(1)} %collective-permute-done.15.chip_ref, bf16[8,256,128]{2,1,0:T(8,128)(2,1)S(1)} %pick_requested.7.here_ref, ...), custom_call_target="tpu_custom_call" | custom-call | tf_op jit(solution)/shard_map/back_to_first/pallas_call | solution.py:32
  82.8 2.7 %collective-permute-done.22.three = bf16[4,128,256]{2,1,0:T(8,128)(2,1)S(1)} collective-permute-done((bf16[4,128,256]{2,1,0:T(8,128)(2,1)S(1)}, bf16[4,128,256]{2,1,0:T(8,128)(2,1)S(1)}, u32[]{:S(2)}, u32[]{:S(2)}) %collective-permute-start.22) | collective-permute-done | bytes 262176 | tf_op jit(solution)/shard_map/ppermute | solution.py:308
  86.7 2.1 %collective-permute-start.23 = (bf16[15,16,128]{2,1,0:T(8,128)(2,1)S(1)}, bf16[15,16,128]{2,1,0:T(8,128)(2,1)S(1)}, u32[]{:S(2)}, u32[]{:S(2)}) collective-permute-start(bf16[15,16,128]{2,1,0:T(8,128)(2,1)S(1)} %get-tuple-element.85), channel_id=1, source_target_pairs={{0,1},{1,0},{2,3},{3,2},{4,5},{5,4},{6,7},{7,6},{8,9},{9,8},{10,11... | collective-permute-start | bytes 184328 | tf_op jit(solution)/shard_map/ppermute | solution.py:308
  88.7 2.8 %to_first.1.total = f32[4,256,128]{2,1,0:T(8,128)S(1)} custom-call(s32[8]{0:T(128)S(1)} %compare_select_fusion.code.refs_0_.code_c, bf16[8,256,1920]{2,1,0:T(8,128)(2,1)S(1)} %get-tuple-element.78.z_ref, bf16[15,128,128]{2,1,0:T(8,128)(2,1)S(1)} %get-tuple-element.79.wmt_ref), custom_call_target="tpu_custom_call" | custom-call | tf_op jit(solution)/shard_map/to_first/pallas_call | solution.py:32
  92.6 6.2 %collective-permute-start.28 = (bf16[15,16,128]{2,1,0:T(8,128)(2,1)S(1)}, bf16[15,16,128]{2,1,0:T(8,128)(2,1)S(1)}, u32[]{:S(2)}, u32[]{:S(2)}) collective-permute-start(bf16[15,16,128]{2,1,0:T(8,128)(2,1)S(1)} %add_quarters.1.own), channel_id=1, source_target_pairs={{0,24},{4,28},{8,16},{12,20},{16,8},{20,12},{24,0},{28,4},{32,56},... | collective-permute-start | bytes 184328 | tf_op jit(solution)/shard_map/ppermute | solution.py:308
  101.0 2.5 %collective-permute-done.27.two = bf16[15,16,128]{2,1,0:T(8,128)(2,1)S(1)} collective-permute-done((bf16[15,16,128]{2,1,0:T(8,128)(2,1)S(1)}, bf16[15,16,128]{2,1,0:T(8,128)(2,1)S(1)}, u32[]{:S(2)}, u32[]{:S(2)}) %collective-permute-start.27) | collective-permute-done | bytes 61472 | tf_op jit(solution)/shard_map/ppermute | solution.py:308
  105.0 5.3 %collective-permute-start.30 = (bf16[15,16,128]{2,1,0:T(8,128)(2,1)S(1)}, bf16[15,16,128]{2,1,0:T(8,128)(2,1)S(1)}, u32[]{:S(2)}, u32[]{:S(2)}) collective-permute-start(bf16[15,16,128]{2,1,0:T(8,128)(2,1)S(1)} %add_in_order.2.own), channel_id=1, source_target_pairs={{0,64},{4,68},{8,72},{12,76},{16,80},{20,84},{24,88},{28,92},{32,9... | collective-permute-start | bytes 184328 | tf_op jit(solution)/shard_map/ppermute | solution.py:308
  113.6 2.1 %collective-permute-start.34 = (bf16[15,16,128]{2,1,0:T(8,128)(2,1)S(1)}, bf16[15,16,128]{2,1,0:T(8,128)(2,1)S(1)}, u32[]{:S(2)}, u32[]{:S(2)}) collective-permute-start(bf16[15,16,128]{2,1,0:T(8,128)(2,1)S(1)} %add_in_order.3.own), channel_id=1, source_target_pairs={{0,3},{1,2},{2,1},{3,0},{4,7},{5,6},{6,5},{7,4},{8,11},{9,10},{10,... | collective-permute-start | bytes 184328 | tf_op jit(solution)/shard_map/ppermute | solution.py:308
  117.9 2.3 %collective-permute-done.33.two = bf16[15,16,128]{2,1,0:T(8,128)(2,1)S(1)} collective-permute-done((bf16[15,16,128]{2,1,0:T(8,128)(2,1)S(1)}, bf16[15,16,128]{2,1,0:T(8,128)(2,1)S(1)}, u32[]{:S(2)}, u32[]{:S(2)}) %collective-permute-start.33) | collective-permute-done | bytes 61472 | tf_op jit(solution)/shard_map/ppermute | solution.py:308
  120.3 5.7 %collective-permute-start.35 = (bf16[15,64,128]{2,1,0:T(8,128)(2,1)S(1)}, bf16[15,64,128]{2,1,0:T(8,128)(2,1)S(1)}, u32[]{:S(2)}, u32[]{:S(2)}) collective-permute-start(bf16[15,64,128]{2,1,0:T(8,128)(2,1)S(1)} %join_quarters.1.own), channel_id=1, source_target_pairs={{0,4},{4,0},{8,12},{12,8},{16,20},{20,16},{24,28},{28,24},{32,36},... | collective-permute-start | bytes 737288 | tf_op jit(solution)/shard_map/ppermute | solution.py:308
  (75 shorter events, 38.0 us)
Async XLA Ops:
  1.7 18.7 %collective-permute-start.4 = (bf16[4,256,128]{2,1,0:T(8,128)(2,1)S(1)}, bf16[4,256,128]{2,1,0:T(8,128)(2,1)S(1)}, u32[]{:S(2)}, u32[]{:S(2)}) collective-permute-start(bf16[4,256,128]{2,1,0:T(8,128)(2,1)S(1)} %fusion.m_ref.refs_2_.refs_1_), channel_id=1, source_target_pairs={{0,3},{1,2},{2,1},{3,0},{4,7},{5,6},{6,5},{7,4},{8,11},{9,10},{10,... | collective-permute-start | bytes 786440 | tf_op jit(solution)/shard_map/ppermute | solution.py:308
  5.4 15.1 %collective-permute-start.3 = (bf16[4,256,128]{2,1,0:T(8,128)(2,1)S(1)}, bf16[4,256,128]{2,1,0:T(8,128)(2,1)S(1)}, u32[]{:S(2)}, u32[]{:S(2)}) collective-permute-start(bf16[4,256,128]{2,1,0:T(8,128)(2,1)S(1)} %fusion.m_ref.refs_2_.refs_1_), channel_id=1, source_target_pairs={{0,2},{1,3},{2,0},{3,1},{4,6},{5,7},{6,4},{7,5},{8,10},{9,11},{10,... | collective-permute-start | bytes 786440 | tf_op jit(solution)/shard_map/ppermute | solution.py:308
  5.7 14.8 %collective-permute-start.2 = (bf16[4,256,128]{2,1,0:T(8,128)(2,1)S(1)}, bf16[4,256,128]{2,1,0:T(8,128)(2,1)S(1)}, u32[]{:S(2)}, u32[]{:S(2)}) collective-permute-start(bf16[4,256,128]{2,1,0:T(8,128)(2,1)S(1)} %fusion.m_ref.refs_2_.refs_1_), channel_id=1, source_target_pairs={{0,1},{1,0},{2,3},{3,2},{4,5},{5,4},{6,7},{7,6},{8,9},{9,8},{10,11... | collective-permute-start | bytes 786440 | tf_op jit(solution)/shard_map/ppermute | solution.py:308
  7.5 9.3 %collective-permute-start.1 = (s32[8]{0:T(128)S(1)}, s32[8]{0:T(128)S(1)}, u32[]{:S(2)}, u32[]{:S(2)}) collective-permute-start(s32[8]{0:T(128)S(1)} %compare_select_fusion.code.refs_0_.code_c), channel_id=1, source_target_pairs={{0,4},{4,0},{8,12},{12,8},{16,20},{20,16},{24,28},{28,24},{32,36},... | collective-permute-start | bytes 104 | tf_op jit(solution)/shard_map/ppermute | solution.py:308
  8.8 11.6 %collective-permute-start = (s32[8]{0:T(128)S(1)}, s32[8]{0:T(128)S(1)}, u32[]{:S(2)}, u32[]{:S(2)}) collective-permute-start(s32[8]{0:T(128)S(1)} %compare_select_fusion.code.refs_0_.code_c), channel_id=1, source_target_pairs={{4,8},{8,4},{12,16},{16,12},{20,24},{24,20},{28,32},{32,28},{36,40... | collective-permute-start | bytes 104 | tf_op jit(solution)/shard_map/ppermute | solution.py:308
  16.8 10.5 %collective-permute-start.7 = (bf16[8,128,256]{2,1,0:T(8,128)(2,1)S(1)}, bf16[8,128,256]{2,1,0:T(8,128)(2,1)S(1)}, u32[]{:S(2)}, u32[]{:S(2)}) collective-permute-start(bf16[8,128,256]{2,1,0:T(8,128)(2,1)S(1)} %get-tuple-element.52.part_c), channel_id=1, source_target_pairs={{4,8},{8,4},{12,16},{16,12},{20,24},{24,20},{28,32},{32,28},{36,40... | collective-permute-start | bytes 1572872 | tf_op jit(solution)/shard_map/ppermute | solution.py:308
  20.4 6.9 %collective-permute-start.6 = (bf16[8,128,256]{2,1,0:T(8,128)(2,1)S(1)}, bf16[8,128,256]{2,1,0:T(8,128)(2,1)S(1)}, u32[]{:S(2)}, u32[]{:S(2)}) collective-permute-start(bf16[8,128,256]{2,1,0:T(8,128)(2,1)S(1)} %get-tuple-element.52.part_c), channel_id=1, source_target_pairs={{0,4},{4,0},{8,12},{12,8},{16,20},{20,16},{24,28},{28,24},{32,36},... | collective-permute-start | bytes 1572872 | tf_op jit(solution)/shard_map/ppermute | solution.py:308
  21.4 14.0 %collective-permute-start.5 = (bf16[8,256,128]{2,1,0:T(8,128)(2,1)S(1)}, bf16[8,256,128]{2,1,0:T(8,128)(2,1)S(1)}, u32[]{:S(2)}, u32[]{:S(2)}) collective-permute-start(bf16[8,256,128]{2,1,0:T(8,128)(2,1)S(1)} %get-tuple-element.49), channel_id=1, source_target_pairs={{0,4},{4,0},{8,12},{12,8},{16,20},{20,16},{24,28},{28,24},{32,36},... | collective-permute-start | bytes 1572872 | tf_op jit(solution)/shard_map/ppermute | solution.py:308
  22.0 13.5 %collective-permute-start.8 = (bf16[8,256,128]{2,1,0:T(8,128)(2,1)S(1)}, bf16[8,256,128]{2,1,0:T(8,128)(2,1)S(1)}, u32[]{:S(2)}, u32[]{:S(2)}) collective-permute-start(bf16[8,256,128]{2,1,0:T(8,128)(2,1)S(1)} %get-tuple-element.50), channel_id=1, source_target_pairs={{4,8},{8,4},{12,16},{16,12},{20,24},{24,20},{28,32},{32,28},{36,40... | collective-permute-start | bytes 1572872 | tf_op jit(solution)/shard_map/ppermute | solution.py:308
  28.6 10.4 %collective-permute-start.9 = (bf16[4,128,256]{2,1,0:T(8,128)(2,1)S(1)}, bf16[4,128,256]{2,1,0:T(8,128)(2,1)S(1)}, u32[]{:S(2)}, u32[]{:S(2)}) collective-permute-start(bf16[4,128,256]{2,1,0:T(8,128)(2,1)S(1)} %get-tuple-element.57), channel_id=1, source_target_pairs={{0,1},{1,0},{2,3},{3,2},{4,5},{5,4},{6,7},{7,6},{8,9},{9,8},{10,11... | collective-permute-start | bytes 786440 | tf_op jit(solution)/shard_map/ppermute | solution.py:308
  33.0 9.3 %collective-permute-start.10 = (bf16[4,128,256]{2,1,0:T(8,128)(2,1)S(1)}, bf16[4,128,256]{2,1,0:T(8,128)(2,1)S(1)}, u32[]{:S(2)}, u32[]{:S(2)}) collective-permute-start(bf16[4,128,256]{2,1,0:T(8,128)(2,1)S(1)} %get-tuple-element.58), channel_id=1, source_target_pairs={{0,2},{1,3},{2,0},{3,1},{4,6},{5,7},{6,4},{7,5},{8,10},{9,11},{10,... | collective-permute-start | bytes 786440 | tf_op jit(solution)/shard_map/ppermute | solution.py:308
  34.8 10.2 %collective-permute-start.11 = (bf16[4,128,256]{2,1,0:T(8,128)(2,1)S(1)}, bf16[4,128,256]{2,1,0:T(8,128)(2,1)S(1)}, u32[]{:S(2)}, u32[]{:S(2)}) collective-permute-start(bf16[4,128,256]{2,1,0:T(8,128)(2,1)S(1)} %get-tuple-element.59), channel_id=1, source_target_pairs={{0,3},{1,2},{2,1},{3,0},{4,7},{5,6},{6,5},{7,4},{8,11},{9,10},{10,... | collective-permute-start | bytes 786440 | tf_op jit(solution)/shard_map/ppermute | solution.py:308
  46.7 15.9 %collective-permute-start.14 = (bf16[4,256,128]{2,1,0:T(8,128)(2,1)S(1)}, bf16[4,256,128]{2,1,0:T(8,128)(2,1)S(1)}, u32[]{:S(2)}, u32[]{:S(2)}) collective-permute-start(bf16[4,256,128]{2,1,0:T(8,128)(2,1)S(1)} %get-tuple-element.65.refs_2_.refs_1_), channel_id=1, source_target_pairs={{0,3},{1,2},{2,1},{3,0},{4,7},{5,6},{6,5},{7,4},{8,11},{9,10},{10,... | collective-permute-start | bytes 786440 | tf_op jit(solution)/shard_map/ppermute | solution.py:308
  46.9 15.7 %collective-permute-start.13 = (bf16[4,256,128]{2,1,0:T(8,128)(2,1)S(1)}, bf16[4,256,128]{2,1,0:T(8,128)(2,1)S(1)}, u32[]{:S(2)}, u32[]{:S(2)}) collective-permute-start(bf16[4,256,128]{2,1,0:T(8,128)(2,1)S(1)} %get-tuple-element.65.refs_2_.refs_1_), channel_id=1, source_target_pairs={{0,2},{1,3},{2,0},{3,1},{4,6},{5,7},{6,4},{7,5},{8,10},{9,11},{10,... | collective-permute-start | bytes 786440 | tf_op jit(solution)/shard_map/ppermute | solution.py:308
  49.0 13.6 %collective-permute-start.12 = (bf16[4,256,128]{2,1,0:T(8,128)(2,1)S(1)}, bf16[4,256,128]{2,1,0:T(8,128)(2,1)S(1)}, u32[]{:S(2)}, u32[]{:S(2)}) collective-permute-start(bf16[4,256,128]{2,1,0:T(8,128)(2,1)S(1)} %get-tuple-element.65.refs_2_.refs_1_), channel_id=1, source_target_pairs={{0,1},{1,0},{2,3},{3,2},{4,5},{5,4},{6,7},{7,6},{8,9},{9,8},{10,11... | collective-permute-start | bytes 786440 | tf_op jit(solution)/shard_map/ppermute | solution.py:308
  53.9 15.4 %collective-permute-start.17 = (bf16[8,128,256]{2,1,0:T(8,128)(2,1)S(1)}, bf16[8,128,256]{2,1,0:T(8,128)(2,1)S(1)}, u32[]{:S(2)}, u32[]{:S(2)}) collective-permute-start(bf16[8,128,256]{2,1,0:T(8,128)(2,1)S(1)} %get-tuple-element.69.part_c), channel_id=1, source_target_pairs={{4,8},{8,4},{12,16},{16,12},{20,24},{24,20},{28,32},{32,28},{36,40... | collective-permute-start | bytes 1572872 | tf_op jit(solution)/shard_map/ppermute | solution.py:308
  62.5 6.9 %collective-permute-start.16 = (bf16[8,128,256]{2,1,0:T(8,128)(2,1)S(1)}, bf16[8,128,256]{2,1,0:T(8,128)(2,1)S(1)}, u32[]{:S(2)}, u32[]{:S(2)}) collective-permute-start(bf16[8,128,256]{2,1,0:T(8,128)(2,1)S(1)} %get-tuple-element.69.part_c), channel_id=1, source_target_pairs={{0,4},{4,0},{8,12},{12,8},{16,20},{20,16},{24,28},{28,24},{32,36},... | collective-permute-start | bytes 1572872 | tf_op jit(solution)/shard_map/ppermute | solution.py:308
  63.6 11.0 %collective-permute-start.15 = (bf16[8,256,128]{2,1,0:T(8,128)(2,1)S(1)}, bf16[8,256,128]{2,1,0:T(8,128)(2,1)S(1)}, u32[]{:S(2)}, u32[]{:S(2)}) collective-permute-start(bf16[8,256,128]{2,1,0:T(8,128)(2,1)S(1)} %get-tuple-element.66), channel_id=1, source_target_pairs={{0,4},{4,0},{8,12},{12,8},{16,20},{20,16},{24,28},{28,24},{32,36},... | collective-permute-start | bytes 1572872 | tf_op jit(solution)/shard_map/ppermute | solution.py:308
  64.3 11.3 %collective-permute-start.18 = (bf16[8,256,128]{2,1,0:T(8,128)(2,1)S(1)}, bf16[8,256,128]{2,1,0:T(8,128)(2,1)S(1)}, u32[]{:S(2)}, u32[]{:S(2)}) collective-permute-start(bf16[8,256,128]{2,1,0:T(8,128)(2,1)S(1)} %get-tuple-element.67), channel_id=1, source_target_pairs={{4,8},{8,4},{12,16},{16,12},{20,24},{24,20},{28,32},{32,28},{36,40... | collective-permute-start | bytes 1572872 | tf_op jit(solution)/shard_map/ppermute | solution.py:308
  70.7 10.9 %collective-permute-start.20 = (bf16[4,128,256]{2,1,0:T(8,128)(2,1)S(1)}, bf16[4,128,256]{2,1,0:T(8,128)(2,1)S(1)}, u32[]{:S(2)}, u32[]{:S(2)}) collective-permute-start(bf16[4,128,256]{2,1,0:T(8,128)(2,1)S(1)} %get-tuple-element.80), channel_id=1, source_target_pairs={{0,1},{1,0},{2,3},{3,2},{4,5},{5,4},{6,7},{7,6},{8,9},{9,8},{10,11... | collective-permute-start | bytes 786440 | tf_op jit(solution)/shard_map/ppermute | solution.py:308
  71.1 11.7 %collective-permute-start.21 = (bf16[4,128,256]{2,1,0:T(8,128)(2,1)S(1)}, bf16[4,128,256]{2,1,0:T(8,128)(2,1)S(1)}, u32[]{:S(2)}, u32[]{:S(2)}) collective-permute-start(bf16[4,128,256]{2,1,0:T(8,128)(2,1)S(1)} %get-tuple-element.81), channel_id=1, source_target_pairs={{0,2},{1,3},{2,0},{3,1},{4,6},{5,7},{6,4},{7,5},{8,10},{9,11},{10,... | collective-permute-start | bytes 786440 | tf_op jit(solution)/shard_map/ppermute | solution.py:308
  73.7 11.8 %collective-permute-start.22 = (bf16[4,128,256]{2,1,0:T(8,128)(2,1)S(1)}, bf16[4,128,256]{2,1,0:T(8,128)(2,1)S(1)}, u32[]{:S(2)}, u32[]{:S(2)}) collective-permute-start(bf16[4,128,256]{2,1,0:T(8,128)(2,1)S(1)} %get-tuple-element.82), channel_id=1, source_target_pairs={{0,3},{1,2},{2,1},{3,0},{4,7},{5,6},{6,5},{7,4},{8,11},{9,10},{10,... | collective-permute-start | bytes 786440 | tf_op jit(solution)/shard_map/ppermute | solution.py:308
  92.6 8.4 %collective-permute-start.28 = (bf16[15,16,128]{2,1,0:T(8,128)(2,1)S(1)}, bf16[15,16,128]{2,1,0:T(8,128)(2,1)S(1)}, u32[]{:S(2)}, u32[]{:S(2)}) collective-permute-start(bf16[15,16,128]{2,1,0:T(8,128)(2,1)S(1)} %add_quarters.1.own), channel_id=1, source_target_pairs={{0,24},{4,28},{8,16},{12,20},{16,8},{20,12},{24,0},{28,4},{32,56},... | collective-permute-start | bytes 184328 | tf_op jit(solution)/shard_map/ppermute | solution.py:308
  105.0 6.9 %collective-permute-start.30 = (bf16[15,16,128]{2,1,0:T(8,128)(2,1)S(1)}, bf16[15,16,128]{2,1,0:T(8,128)(2,1)S(1)}, u32[]{:S(2)}, u32[]{:S(2)}) collective-permute-start(bf16[15,16,128]{2,1,0:T(8,128)(2,1)S(1)} %add_in_order.2.own), channel_id=1, source_target_pairs={{0,64},{4,68},{8,72},{12,76},{16,80},{20,84},{24,88},{28,92},{32,9... | collective-permute-start | bytes 184328 | tf_op jit(solution)/shard_map/ppermute | solution.py:308
  (15 other events, 129.2 us)
